TPU v7x, 256 devices: a whole 4x4x8 slice. The times are simulated.
256 devices in a mesh: view: 8 (over z), tile: 32 (over x, y, core).
Axes of the slice: x: 4, y: 4, z: 8, core: 2. Of those that a mesh axis runs over, the one named last changes fastest.
Arguments:
- features: float32 [2048, 64, 128], P(('view', 'tile')), may hold values from -24 to 24
- moment_first: float32 [2048, 64, 128], P(('view', 'tile')), may hold values from -0.6 to 0.6
- moment_second: float32 [2048, 64, 128], P(('view', 'tile')), may hold values from 0.0001 to 0.1
- positions: float32 [2048, 3, 128], P(('view', 'tile')), may hold values from 0 to 1
- scales: float32 [2048, 128], P(('view', 'tile')), may hold values from 1.5 to 5
- opacity: float32 [2048, 128], P(('view', 'tile')), may hold values from -7 to -3
- cameras_first: float32 [8, 2, 4], P('view'), may hold values from -4 to 16
- shift_first: float32 [8, 512, 2], P('view', 'tile'), may hold values from -2 to 2
- lists_first: int32 [8, 512, 8], P('view', 'tile'), may hold values from 0 to 255, as said below
- loads_first: int32 [8, 512], P('view', 'tile'), may hold values from 1 to 8
- target: bfloat16 [8, 512, 64, 256], P('view', 'tile'), may hold values from -12 to 12
- owner_after: int32 [2048], P(('view', 'tile')), may hold values from 0 to 7, as said below
- cameras_second: float32 [8, 2, 4], P('view'), may hold values from -4 to 16
- shift_second: float32 [8, 512, 2], P('view', 'tile'), may hold values from -2 to 2
- lists_second: int32 [8, 512, 8], P('view', 'tile'), may hold values from 0 to 255, as said below
- loads_second: int32 [8, 512], P('view', 'tile'), may hold values from 1 to 8
Outputs:
- image_second: float32 [8, 512, 64, 256], P('view', 'tile')
- new_features: float32 [2048, 64, 128], P(('view', 'tile'))
- new_first: float32 [2048, 64, 128], P(('view', 'tile'))
- new_second: float32 [2048, 64, 128], P(('view', 'tile'))
Inputs may be any that keep to these rules, and one draw needn't show every extreme that they name: `lists_first`: on each device, at most 6 of its list entries name bins of any one device of its view group, and some device of the group is named exactly 6 times. `lists_second`: on each device, at most 6 of its list entries name bins of any one device of its view group after the move, and some device of the group is named exactly 6 times. `owner_after`: each device's 8 entries name every view group exactly 1 times.
All inputs are finite; a program needn't handle non-finite values.
Results may differ from a plain program's by a relative error of at most 0.0015.
The roundings to bfloat16 on the way count: a program that leaves them out, or rounds other values in their place, can miss the bound.
Values may be sent and summed in bfloat16 or wider, within the bound.
No kernel may reach another device: no remote copies, remote signals or barrier semaphores. Data moves between devices by JAX's collectives and lax.ppermute only.
A program may use at most 64 MiB of HBM per device.

v0:
```python
import functools

import jax
import jax.numpy as jnp
from jax import lax
from jax.experimental import pallas as pl
from jax.experimental.pallas import tpu as pltpu
from jax.sharding import PartitionSpec as P

C = 64
GB = 128
PIX = 256
SIDE = 16
LBLK = 8
TILES = 16
BINS = 8
N_VIEW = 8
N_TILE = 32
ROWS = GB // 8

beta_first = 0.9
beta_second = 0.999
learn_rate = 0.05
adam_epsilon = 1e-08
bias_first = 1.0 - 0.9**10
bias_second = 1.0 - 0.999**10

VM = pl.BlockSpec(memory_space=pltpu.VMEM)
SM = pl.BlockSpec(memory_space=pltpu.SMEM)
ANY = pl.BlockSpec(memory_space=pl.ANY)
GROUP = 8
WEIGHTS_MIB = 60
RENDER_MIB = 60
LOG2E = 1.4426950408889634
f32 = jnp.float32
bf16 = jnp.bfloat16


def params(mib, **more):
    return pltpu.CompilerParams(vmem_limit_bytes=mib * 1024 * 1024, **more)


def onehot(inverse):
    row = lax.broadcasted_iota(jnp.int32, (GB, GB), 0)
    col = lax.broadcasted_iota(jnp.int32, (GB, GB), 1)
    if inverse:
        row, col = col, row
    return jnp.where(col == (row % ROWS) * 8 + row // ROWS, 1.0, 0.0).astype(bf16)


def reorder(values, inverse):
    return jnp.dot(values, onehot(inverse), preferred_element_type=f32)


def reorder_wide(values, inverse):
    high = values.astype(bf16)
    rest = values - high.astype(f32)
    middle = rest.astype(bf16)
    low = (rest - middle.astype(f32)).astype(bf16)
    return (reorder(high, inverse) + reorder(middle, inverse)) + reorder(low, inverse)


def project_rows(p0, p1, p2, scales, opacity, camera):
    mean_x = camera[0, 0] * p0 + camera[0, 1] * p1 + camera[0, 2] * p2 + camera[0, 3]
    mean_y = camera[1, 0] * p0 + camera[1, 1] * p1 + camera[1, 2] * p2 + camera[1, 3]
    falloff = 0.5 / (scales * scales)
    opaque = 1.0 / (1.0 + jnp.exp(-opacity))
    stack = jnp.concatenate([mean_x, mean_y, falloff, opaque], axis=0)
    return reorder(stack.astype(bf16), False)


def screen_rows(stack):
    rows = [stack[k * BINS + b : k * BINS + b + 1] for b in range(BINS) for k in range(4)]
    return jnp.concatenate(rows, axis=0).astype(bf16)


def spread(stack, screen):
    rows = screen_rows(stack)
    for t in range(N_TILE):
        screen[t] = rows


def fetch(pairs, sems):
    copies = [pltpu.make_async_copy(source, to, sems.at[i]) for i, (source, to) in enumerate(pairs)]
    for copy in copies:
        copy.start()
    return copies


def prep_kernel(camera_hbm, owner_hbm, feat_hbm, pos_hbm, scales_hbm, opacity_hbm, colors, screen, geometry, *scratch):
    camera, owner, feat, pos, scales, opacity, sems = scratch
    copies = fetch(
        [
            (camera_hbm, camera),
            (owner_hbm, owner),
            (feat_hbm, feat),
            (pos_hbm, pos),
            (scales_hbm, scales),
            (opacity_hbm, opacity),
        ],
        sems,
    )
    for copy in copies:
        copy.wait()
    flat = feat[...].reshape(BINS * C, GB).astype(bf16)
    colors[...] = reorder(flat, False).astype(bf16).reshape(BINS, C, GB)
    stack = project_rows(pos[0], pos[1], pos[2], scales[...], opacity[...], camera.at[0])
    spread(stack, screen)
    for s in range(BINS):
        rows = [pos[k, s : s + 1] for k in range(3)]
        rows += [scales[s : s + 1], opacity[s : s + 1], jnp.zeros((3, GB), f32)]
        geometry[owner[s]] = jnp.concatenate(rows, axis=0)


def prep(camera, owner, feat, pos, scales, opacity):
    return pl.pallas_call(
        prep_kernel,
        out_shape=(
            jax.ShapeDtypeStruct((BINS, C, GB), bf16),
            jax.ShapeDtypeStruct((N_TILE, BINS * 4, GB), bf16),
            jax.ShapeDtypeStruct((N_VIEW, 8, GB), f32),
        ),
        in_specs=[ANY] * 6,
        out_specs=(VM, VM, VM),
        scratch_shapes=[
            pltpu.SMEM((1, 2, 4), f32),
            pltpu.SMEM((BINS,), jnp.int32),
            pltpu.VMEM((BINS, C, GB), f32),
            pltpu.VMEM((3, BINS, GB), f32),
            pltpu.VMEM((BINS, GB), f32),
            pltpu.VMEM((BINS, GB), f32),
            pltpu.SemaphoreType.DMA((6,)),
        ],
        compiler_params=params(60),
        name="prep",
    )(camera, owner, feat, pos, scales, opacity)


def screen_kernel(camera, geometry, screen):
    rows = [jnp.concatenate([geometry[b, k : k + 1] for b in range(BINS)], axis=0) for k in range(5)]
    spread(project_rows(*rows, camera), screen)


def screen_again(camera, geometry):
    return pl.pallas_call(
        screen_kernel,
        out_shape=jax.ShapeDtypeStruct((N_TILE, BINS * 4, GB), bf16),
        in_specs=[SM, VM],
        out_specs=VM,
        compiler_params=params(8),
        name="screen_again",
    )(camera, geometry)


def weights_kernel(lists_hbm, loads_hbm, shift_hbm, screen_hbm, out_hbm, token, *scratch):
    lists, loads, shift, screen, bins, out, work, sem, sems = scratch
    copies = fetch([(lists_hbm, lists), (loads_hbm, loads), (shift_hbm, shift), (screen_hbm, screen)], sems)
    token[...] = jnp.zeros((8, GB), f32)
    row = lax.broadcasted_iota(jnp.int32, (8, GB), 0)
    lane = lax.broadcasted_iota(jnp.int32, (8, GB), 1)
    pixel_x = (lane % SIDE).astype(f32) + 0.5
    pixel_y = (lane // SIDE).astype(f32) + 0.5
    for copy in copies:
        copy.wait()

    def widen(t, unused):
        rows = screen[t].astype(f32)
        for i in range(BINS // 2):
            two = rows[8 * i : 8 * i + 8]
            bins[t * BINS + 2 * i] = two
            bins[t * BINS + 2 * i + 1] = pltpu.roll(two, 4, 0)
        return unused

    lax.fori_loop(0, N_TILE, widen, 0, unroll=4)
    source = lax.broadcasted_iota(jnp.int32, (GROUP * 8, 4 * GB), 0)
    wanted = lax.broadcasted_iota(jnp.int32, (GROUP * 8, 4 * GB), 1) // GB

    def one(wide, place_x, place_y):
        running = [jnp.ones((8, GB), f32) for half in range(2)]
        parts = [[], []]
        for v in range(ROWS):
            some = wide[v * 8 : v * 8 + 8]
            mean_x, mean_y, fall, opaque = (some[:, k * GB : k * GB + GB] for k in range(4))
            fall = fall * -LOG2E
            delta_x = place_x - mean_x
            along_x = delta_x * delta_x * fall
            for half in range(2):
                delta_y = place_y[half] - mean_y
                part = opaque * jnp.exp2(along_x + delta_y * delta_y * fall) * running[half]
                parts[half].append(part)
                running[half] = running[half] - part
        before, after = [], []
        for total in running:
            for step in (1, 2, 4):
                total = total * jnp.where(row >= step, pltpu.roll(total, step, 0), 1.0)
            before.append(jnp.where(row >= 1, pltpu.roll(total, 1, 0), 1.0))
            after.append(jnp.broadcast_to(total[7:8], (8, GB)))
        return parts, before, after

    def plan(tile, state):
        count, spare = state
        live = loads[tile]
        for q in range(LBLK):
            work[count + q] = tile * LBLK + q
        return count + live, jnp.where(live < LBLK, tile * LBLK + LBLK - 1, spare)

    count, spare = lax.fori_loop(0, TILES, plan, (0, 0))
    for k in range(GROUP):
        work[count + k] = spare

    def leave(item):
        return pltpu.make_async_copy(out.at[item], out_hbm.at[item // LBLK, item % LBLK], sem)

    def group(step, carried):
        items = [work[step * GROUP + k] for k in range(GROUP)]
        done, values = [], []
        for item in items:
            tile, q = item // LBLK, item % LBLK
            alive = jnp.where(q < loads[tile], 1.0, 0.0)
            value = bins[lists[q, tile]]
            values.append(jnp.where(row == 3, value * alive, value))
        columns = jnp.concatenate(values, axis=0).T.astype(bf16)
        for k, item in enumerate(items):
            tile = item // LBLK
            pick = jnp.where(source == wanted + 8 * k, 1.0, 0.0).astype(bf16)
            wide = jnp.dot(columns, pick, preferred_element_type=f32)
            place_x = pixel_x + shift[0, tile]
            place_y = [pixel_y + shift[1, tile] + 8.0 * half for half in range(2)]
            done.append(one(wide, place_x, place_y))
        for item, (parts, before, after) in zip(items, done):
            fresh = item % LBLK == 0
            carried = [jnp.where(fresh, 1.0, value) for value in carried]
            for half in range(2):
                scale = carried[half] * before[half]
                rows = [part * scale for part in parts[half]]
                out[item, :, half * GB : half * GB + GB] = jnp.concatenate(rows, axis=0).astype(bf16)
            carried = [carried[half] * after[half] for half in range(2)]
        for k, item in enumerate(items):

            @pl.when(step * GROUP + k < count)
            def _():
                leave(item).start()

        return tuple(carried)

    lax.fori_loop(0, (count + GROUP - 1) // GROUP, group, (jnp.ones((8, GB), f32),) * 2)

    def arrived(i, unused):
        leave(0).wait()
        return unused

    lax.fori_loop(0, count, arrived, 0)


def weights(lists, loads, shift, screen, name):
    return pl.pallas_call(
        weights_kernel,
        out_shape=(jax.ShapeDtypeStruct((TILES, LBLK, GB, PIX), bf16), jax.ShapeDtypeStruct((8, GB), f32)),
        in_specs=[ANY] * 4,
        out_specs=(ANY, VM),
        scratch_shapes=[
            pltpu.SMEM((LBLK, TILES), jnp.int32),
            pltpu.SMEM((TILES,), jnp.int32),
            pltpu.SMEM((2, TILES), f32),
            pltpu.VMEM((N_TILE, BINS * 4, GB), bf16),
            pltpu.VMEM((N_TILE * BINS, 8, GB), f32),
            pltpu.VMEM((TILES * LBLK, GB, PIX), bf16),
            pltpu.SMEM((TILES * LBLK + LBLK,), jnp.int32),
            pltpu.SemaphoreType.DMA,
            pltpu.SemaphoreType.DMA((4,)),
        ],
        compiler_params=params(WEIGHTS_MIB),
        cost_estimate=pl.CostEstimate(
            flops=TILES * LBLK * GB * PIX * 14, bytes_accessed=10_000_000, transcendentals=TILES * LBLK * GB * PIX
        ),
        name=name,
    )(lists.T, loads, shift.T, screen)


def load_colors(blocks, colors, sems):
    return fetch([(block, colors.at[pl.ds(i * 32, 32)]) for i, block in enumerate(blocks)], sems)


def fetch_weights(loads, w_hbm, w, sems):
    def tile_start(tile, unused):
        for q in range(LBLK):

            @pl.when(q < loads[tile])
            def _():
                pltpu.make_async_copy(w_hbm.at[tile, q], w.at[tile, q], sems.at[tile]).start()

        return unused

    lax.fori_loop(0, TILES, tile_start, 0)


def over_tiles(loads, w_hbm, w, sems, body):
    def each_tile(tile, unused):
        live = loads[tile]
        for size in range(1, LBLK + 1):

            @pl.when(live == size)
            def _():
                pltpu.make_async_copy(
                    w_hbm.at[tile, pl.ds(0, size)], w.at[tile, pl.ds(0, size)], sems.at[tile]
                ).wait()
                body(tile, w[tile, :size].reshape(size * GB, PIX), size)

        return unused

    lax.fori_loop(0, TILES, each_tile, 0)


def picture(slots, tile, w, size, colors):
    row = jnp.concatenate([colors[slots[tile, q]] for q in range(size)], axis=1)
    return jnp.dot(row, w, preferred_element_type=f32)


def first_kernel(slots, loads, token, w_hbm, target_hbm, *rest):
    blocks, outs, (colors, w, target, total, sems, w_sems, t_sem) = rest[:8], rest[8:16], rest[16:]
    copies = load_colors(blocks, colors, sems) + fetch([(target_hbm, target)], t_sem)
    fetch_weights(loads, w_hbm, w, w_sems)

    def clear(i, unused):
        total[pl.ds(i * 8, 8)] = jnp.zeros((8, C, GB), f32)
        return unused

    lax.fori_loop(0, N_TILE, clear, 0)
    for copy in copies:
        copy.wait()

    def body(tile, w, size):
        residual = (picture(slots, tile, w, size, colors) - target[tile].astype(f32)).astype(bf16)
        pieces = lax.dot_general(residual, w, (((1,), (1,)), ((), ())), preferred_element_type=f32)
        for q in range(size):
            slot = slots[tile, q]
            total[slot] = total[slot] + pieces[:, q * GB : q * GB + GB]

    over_tiles(loads, w_hbm, w, w_sems, body)
    copies = fetch([(total.at[pl.ds(i * 32, 32)], out) for i, out in enumerate(outs)], sems)
    for copy in copies:
        copy.wait()


def first_render(slots, loads, token, w, target, blocks):
    return pl.pallas_call(
        first_kernel,
        out_shape=(jax.ShapeDtypeStruct((32, C, GB), f32),) * 8,
        in_specs=[SM, SM, ANY, ANY, ANY] + [ANY] * 8,
        out_specs=(ANY,) * 8,
        scratch_shapes=[
            pltpu.VMEM((N_TILE * BINS, C, GB), bf16),
            pltpu.VMEM((TILES, LBLK, GB, PIX), bf16),
            pltpu.VMEM((TILES, C, PIX), bf16),
            pltpu.VMEM((N_TILE * BINS, C, GB), f32),
            pltpu.SemaphoreType.DMA((8,)),
            pltpu.SemaphoreType.DMA((TILES,)),
            pltpu.SemaphoreType.DMA((1,)),
        ],
        compiler_params=params(RENDER_MIB),
        cost_estimate=pl.CostEstimate(flops=TILES * LBLK * C * GB * PIX * 4, bytes_accessed=25_000_000, transcendentals=0),
        name="first_render",
    )(slots, loads, token, w, target, *blocks)


def second_kernel(slots, loads, token, w_hbm, *rest):
    blocks, image, (colors, w, sems, w_sems) = rest[:8], rest[8], rest[9:]
    copies = load_colors(blocks, colors, sems)
    fetch_weights(loads, w_hbm, w, w_sems)
    for copy in copies:
        copy.wait()

    def body(tile, w, size):
        image[tile] = picture(slots, tile, w, size, colors)

    over_tiles(loads, w_hbm, w, w_sems, body)


def second_render(slots, loads, token, w, blocks):
    return pl.pallas_call(
        second_kernel,
        out_shape=jax.ShapeDtypeStruct((TILES, C, PIX), f32),
        in_specs=[SM, SM, ANY, ANY] + [ANY] * 8,
        out_specs=VM,
        scratch_shapes=[
            pltpu.VMEM((N_TILE * BINS, C, GB), bf16),
            pltpu.VMEM((TILES, LBLK, GB, PIX), bf16),
            pltpu.SemaphoreType.DMA((8,)),
            pltpu.SemaphoreType.DMA((TILES,)),
        ],
        compiler_params=params(RENDER_MIB),
        cost_estimate=pl.CostEstimate(flops=TILES * LBLK * C * GB * PIX * 2, bytes_accessed=14_000_000, transcendentals=0),
        name="second_render",
    )(slots, loads, token, w, *blocks)


def adam_kernel(owner, me, gradient, feat, m1, m2, colors, packed):
    g = reorder_wide(gradient[...].reshape(BINS * C, GB), True).reshape(BINS, C, GB)
    first_new = beta_first * m1[...] + (1.0 - beta_first) * g
    second_new = beta_second * m2[...] + (1.0 - beta_second) * g * g
    stepped = feat[...] - learn_rate * (first_new / bias_first) / (jnp.sqrt(second_new / bias_second) + adam_epsilon)
    flat = stepped.reshape(BINS * C, GB).astype(bf16)
    sent = reorder(flat, False).astype(bf16).reshape(BINS, C, GB)
    for s in range(BINS):
        w = owner[s]
        colors[w ^ me[0]] = sent[s]
        packed[w, 0:C] = stepped[s]
        packed[w, C : 2 * C] = first_new[s]
        packed[w, 2 * C : 3 * C] = second_new[s]


def adam(owner, me, gradient, feat, m1, m2):
    return pl.pallas_call(
        adam_kernel,
        out_shape=(
            jax.ShapeDtypeStruct((N_VIEW, C, GB), bf16),
            jax.ShapeDtypeStruct((N_VIEW, 3 * C, GB), f32),
        ),
        in_specs=[SM, SM, VM, VM, VM, VM],
        out_specs=(VM, VM),
        compiler_params=params(16),
        name="adam",
    )(owner, me, gradient, feat, m1, m2)


def device(x, y, c):
    return ((x % 4) * 4 + y % 4) * 2 + c


def shift_by(value, level, k):
    pairs = []
    for x in range(4):
        for y in range(4):
            for c in range(2):
                dx, dy = (k, 0) if c == level else (0, k)
                pairs.append((device(x, y, c), device(x + dx, y + dy, c)))
    return lax.ppermute(value, "tile", pairs)


def swap_core(value):
    pairs = [(t, t ^ 1) for t in range(N_TILE)]
    return lax.ppermute(value, "tile", pairs)


ORDER = (2, 1, 3)


def tie(*values):
    return lax.optimization_barrier(values)


def gather_line(colors):
    near = {0: colors}
    for k in ORDER:
        near[k] = shift_by(colors, 0, k)
    return jnp.concatenate([near[k] for k in range(4)], axis=0)


def gather_plane(line):
    plane = {0: line}
    for k in ORDER:
        plane[k] = shift_by(line, 1, k)
    return [plane[k] for k in range(4)]


def swapped(own):
    return list(own) + [swap_core(block) for block in own]


def scatter_far(parts):
    half16 = jnp.float16
    summed = {}
    for k in ORDER + (0,):
        summed[k] = parts[k] + swap_core(parts[4 + k])
    line = summed[0]
    for k in ORDER:
        line = line + shift_by(summed[k].astype(half16), 1, -k).astype(f32)
    return line


def scatter_near(line):
    half16 = jnp.float16
    total = line[0:BINS]
    for k in ORDER:
        total = total + shift_by(line[k * BINS : (k + 1) * BINS].astype(half16), 0, -k).astype(f32)
    return total


def color_slots(lists, within):
    me = lax.axis_index("tile")
    x, y, c = me // 8, (me // 2) % 4, me % 2
    owner = lists // BINS
    far_x = (x - owner // 8) % 4
    far_y = (y - (owner // 2) % 4) % 4
    core = owner % 2
    near = jnp.where(core == 0, far_x, far_y)
    far = jnp.where(core == 0, far_y, far_x)
    return (((core ^ c) * 4 + far) * 4 + near) * BINS + within


def exchange_views(colors):
    def step(value, r):
        return lax.ppermute(value, "view", [(v, v ^ r) for v in range(N_VIEW)])

    handed = step(colors[4:], 4)
    pairs = [jnp.concatenate([colors[r : r + 1], handed[r : r + 1]], axis=0) for r in range(4)]
    return jnp.concatenate([pairs[0]] + [step(pairs[r], r) for r in (1, 2, 3)], axis=0)


def place_of(view):
    r = view ^ lax.axis_index("view")
    return (r % 4) * 2 + r // 4


def across_view(value):
    return lax.all_to_all(value, "view", split_axis=0, concat_axis=0, tiled=True)


def across_tile(value):
    return lax.all_to_all(value, "tile", split_axis=0, concat_axis=0, tiled=True)


def local(
    features,
    moment_first,
    moment_second,
    positions,
    scales,
    opacity,
    cameras_first,
    shift_first,
    lists_first,
    loads_first,
    target,
    owner_after,
    cameras_second,
    shift_second,
    lists_second,
    loads_second,
):
    positions = jnp.transpose(positions, (1, 0, 2))
    colors, screen, geometry = prep(cameras_first, owner_after, features, positions, scales, opacity)
    screen = across_tile(screen)
    line, screen, geometry = tie(gather_line(colors), screen, geometry)
    geometry = across_view(geometry)
    own = gather_plane(line)
    w_first, token = weights(lists_first[0], loads_first[0], shift_first[0], screen, "weights_first")
    *own, token, geometry = tie(*own, token, geometry)
    slots = color_slots(lists_first[0], lists_first[0] % BINS)
    parts = first_render(slots, loads_first[0], token, w_first, target[0], swapped(own))
    screen = across_tile(screen_again(cameras_second[0], geometry))
    *parts, screen = tie(*parts, screen)
    w_second, token = weights(lists_second[0], loads_second[0], shift_second[0], screen, "weights_second")
    line, token = tie(scatter_far(parts), token)
    me = lax.axis_index("view").reshape(1)
    colors, packed = adam(owner_after, me, scatter_near(line), features, moment_first, moment_second)
    colors, packed = tie(exchange_views(colors), packed)
    packed = across_view(packed)
    blocks = swapped(gather_plane(gather_line(colors)))
    slots = color_slots(lists_second[0], place_of(lists_second[0] % BINS))
    image = second_render(slots, loads_second[0], token, w_second, blocks)
    new_features, new_first, new_second = (packed[:, i * C : i * C + C] for i in range(3))
    return (image[None], new_features, new_first, new_second)


def solution(mesh):
    return jax.shard_map(
        local,
        mesh=mesh,
        in_specs=(
            P(("view", "tile"), None, None),
            P(("view", "tile"), None, None),
            P(("view", "tile"), None, None),
            P(("view", "tile"), None, None),
            P(("view", "tile"), None),
            P(("view", "tile"), None),
            P("view", None, None),
            P("view", "tile", None),
            P("view", "tile", None),
            P("view", "tile"),
            P("view", "tile", None, None),
            P(("view", "tile")),
            P("view", None, None),
            P("view", "tile", None),
            P("view", "tile", None),
            P("view", "tile"),
        ),
        out_specs=(
            P("view", "tile", None, None),
            P(("view", "tile"), None, None),
            P(("view", "tile"), None, None),
            P(("view", "tile"), None, None),
        ),
        check_vma=False,
    )
```

profile of v0, /device:TPU:1, one launch (start us, length us, event | category | flops | bytes accessed | tf_op | source)
XLA Modules:
  0.0 171.2 jit_solution(6026644331887858361)
XLA Ops:
  0.7 2.0 %prep.1 = (bf16[8,64,128]{2,1,0:T(8,128)(2,1)}, bf16[32,32,128]{2,1,0:T(8,128)(2,1)}, f32[8,8,128]{2,1,0:T(8,128)}) custom-call(f32[1,2,4]{2,1,0:T(2,128)} %camera_hbm.1, s32[8]{0:T(128)} %owner.1, f32[8,64,128]{2,1,0:T(8,128)} %feat.1, f32[3,8,128]{2,1,0:T(8,128)} %bitcast.22, f32[8,128]{1,0:T(8,128)} %scales_hbm.1, f32[8,128]{1,0:T(8,128)} %opacity_hbm.1), custom_call_target="tpu_custom_call" | custom-call | tf_op jit(solution)/shard_map/prep/pallas_call | solution.py:116
  2.6 2.2 %collective-permute-start = (bf16[8,64,128]{2,1,0:T(8,128)(2,1)}, bf16[8,64,128]{2,1,0:T(8,128)(2,1)S(1)}, u32[]{:S(2)}, u32[]{:S(2)}) collective-permute-start(bf16[8,64,128]{2,1,0:T(8,128)(2,1)} %get-tuple-element.43), channel_id=1, source_target_pairs={{0,8},{1,3},{2,10},{3,5},{4,12},{5,7},{6,14},{7,1},{8,16},{9,11},{... | collective-permute-start | bytes 393224 | tf_op jit(solution)/shard_map/ppermute | solution.py:437
  4.8 2.6 %collective-permute-start.1 = (bf16[8,64,128]{2,1,0:T(8,128)(2,1)}, bf16[8,64,128]{2,1,0:T(8,128)(2,1)S(1)}, u32[]{:S(2)}, u32[]{:S(2)}) collective-permute-start(bf16[8,64,128]{2,1,0:T(8,128)(2,1)} %get-tuple-element.43), channel_id=1, source_target_pairs={{0,16},{1,5},{2,18},{3,7},{4,20},{5,1},{6,22},{7,3},{8,24},{9,13},... | collective-permute-start | bytes 393224 | tf_op jit(solution)/shard_map/ppermute | solution.py:437
  7.5 1.1 collective-permute-start.2
  8.5 6.0 %all-to-all-start = ((bf16[32,32,128]{2,1,0:T(8,128)(2,1)}), bf16[32,32,128]{2,1,0:T(8,128)(2,1)S(1)}, u32[]{:S(2)}, u32[]{:S(2)}) async-start(bf16[32,32,128]{2,1,0:T(8,128)(2,1)} %get-tuple-element.44), calls=%async_computation | async-start | bytes 524288 | tf_op jit(solution)/shard_map/all_to_all | solution.py:520
  14.6 1.0 pad_maximum_fusion.rest_0_
  15.5 8.0 %all-to-all-done.screen_hbm = bf16[32,32,128]{2,1,0:T(8,128)(2,1)S(1)} async-done(((bf16[32,32,128]{2,1,0:T(8,128)(2,1)}), bf16[32,32,128]{2,1,0:T(8,128)(2,1)S(1)}, u32[]{:S(2)}, u32[]{:S(2)}) %all-to-all-start) | async-done | bytes 262176 | tf_op jit(solution)/shard_map/all_to_all | solution.py:520
  23.8 1.7 %collective-permute-start.4 = (bf16[32,64,128]{2,1,0:T(8,128)(2,1)S(1)}, bf16[32,64,128]{2,1,0:T(8,128)(2,1)S(1)}, u32[]{:S(2)}, u32[]{:S(2)}) collective-permute-start(bf16[32,64,128]{2,1,0:T(8,128)(2,1)S(1)} %pad_maximum_fusion.rest_0_), channel_id=1, source_target_pairs={{0,4},{1,17},{2,6},{3,19},{4,0},{5,21},{6,2},{7,23},{8,12},{9,25},... | collective-permute-start | bytes 1572872 | tf_op jit(solution)/shard_map/ppermute | solution.py:437
  25.5 1.1 collective-permute-start.5
  26.6 8.2 %all-to-all-start.1 = ((f32[8,8,128]{2,1,0:T(8,128)}), f32[8,8,128]{2,1,0:T(8,128)S(1)}, u32[]{:S(2)}, u32[]{:S(2)}) async-start(f32[8,8,128]{2,1,0:T(8,128)} %get-tuple-element.49), calls=%async_computation.1 | async-start | bytes 65536 | tf_op jit(solution)/shard_map/all_to_all | solution.py:516
  34.8 9.3 %weights_first.1 = (bf16[16,8,128,256]{3,2,1,0:T(8,128)(2,1)}, f32[8,128]{1,0:T(8,128)}) custom-call(s32[8,16]{1,0:T(8,128)} %bitcast.23, s32[16]{0:T(128)} %bitcast.27, f32[2,16]{1,0:T(2,128)} %bitcast.31, bf16[32,32,128]{2,1,0:T(8,128)(2,1)} %copy-done.19), custom_call_target="tpu_custom_call" | custom-call | flops 58720256 | bytes 10000000 | tf_op jit(solution)/shard_map/weights_first/pallas_call | solution.py:256
  44.2 2.3 %collective-permute-start.6 = (bf16[32,64,128]{2,1,0:T(8,128)(2,1)S(1)}, bf16[32,64,128]{2,1,0:T(8,128)(2,1)S(1)}, u32[]{:S(2)}, u32[]{:S(2)}) collective-permute-start(bf16[32,64,128]{2,1,0:T(8,128)(2,1)S(1)} %pad_maximum_fusion.rest_0_), channel_id=1, source_target_pairs={{0,1},{1,0},{2,3},{3,2},{4,5},{5,4},{6,7},{7,6},{8,9},{9,8},{10,11... | collective-permute-start | bytes 1572872 | tf_op jit(solution)/shard_map/ppermute | solution.py:442
  47.2 1.4 screen_again.1
  48.6 7.6 %all-to-all-start.2 = ((bf16[32,32,128]{2,1,0:T(8,128)(2,1)}), bf16[32,32,128]{2,1,0:T(8,128)(2,1)S(1)}, u32[]{:S(2)}, u32[]{:S(2)}) async-start(bf16[32,32,128]{2,1,0:T(8,128)(2,1)} %screen_again.1), calls=%async_computation.2 | async-start | bytes 524288 | tf_op jit(solution)/shard_map/all_to_all | solution.py:520
  57.8 13.0 %first_render.1 = (f32[32,64,128]{2,1,0:T(8,128)}, f32[32,64,128]{2,1,0:T(8,128)}, f32[32,64,128]{2,1,0:T(8,128)}, f32[32,64,128]{2,1,0:T(8,128)}, f32[32,64,128...) custom-call(s32[16,8]{1,0:T(8,128)} %fusion.16.slots, s32[16]{0:T(128)} %bitcast.28, ...), custom_call_target="tpu_custom_call" | custom-call | flops 1073741824 | bytes 25000000 | tf_op jit(solution)/shard_map/first_render/pallas_call | solution.py:346
  72.2 1.9 %collective-permute-done.11 = f32[32,64,128]{2,1,0:T(8,128)S(1)} collective-permute-done((f32[32,64,128]{2,1,0:T(8,128)}, f32[32,64,128]{2,1,0:T(8,128)S(1)}, u32[]{:S(2)}, u32[]{:S(2)}) %collective-permute-start.11) | collective-permute-done | bytes 1048608 | tf_op jit(solution)/shard_map/ppermute | solution.py:442
  74.1 1.4 add_convert_fusion.2
  75.5 3.3 %collective-permute-start.12 = (f16[32,64,128]{2,1,0:T(8,128)(2,1)S(1)}, f16[32,64,128]{2,1,0:T(8,128)(2,1)S(1)}, u32[]{:S(2)}, u32[]{:S(2)}) collective-permute-start(f16[32,64,128]{2,1,0:T(8,128)(2,1)S(1)} %add_convert_fusion.2), channel_id=1, source_target_pairs={{0,4},{1,17},{2,6},{3,19},{4,0},{5,21},{6,2},{7,23},{8,12},{9,25},... | collective-permute-start | bytes 1572872 | tf_op jit(solution)/shard_map/ppermute | solution.py:437
  78.7 2.2 %add_convert_fusion.1 = f16[32,64,128]{2,1,0:T(8,128)(2,1)} fusion(f32[32,64,128]{2,1,0:T(8,128)} %get-tuple-element.69, f32[32,64,128]{2,1,0:T(8,128)S(1)} %collective-permute-done.13), kind=kLoop, calls=%fused_computation.2 | loop fusion | flops 524288 | bytes 2621440 | tf_op jit(solution)/shard_map/convert_element_type | solution.py:477
  80.9 1.5 collective-permute-start.14
  82.4 2.2 %add_convert_fusion = f16[32,64,128]{2,1,0:T(8,128)(2,1)} fusion(f32[32,64,128]{2,1,0:T(8,128)} %get-tuple-element.71, f32[32,64,128]{2,1,0:T(8,128)S(1)} %collective-permute-done.15), kind=kLoop, calls=%fused_computation.1 | loop fusion | flops 524288 | bytes 2621440 | tf_op jit(solution)/shard_map/convert_element_type | solution.py:477
  84.8 10.3 %weights_second.1 = (bf16[16,8,128,256]{3,2,1,0:T(8,128)(2,1)}, f32[8,128]{1,0:T(8,128)}) custom-call(s32[8,16]{1,0:T(8,128)} %bitcast.25, s32[16]{0:T(128)} %bitcast.29, f32[2,16]{1,0:T(2,128)} %bitcast.32, bf16[32,32,128]{2,1,0:T(8,128)(2,1)} %copy-done.18), custom_call_target="tpu_custom_call" | custom-call | flops 58720256 | bytes 10000000 | tf_op jit(solution)/shard_map/weights_second/pallas_call | solution.py:256
  95.1 0.9 copy-done.7
  96.1 2.0 %convert_add_fusion = f32[32,64,128]{2,1,0:T(8,128)S(1)} fusion(f16[32,64,128]{2,1,0:T(8,128)(2,1)} %collective-permute-done.16, f16[32,64,128]{2,1,0:T(8,128)(2,1)} %collective-permute-done.14, f16[32,64,128]{2,1,0:T(8,128)(2,1)S(1)} %collective-permute-done.12, f32[32,64,128]{2,1,0:T(8,128)S(1)} %copy-done.6, f32[32,64,128]{2,1,0:T(8,128)} %copy-done.7), kind=kLoop, calls=%fused_computation | loop fusion | flops 1835008 | bytes 4718592 | tf_op jit(solution)/shard_map/add | solution.py:477
  98.3 4.3 %collective-permute-start.17 = (f16[8,64,128]{2,1,0:T(8,128)(2,1)S(1)}, f16[8,64,128]{2,1,0:T(8,128)(2,1)S(1)}, u32[]{:S(2)}, u32[]{:S(2)}) collective-permute-start(f16[8,64,128]{2,1,0:T(8,128)(2,1)S(1)} %get-tuple-element.85), channel_id=1, source_target_pairs={{0,16},{1,5},{2,18},{3,7},{4,20},{5,1},{6,22},{7,3},{8,24},{9,13},... | collective-permute-start | bytes 393224 | tf_op jit(solution)/shard_map/ppermute | solution.py:437
  102.6 1.5 collective-permute-start.19
  104.1 0.9 collective-permute-done.17
  104.9 1.5 collective-permute-done.18
  106.4 1.5 collective-permute-done.19
  108.0 1.9 %adam.1 = (bf16[8,64,128]{2,1,0:T(8,128)(2,1)S(1)}, f32[8,192,128]{2,1,0:T(8,128)}) custom-call(s32[8]{0:T(128)S(1)} %copy-done.3, s32[1]{0:T(128)} %bitcast.13.me, f32[8,64,128]{2,1,0:T(8,128)S(1)} %convert_add_fusion.1.gradient, f32[8,64,128]{2,1,0:T(8,128)S(1)} %copy-done, f32[8,64,128]{2,1,0:T(8,128)S(1)} %copy-done.1, f32[8,64,128]{2,1,0:T(8,128)S(1)} %copy-done.2), custom_call_target="tpu_custom_call" | custom-call | tf_op jit(solution)/shard_map/adam/pallas_call | solution.py:413
  110.0 3.2 %collective-permute-start.20 = (bf16[4,64,128]{2,1,0:T(8,128)(2,1)S(1)}, bf16[4,64,128]{2,1,0:T(8,128)(2,1)S(1)}, u32[]{:S(2)}, u32[]{:S(2)}) collective-permute-start(bf16[4,64,128]{2,1,0:T(8,128)(2,1)S(1)} %slice.56), channel_id=1, source_target_pairs={{0,128},{32,160},{64,192},{96,224},{128,0},{160,32},{192,64},{224,... | collective-permute-start | bytes 196616 | tf_op jit(solution)/shard_map/ppermute | solution.py:503
  113.2 3.9 %collective-permute-done.20 = bf16[4,64,128]{2,1,0:T(8,128)(2,1)S(1)} collective-permute-done((bf16[4,64,128]{2,1,0:T(8,128)(2,1)S(1)}, bf16[4,64,128]{2,1,0:T(8,128)(2,1)S(1)}, u32[]{:S(2)}, u32[]{:S(2)}) %collective-permute-start.20) | collective-permute-done | bytes 65568 | tf_op jit(solution)/shard_map/ppermute | solution.py:503
  117.1 1.8 %collective-permute-start.23 = (bf16[2,64,128]{2,1,0:T(8,128)(2,1)S(1)}, bf16[2,64,128]{2,1,0:T(8,128)(2,1)S(1)}, u32[]{:S(2)}, u32[]{:S(2)}) collective-permute-start(bf16[2,64,128]{2,1,0:T(8,128)(2,1)S(1)} %pad_maximum_fusion.3), channel_id=1, source_target_pairs={{0,96},{32,64},{64,32},{96,0},{128,224},{160,192},{192,160},{224,1... | collective-permute-start | bytes 98312 | tf_op jit(solution)/shard_map/ppermute | solution.py:503
  118.9 1.2 collective-permute-start.21
  120.8 1.5 collective-permute-done.21
  122.3 1.9 %collective-permute-done.22 = bf16[2,64,128]{2,1,0:T(8,128)(2,1)S(1)} collective-permute-done((bf16[2,64,128]{2,1,0:T(8,128)(2,1)S(1)}, bf16[2,64,128]{2,1,0:T(8,128)(2,1)S(1)}, u32[]{:S(2)}, u32[]{:S(2)}) %collective-permute-start.22) | collective-permute-done | bytes 32800 | tf_op jit(solution)/shard_map/ppermute | solution.py:503
  124.3 1.0 collective-permute-start.25
  125.3 1.7 %collective-permute-start.26 = (bf16[8,64,128]{2,1,0:T(8,128)(2,1)S(1)}, bf16[8,64,128]{2,1,0:T(8,128)(2,1)S(1)}, u32[]{:S(2)}, u32[]{:S(2)}) collective-permute-start(bf16[8,64,128]{2,1,0:T(8,128)(2,1)S(1)} %constant_dynamic-update-slice_fusion), channel_id=1, source_target_pairs={{0,24},{1,7},{2,26},{3,1},{4,28},{5,3},{6,30},{7,5},{8,0},{9,15},{... | collective-permute-start | bytes 393224 | tf_op jit(solution)/shard_map/ppermute | solution.py:437
  127.1 4.7 %all-to-all-start.3 = ((f32[8,192,128]{2,1,0:T(8,128)}), f32[8,192,128]{2,1,0:T(8,128)S(1)}, u32[]{:S(2)}, u32[]{:S(2)}) async-start(f32[8,192,128]{2,1,0:T(8,128)} %get-tuple-element.81), calls=%async_computation.3 | async-start | bytes 1572864 | tf_op jit(solution)/shard_map/all_to_all | solution.py:516
  131.9 1.7 collective-permute-start.27
  133.6 2.0 %collective-permute-start.28 = (bf16[32,64,128]{2,1,0:T(8,128)(2,1)S(1)}, bf16[32,64,128]{2,1,0:T(8,128)(2,1)S(1)}, u32[]{:S(2)}, u32[]{:S(2)}) collective-permute-start(bf16[32,64,128]{2,1,0:T(8,128)(2,1)S(1)} %constant_dynamic-update-slice_fusion.5.rest_0_), channel_id=1, source_target_pairs={{0,4},{1,17},{2,6},{3,19},{4,0},{5,21},{6,2},{7,23},{8,12},{9,25},... | collective-permute-start | bytes 1572872 | tf_op jit(solution)/shard_map/ppermute | solution.py:437
  136.3 11.3 %collective-permute-start.30 = (bf16[32,64,128]{2,1,0:T(8,128)(2,1)S(1)}, bf16[32,64,128]{2,1,0:T(8,128)(2,1)S(1)}, u32[]{:S(2)}, u32[]{:S(2)}) collective-permute-start(bf16[32,64,128]{2,1,0:T(8,128)(2,1)S(1)} %constant_dynamic-update-slice_fusion.5.rest_0_), channel_id=1, source_target_pairs={{0,1},{1,0},{2,3},{3,2},{4,5},{5,4},{6,7},{7,6},{8,9},{9,8},{10,11... | collective-permute-start | bytes 1572872 | tf_op jit(solution)/shard_map/ppermute | solution.py:442
  148.4 5.0 %collective-permute-start.31 = (bf16[32,64,128]{2,1,0:T(8,128)(2,1)S(1)}, bf16[32,64,128]{2,1,0:T(8,128)(2,1)}, u32[]{:S(2)}, u32[]{:S(2)}) collective-permute-start(bf16[32,64,128]{2,1,0:T(8,128)(2,1)S(1)} %collective-permute-done.27.rest_1_), channel_id=1, source_target_pairs={{0,1},{1,0},{2,3},{3,2},{4,5},{5,4},{6,7},{7,6},{8,9},{9,8},{10,11... | collective-permute-start | bytes 1572872 | tf_op jit(solution)/shard_map/ppermute | solution.py:442
  153.3 7.1 %collective-permute-start.32 = (bf16[32,64,128]{2,1,0:T(8,128)(2,1)S(1)}, bf16[32,64,128]{2,1,0:T(8,128)(2,1)}, u32[]{:S(2)}, u32[]{:S(2)}) collective-permute-start(bf16[32,64,128]{2,1,0:T(8,128)(2,1)S(1)} %collective-permute-done.28.rest_2_), channel_id=1, source_target_pairs={{0,1},{1,0},{2,3},{3,2},{4,5},{5,4},{6,7},{7,6},{8,9},{9,8},{10,11... | collective-permute-start | bytes 1572872 | tf_op jit(solution)/shard_map/ppermute | solution.py:442
  161.2 0.8 collective-permute-done.32.rest_6_
  162.1 0.7 collective-permute-done.33.rest_7_
  162.8 7.5 %second_render.1 = f32[16,64,256]{2,1,0:T(8,128)} custom-call(s32[16,8]{1,0:T(8,128)} %fusion.9.slots, s32[16]{0:T(128)} %bitcast.30, f32[8,128]{1,0:T(8,128)} %get-tuple-element.75.token, bf16[16,8,128,256]{3,2,1,0:T(8,128)(2,1)} %get-tuple-element.76.w_hbm, bf16[32,64,128]{2,1,0:T(8,128)(2,1)} %copy-done.8, bf16[32,64,128]{2,1,0:T(8,128)(2,1)} %copy-done.14, ...), custom_call_target="tpu_custom_call" | custom-call | flops 536870912 | bytes 14000000 | tf_op jit(solution)/shard_map/second_render/pallas_call | solution.py:380
  170.4 0.9 fusion.27
  (105 shorter events, 7.4 us)
Async XLA Ops:
  0.6 46.5 %copy-start.20 = (s32[1,16,8]{1,2,0:T(8,128)S(1)}, s32[1,16,8]{1,2,0:T(8,128)}, u32[]{:S(2)}) copy-start(s32[1,16,8]{1,2,0:T(8,128)} %param.24) | copy-start | bytes 1540
  0.6 46.5 %copy-start.4 = (f32[1,2,4]{2,1,0:T(2,128)S(1)}, f32[1,2,4]{2,1,0:T(2,128)}, u32[]{:S(2)}) copy-start(f32[1,2,4]{2,1,0:T(2,128)} %param.28) | copy-start | bytes 100
  2.6 11.9 %collective-permute-start = (bf16[8,64,128]{2,1,0:T(8,128)(2,1)}, bf16[8,64,128]{2,1,0:T(8,128)(2,1)S(1)}, u32[]{:S(2)}, u32[]{:S(2)}) collective-permute-start(bf16[8,64,128]{2,1,0:T(8,128)(2,1)} %get-tuple-element.43), channel_id=1, source_target_pairs={{0,8},{1,3},{2,10},{3,5},{4,12},{5,7},{6,14},{7,1},{8,16},{9,11},{... | collective-permute-start | bytes 393224 | tf_op jit(solution)/shard_map/ppermute | solution.py:437
  4.8 9.7 %collective-permute-start.1 = (bf16[8,64,128]{2,1,0:T(8,128)(2,1)}, bf16[8,64,128]{2,1,0:T(8,128)(2,1)S(1)}, u32[]{:S(2)}, u32[]{:S(2)}) collective-permute-start(bf16[8,64,128]{2,1,0:T(8,128)(2,1)} %get-tuple-element.43), channel_id=1, source_target_pairs={{0,16},{1,5},{2,18},{3,7},{4,20},{5,1},{6,22},{7,3},{8,24},{9,13},... | collective-permute-start | bytes 393224 | tf_op jit(solution)/shard_map/ppermute | solution.py:437
  7.5 7.1 %collective-permute-start.2 = (bf16[8,64,128]{2,1,0:T(8,128)(2,1)}, bf16[8,64,128]{2,1,0:T(8,128)(2,1)S(1)}, u32[]{:S(2)}, u32[]{:S(2)}) collective-permute-start(bf16[8,64,128]{2,1,0:T(8,128)(2,1)} %get-tuple-element.43), channel_id=1, source_target_pairs={{0,24},{1,7},{2,26},{3,1},{4,28},{5,3},{6,30},{7,5},{8,0},{9,15},{... | collective-permute-start | bytes 393224 | tf_op jit(solution)/shard_map/ppermute | solution.py:437
  8.5 15.0 %all-to-all-start = ((bf16[32,32,128]{2,1,0:T(8,128)(2,1)}), bf16[32,32,128]{2,1,0:T(8,128)(2,1)S(1)}, u32[]{:S(2)}, u32[]{:S(2)}) async-start(bf16[32,32,128]{2,1,0:T(8,128)(2,1)} %get-tuple-element.44), calls=%async_computation | async-start | bytes 524288 | tf_op jit(solution)/shard_map/all_to_all | solution.py:520
  15.5 41.4 %copy-start.5 = (bf16[32,64,128]{2,1,0:T(8,128)(2,1)}, bf16[32,64,128]{2,1,0:T(8,128)(2,1)S(1)}, u32[]{:S(2)}) copy-start(bf16[32,64,128]{2,1,0:T(8,128)(2,1)S(1)} %pad_maximum_fusion.rest_0_) | copy-start | bytes 1572868
  23.5 20.6 %collective-permute-start.3 = (bf16[32,64,128]{2,1,0:T(8,128)(2,1)S(1)}, bf16[32,64,128]{2,1,0:T(8,128)(2,1)S(1)}, u32[]{:S(2)}, u32[]{:S(2)}) collective-permute-start(bf16[32,64,128]{2,1,0:T(8,128)(2,1)S(1)} %pad_maximum_fusion.rest_0_), channel_id=1, source_target_pairs={{0,2},{1,9},{2,4},{3,11},{4,6},{5,13},{6,0},{7,15},{8,10},{9,17},{... | collective-permute-start | bytes 1572872 | tf_op jit(solution)/shard_map/ppermute | solution.py:437
  23.8 20.4 %collective-permute-start.4 = (bf16[32,64,128]{2,1,0:T(8,128)(2,1)S(1)}, bf16[32,64,128]{2,1,0:T(8,128)(2,1)S(1)}, u32[]{:S(2)}, u32[]{:S(2)}) collective-permute-start(bf16[32,64,128]{2,1,0:T(8,128)(2,1)S(1)} %pad_maximum_fusion.rest_0_), channel_id=1, source_target_pairs={{0,4},{1,17},{2,6},{3,19},{4,0},{5,21},{6,2},{7,23},{8,12},{9,25},... | collective-permute-start | bytes 1572872 | tf_op jit(solution)/shard_map/ppermute | solution.py:437
  25.5 18.7 %collective-permute-start.5 = (bf16[32,64,128]{2,1,0:T(8,128)(2,1)S(1)}, bf16[32,64,128]{2,1,0:T(8,128)(2,1)S(1)}, u32[]{:S(2)}, u32[]{:S(2)}) collective-permute-start(bf16[32,64,128]{2,1,0:T(8,128)(2,1)S(1)} %pad_maximum_fusion.rest_0_), channel_id=1, source_target_pairs={{0,6},{1,25},{2,0},{3,27},{4,2},{5,29},{6,4},{7,31},{8,14},{9,1},{... | collective-permute-start | bytes 1572872 | tf_op jit(solution)/shard_map/ppermute | solution.py:437
  26.6 17.5 %all-to-all-start.1 = ((f32[8,8,128]{2,1,0:T(8,128)}), f32[8,8,128]{2,1,0:T(8,128)S(1)}, u32[]{:S(2)}, u32[]{:S(2)}) async-start(f32[8,8,128]{2,1,0:T(8,128)} %get-tuple-element.49), calls=%async_computation.1 | async-start | bytes 65536 | tf_op jit(solution)/shard_map/all_to_all | solution.py:516
  44.2 12.6 %collective-permute-start.6 = (bf16[32,64,128]{2,1,0:T(8,128)(2,1)S(1)}, bf16[32,64,128]{2,1,0:T(8,128)(2,1)S(1)}, u32[]{:S(2)}, u32[]{:S(2)}) collective-permute-start(bf16[32,64,128]{2,1,0:T(8,128)(2,1)S(1)} %pad_maximum_fusion.rest_0_), channel_id=1, source_target_pairs={{0,1},{1,0},{2,3},{3,2},{4,5},{5,4},{6,7},{7,6},{8,9},{9,8},{10,11... | collective-permute-start | bytes 1572872 | tf_op jit(solution)/shard_map/ppermute | solution.py:442
  46.5 10.4 %collective-permute-start.7 = (bf16[32,64,128]{2,1,0:T(8,128)(2,1)S(1)}, bf16[32,64,128]{2,1,0:T(8,128)(2,1)S(1)}, u32[]{:S(2)}, u32[]{:S(2)}) collective-permute-start(bf16[32,64,128]{2,1,0:T(8,128)(2,1)S(1)} %collective-permute-done.3.rest_1_), channel_id=1, source_target_pairs={{0,1},{1,0},{2,3},{3,2},{4,5},{5,4},{6,7},{7,6},{8,9},{9,8},{10,11... | collective-permute-start | bytes 1572872 | tf_op jit(solution)/shard_map/ppermute | solution.py:442
  46.6 10.3 %collective-permute-start.8 = (bf16[32,64,128]{2,1,0:T(8,128)(2,1)S(1)}, bf16[32,64,128]{2,1,0:T(8,128)(2,1)}, u32[]{:S(2)}, u32[]{:S(2)}) collective-permute-start(bf16[32,64,128]{2,1,0:T(8,128)(2,1)S(1)} %collective-permute-done.4.rest_2_), channel_id=1, source_target_pairs={{0,1},{1,0},{2,3},{3,2},{4,5},{5,4},{6,7},{7,6},{8,9},{9,8},{10,11... | collective-permute-start | bytes 1572872 | tf_op jit(solution)/shard_map/ppermute | solution.py:442
  47.0 9.9 %collective-permute-start.9 = (bf16[32,64,128]{2,1,0:T(8,128)(2,1)S(1)}, bf16[32,64,128]{2,1,0:T(8,128)(2,1)}, u32[]{:S(2)}, u32[]{:S(2)}) collective-permute-start(bf16[32,64,128]{2,1,0:T(8,128)(2,1)S(1)} %collective-permute-done.5.rest_3_), channel_id=1, source_target_pairs={{0,1},{1,0},{2,3},{3,2},{4,5},{5,4},{6,7},{7,6},{8,9},{9,8},{10,11... | collective-permute-start | bytes 1572872 | tf_op jit(solution)/shard_map/ppermute | solution.py:442
  48.6 22.2 %all-to-all-start.2 = ((bf16[32,32,128]{2,1,0:T(8,128)(2,1)}), bf16[32,32,128]{2,1,0:T(8,128)(2,1)S(1)}, u32[]{:S(2)}, u32[]{:S(2)}) async-start(bf16[32,32,128]{2,1,0:T(8,128)(2,1)} %screen_again.1), calls=%async_computation.2 | async-start | bytes 524288 | tf_op jit(solution)/shard_map/all_to_all | solution.py:520
  70.8 25.3 %copy-start.6 = (f32[32,64,128]{2,1,0:T(8,128)S(1)}, f32[32,64,128]{2,1,0:T(8,128)}, u32[]{:S(2)}) copy-start(f32[32,64,128]{2,1,0:T(8,128)} %get-tuple-element.65) | copy-start | bytes 3145732
  70.9 3.2 %collective-permute-start.11 = (f32[32,64,128]{2,1,0:T(8,128)}, f32[32,64,128]{2,1,0:T(8,128)S(1)}, u32[]{:S(2)}, u32[]{:S(2)}) collective-permute-start(f32[32,64,128]{2,1,0:T(8,128)} %get-tuple-element.68), channel_id=1, source_target_pairs={{0,1},{1,0},{2,3},{3,2},{4,5},{5,4},{6,7},{7,6},{8,9},{9,8},{10,11... | collective-permute-start | bytes 3145736 | tf_op jit(solution)/shard_map/ppermute | solution.py:442
  71.6 7.2 %collective-permute-start.13 = (f32[32,64,128]{2,1,0:T(8,128)}, f32[32,64,128]{2,1,0:T(8,128)S(1)}, u32[]{:S(2)}, u32[]{:S(2)}) collective-permute-start(f32[32,64,128]{2,1,0:T(8,128)} %get-tuple-element.70), channel_id=1, source_target_pairs={{0,1},{1,0},{2,3},{3,2},{4,5},{5,4},{6,7},{7,6},{8,9},{9,8},{10,11... | collective-permute-start | bytes 3145736 | tf_op jit(solution)/shard_map/ppermute | solution.py:442
  71.7 10.8 %collective-permute-start.15 = (f32[32,64,128]{2,1,0:T(8,128)}, f32[32,64,128]{2,1,0:T(8,128)S(1)}, u32[]{:S(2)}, u32[]{:S(2)}) collective-permute-start(f32[32,64,128]{2,1,0:T(8,128)} %get-tuple-element.72), channel_id=1, source_target_pairs={{0,1},{1,0},{2,3},{3,2},{4,5},{5,4},{6,7},{7,6},{8,9},{9,8},{10,11... | collective-permute-start | bytes 3145736 | tf_op jit(solution)/shard_map/ppermute | solution.py:442
  72.1 23.0 %collective-permute-start.10 = (f32[32,64,128]{2,1,0:T(8,128)}, f32[32,64,128]{2,1,0:T(8,128)S(1)}, u32[]{:S(2)}, u32[]{:S(2)}) collective-permute-start(f32[32,64,128]{2,1,0:T(8,128)} %get-tuple-element.66), channel_id=1, source_target_pairs={{0,1},{1,0},{2,3},{3,2},{4,5},{5,4},{6,7},{7,6},{8,9},{9,8},{10,11... | collective-permute-start | bytes 3145736 | tf_op jit(solution)/shard_map/ppermute | solution.py:442
  75.5 19.7 %collective-permute-start.12 = (f16[32,64,128]{2,1,0:T(8,128)(2,1)S(1)}, f16[32,64,128]{2,1,0:T(8,128)(2,1)S(1)}, u32[]{:S(2)}, u32[]{:S(2)}) collective-permute-start(f16[32,64,128]{2,1,0:T(8,128)(2,1)S(1)} %add_convert_fusion.2), channel_id=1, source_target_pairs={{0,4},{1,17},{2,6},{3,19},{4,0},{5,21},{6,2},{7,23},{8,12},{9,25},... | collective-permute-start | bytes 1572872 | tf_op jit(solution)/shard_map/ppermute | solution.py:437
  80.9 14.2 %collective-permute-start.14 = (f16[32,64,128]{2,1,0:T(8,128)(2,1)}, f16[32,64,128]{2,1,0:T(8,128)(2,1)}, u32[]{:S(2)}, u32[]{:S(2)}) collective-permute-start(f16[32,64,128]{2,1,0:T(8,128)(2,1)} %add_convert_fusion.1), channel_id=1, source_target_pairs={{0,6},{1,25},{2,0},{3,27},{4,2},{5,29},{6,4},{7,31},{8,14},{9,1},{... | collective-permute-start | bytes 1572872 | tf_op jit(solution)/shard_map/ppermute | solution.py:437
  84.7 23.3 %copy-start = (f32[8,64,128]{2,1,0:T(8,128)S(1)}, f32[8,64,128]{2,1,0:T(8,128)}, u32[]{:S(2)}) copy-start(f32[8,64,128]{2,1,0:T(8,128)} %feat.1) | copy-start | bytes 786436
  84.7 23.3 %copy-start.1 = (f32[8,64,128]{2,1,0:T(8,128)S(1)}, f32[8,64,128]{2,1,0:T(8,128)}, u32[]{:S(2)}) copy-start(f32[8,64,128]{2,1,0:T(8,128)} %m1.1) | copy-start | bytes 786436
  84.7 23.3 %copy-start.2 = (f32[8,64,128]{2,1,0:T(8,128)S(1)}, f32[8,64,128]{2,1,0:T(8,128)}, u32[]{:S(2)}) copy-start(f32[8,64,128]{2,1,0:T(8,128)} %m2.1) | copy-start | bytes 786436
  84.7 23.4 %copy-start.3 = (s32[8]{0:T(128)S(1)}, s32[8]{0:T(128)}, u32[]{:S(2)}) copy-start(s32[8]{0:T(128)} %owner.1) | copy-start | bytes 100
  84.7 11.4 %collective-permute-start.16 = (f16[32,64,128]{2,1,0:T(8,128)(2,1)}, f16[32,64,128]{2,1,0:T(8,128)(2,1)}, u32[]{:S(2)}, u32[]{:S(2)}) collective-permute-start(f16[32,64,128]{2,1,0:T(8,128)(2,1)} %add_convert_fusion), channel_id=1, source_target_pairs={{0,2},{1,9},{2,4},{3,11},{4,6},{5,13},{6,0},{7,15},{8,10},{9,17},{... | collective-permute-start | bytes 1572872 | tf_op jit(solution)/shard_map/ppermute | solution.py:437
  84.8 75.7 %copy-start.21 = (s32[1,16,8]{1,2,0:T(8,128)S(1)}, s32[1,16,8]{1,2,0:T(8,128)}, u32[]{:S(2)}) copy-start(s32[1,16,8]{1,2,0:T(8,128)} %param.30) | copy-start | bytes 1540
  98.3 6.7 %collective-permute-start.17 = (f16[8,64,128]{2,1,0:T(8,128)(2,1)S(1)}, f16[8,64,128]{2,1,0:T(8,128)(2,1)S(1)}, u32[]{:S(2)}, u32[]{:S(2)}) collective-permute-start(f16[8,64,128]{2,1,0:T(8,128)(2,1)S(1)} %get-tuple-element.85), channel_id=1, source_target_pairs={{0,16},{1,5},{2,18},{3,7},{4,20},{5,1},{6,22},{7,3},{8,24},{9,13},... | collective-permute-start | bytes 393224 | tf_op jit(solution)/shard_map/ppermute | solution.py:437
  102.6 3.8 %collective-permute-start.18 = (f16[8,64,128]{2,1,0:T(8,128)(2,1)S(1)}, f16[8,64,128]{2,1,0:T(8,128)(2,1)S(1)}, u32[]{:S(2)}, u32[]{:S(2)}) collective-permute-start(f16[8,64,128]{2,1,0:T(8,128)(2,1)S(1)} %get-tuple-element.87), channel_id=1, source_target_pairs={{0,24},{1,7},{2,26},{3,1},{4,28},{5,3},{6,30},{7,5},{8,0},{9,15},{... | collective-permute-start | bytes 393224 | tf_op jit(solution)/shard_map/ppermute | solution.py:437
  102.6 5.3 %collective-permute-start.19 = (f16[8,64,128]{2,1,0:T(8,128)(2,1)S(1)}, f16[8,64,128]{2,1,0:T(8,128)(2,1)S(1)}, u32[]{:S(2)}, u32[]{:S(2)}) collective-permute-start(f16[8,64,128]{2,1,0:T(8,128)(2,1)S(1)} %get-tuple-element.86), channel_id=1, source_target_pairs={{0,8},{1,3},{2,10},{3,5},{4,12},{5,7},{6,14},{7,1},{8,16},{9,11},{... | collective-permute-start | bytes 393224 | tf_op jit(solution)/shard_map/ppermute | solution.py:437
  110.0 7.1 %collective-permute-start.20 = (bf16[4,64,128]{2,1,0:T(8,128)(2,1)S(1)}, bf16[4,64,128]{2,1,0:T(8,128)(2,1)S(1)}, u32[]{:S(2)}, u32[]{:S(2)}) collective-permute-start(bf16[4,64,128]{2,1,0:T(8,128)(2,1)S(1)} %slice.56), channel_id=1, source_target_pairs={{0,128},{32,160},{64,192},{96,224},{128,0},{160,32},{192,64},{224,... | collective-permute-start | bytes 196616 | tf_op jit(solution)/shard_map/ppermute | solution.py:503
  117.1 7.1 %collective-permute-start.23 = (bf16[2,64,128]{2,1,0:T(8,128)(2,1)S(1)}, bf16[2,64,128]{2,1,0:T(8,128)(2,1)S(1)}, u32[]{:S(2)}, u32[]{:S(2)}) collective-permute-start(bf16[2,64,128]{2,1,0:T(8,128)(2,1)S(1)} %pad_maximum_fusion.3), channel_id=1, source_target_pairs={{0,96},{32,64},{64,32},{96,0},{128,224},{160,192},{192,160},{224,1... | collective-permute-start | bytes 98312 | tf_op jit(solution)/shard_map/ppermute | solution.py:503
  118.9 3.4 %collective-permute-start.21 = (bf16[2,64,128]{2,1,0:T(8,128)(2,1)S(1)}, bf16[2,64,128]{2,1,0:T(8,128)(2,1)S(1)}, u32[]{:S(2)}, u32[]{:S(2)}) collective-permute-start(bf16[2,64,128]{2,1,0:T(8,128)(2,1)S(1)} %pad_maximum_fusion.1), channel_id=1, source_target_pairs={{0,32},{32,0},{64,96},{96,64},{128,160},{160,128},{192,224},{224,1... | collective-permute-start | bytes 98312 | tf_op jit(solution)/shard_map/ppermute | solution.py:503
  120.1 4.1 %collective-permute-start.22 = (bf16[2,64,128]{2,1,0:T(8,128)(2,1)S(1)}, bf16[2,64,128]{2,1,0:T(8,128)(2,1)S(1)}, u32[]{:S(2)}, u32[]{:S(2)}) collective-permute-start(bf16[2,64,128]{2,1,0:T(8,128)(2,1)S(1)} %pad_maximum_fusion.2), channel_id=1, source_target_pairs={{0,64},{32,96},{64,0},{96,32},{128,192},{160,224},{192,128},{224,1... | collective-permute-start | bytes 98312 | tf_op jit(solution)/shard_map/ppermute | solution.py:503
  124.2 7.6 %collective-permute-start.24 = (bf16[8,64,128]{2,1,0:T(8,128)(2,1)S(1)}, bf16[8,64,128]{2,1,0:T(8,128)(2,1)S(1)}, u32[]{:S(2)}, u32[]{:S(2)}) collective-permute-start(bf16[8,64,128]{2,1,0:T(8,128)(2,1)S(1)} %constant_dynamic-update-slice_fusion), channel_id=1, source_target_pairs={{0,8},{1,3},{2,10},{3,5},{4,12},{5,7},{6,14},{7,1},{8,16},{9,11},{... | collective-permute-start | bytes 393224 | tf_op jit(solution)/shard_map/ppermute | solution.py:437
  124.3 7.5 %collective-permute-start.25 = (bf16[8,64,128]{2,1,0:T(8,128)(2,1)S(1)}, bf16[8,64,128]{2,1,0:T(8,128)(2,1)S(1)}, u32[]{:S(2)}, u32[]{:S(2)}) collective-permute-start(bf16[8,64,128]{2,1,0:T(8,128)(2,1)S(1)} %constant_dynamic-update-slice_fusion), channel_id=1, source_target_pairs={{0,16},{1,5},{2,18},{3,7},{4,20},{5,1},{6,22},{7,3},{8,24},{9,13},... | collective-permute-start | bytes 393224 | tf_op jit(solution)/shard_map/ppermute | solution.py:437
  125.3 6.5 %collective-permute-start.26 = (bf16[8,64,128]{2,1,0:T(8,128)(2,1)S(1)}, bf16[8,64,128]{2,1,0:T(8,128)(2,1)S(1)}, u32[]{:S(2)}, u32[]{:S(2)}) collective-permute-start(bf16[8,64,128]{2,1,0:T(8,128)(2,1)S(1)} %constant_dynamic-update-slice_fusion), channel_id=1, source_target_pairs={{0,24},{1,7},{2,26},{3,1},{4,28},{5,3},{6,30},{7,5},{8,0},{9,15},{... | collective-permute-start | bytes 393224 | tf_op jit(solution)/shard_map/ppermute | solution.py:437
  127.1 43.3 %all-to-all-start.3 = ((f32[8,192,128]{2,1,0:T(8,128)}), f32[8,192,128]{2,1,0:T(8,128)S(1)}, u32[]{:S(2)}, u32[]{:S(2)}) async-start(f32[8,192,128]{2,1,0:T(8,128)} %get-tuple-element.81), calls=%async_computation.3 | async-start | bytes 1572864 | tf_op jit(solution)/shard_map/all_to_all | solution.py:516
  131.9 30.9 %copy-start.8 = (bf16[32,64,128]{2,1,0:T(8,128)(2,1)}, bf16[32,64,128]{2,1,0:T(8,128)(2,1)S(1)}, u32[]{:S(2)}) copy-start(bf16[32,64,128]{2,1,0:T(8,128)(2,1)S(1)} %constant_dynamic-update-slice_fusion.5.rest_0_) | copy-start | bytes 1572868
  131.9 16.4 %collective-permute-start.27 = (bf16[32,64,128]{2,1,0:T(8,128)(2,1)S(1)}, bf16[32,64,128]{2,1,0:T(8,128)(2,1)S(1)}, u32[]{:S(2)}, u32[]{:S(2)}) collective-permute-start(bf16[32,64,128]{2,1,0:T(8,128)(2,1)S(1)} %constant_dynamic-update-slice_fusion.5.rest_0_), channel_id=1, source_target_pairs={{0,2},{1,9},{2,4},{3,11},{4,6},{5,13},{6,0},{7,15},{8,10},{9,17},{... | collective-permute-start | bytes 1572872 | tf_op jit(solution)/shard_map/ppermute | solution.py:437
  133.6 19.7 %collective-permute-start.28 = (bf16[32,64,128]{2,1,0:T(8,128)(2,1)S(1)}, bf16[32,64,128]{2,1,0:T(8,128)(2,1)S(1)}, u32[]{:S(2)}, u32[]{:S(2)}) collective-permute-start(bf16[32,64,128]{2,1,0:T(8,128)(2,1)S(1)} %constant_dynamic-update-slice_fusion.5.rest_0_), channel_id=1, source_target_pairs={{0,4},{1,17},{2,6},{3,19},{4,0},{5,21},{6,2},{7,23},{8,12},{9,25},... | collective-permute-start | bytes 1572872 | tf_op jit(solution)/shard_map/ppermute | solution.py:437
  135.6 24.8 %collective-permute-start.29 = (bf16[32,64,128]{2,1,0:T(8,128)(2,1)S(1)}, bf16[32,64,128]{2,1,0:T(8,128)(2,1)S(1)}, u32[]{:S(2)}, u32[]{:S(2)}) collective-permute-start(bf16[32,64,128]{2,1,0:T(8,128)(2,1)S(1)} %constant_dynamic-update-slice_fusion.5.rest_0_), channel_id=1, source_target_pairs={{0,6},{1,25},{2,0},{3,27},{4,2},{5,29},{6,4},{7,31},{8,14},{9,1},{... | collective-permute-start | bytes 1572872 | tf_op jit(solution)/shard_map/ppermute | solution.py:437
  136.3 24.9 %collective-permute-start.30 = (bf16[32,64,128]{2,1,0:T(8,128)(2,1)S(1)}, bf16[32,64,128]{2,1,0:T(8,128)(2,1)S(1)}, u32[]{:S(2)}, u32[]{:S(2)}) collective-permute-start(bf16[32,64,128]{2,1,0:T(8,128)(2,1)S(1)} %constant_dynamic-update-slice_fusion.5.rest_0_), channel_id=1, source_target_pairs={{0,1},{1,0},{2,3},{3,2},{4,5},{5,4},{6,7},{7,6},{8,9},{9,8},{10,11... | collective-permute-start | bytes 1572872 | tf_op jit(solution)/shard_map/ppermute | solution.py:442
  148.4 12.9 %collective-permute-start.31 = (bf16[32,64,128]{2,1,0:T(8,128)(2,1)S(1)}, bf16[32,64,128]{2,1,0:T(8,128)(2,1)}, u32[]{:S(2)}, u32[]{:S(2)}) collective-permute-start(bf16[32,64,128]{2,1,0:T(8,128)(2,1)S(1)} %collective-permute-done.27.rest_1_), channel_id=1, source_target_pairs={{0,1},{1,0},{2,3},{3,2},{4,5},{5,4},{6,7},{7,6},{8,9},{9,8},{10,11... | collective-permute-start | bytes 1572872 | tf_op jit(solution)/shard_map/ppermute | solution.py:442
  153.3 8.7 %collective-permute-start.32 = (bf16[32,64,128]{2,1,0:T(8,128)(2,1)S(1)}, bf16[32,64,128]{2,1,0:T(8,128)(2,1)}, u32[]{:S(2)}, u32[]{:S(2)}) collective-permute-start(bf16[32,64,128]{2,1,0:T(8,128)(2,1)S(1)} %collective-permute-done.28.rest_2_), channel_id=1, source_target_pairs={{0,1},{1,0},{2,3},{3,2},{4,5},{5,4},{6,7},{7,6},{8,9},{9,8},{10,11... | collective-permute-start | bytes 1572872 | tf_op jit(solution)/shard_map/ppermute | solution.py:442
  160.4 2.4 %collective-permute-start.33 = (bf16[32,64,128]{2,1,0:T(8,128)(2,1)S(1)}, bf16[32,64,128]{2,1,0:T(8,128)(2,1)}, u32[]{:S(2)}, u32[]{:S(2)}) collective-permute-start(bf16[32,64,128]{2,1,0:T(8,128)(2,1)S(1)} %collective-permute-done.29.rest_3_), channel_id=1, source_target_pairs={{0,1},{1,0},{2,3},{3,2},{4,5},{5,4},{6,7},{7,6},{8,9},{9,8},{10,11... | collective-permute-start | bytes 1572872 | tf_op jit(solution)/shard_map/ppermute | solution.py:442
  (12 other events, 81.6 us)
where the time goes:
time: 171 us
  starting transfers between devices  87.8 us (51%)
  Pallas kernels  45.4 us (27%)
  waiting for transfers between devices  23.4 us (14%)
  other arithmetic  10.3 us (6%)
  local copies, waits for them, and re-layouts  3.18 us (2%)
    ppermute x12, starting transfers between devices, swap_core(): return lax.ppermute(value, 'tile', pairs)  27.6 us
    ppermute x18, starting transfers between devices, shift_by(): return lax.ppermute(value, 'tile', pairs)  26.8 us
    pallas_call x2, Pallas kernels, weights(): pl.pallas_call(weights_kernel, out_shape=(jax.ShapeDtypeStruct((TILES, LB...  19.6 us
    all_to_all x2, starting transfers between devices, across_tile(): lax.all_to_all(value, 'tile', split_axis=0, concat_axis=0, tiled=True)  13.6 us
    pallas_call x1, Pallas kernels, first_render(): pl.pallas_call(first_kernel, out_shape=(jax.ShapeDtypeStruct((32, C, GB),...  13 us
    all_to_all x2, starting transfers between devices, across_view(): lax.all_to_all(value, 'view', split_axis=0, concat_axis=0, tiled=True)  12.9 us
    all_to_all x2, waiting for transfers between devices, across_tile(): lax.all_to_all(value, 'tile', split_axis=0, concat_axis=0, tiled=True)  7.97 us
    pallas_call x1, Pallas kernels, second_render(): pl.pallas_call(second_kernel, out_shape=jax.ShapeDtypeStruct((TILES, C, P...  7.49 us
  transfers between devices with their start and end apart: 38, of which 11 were waited for; matrix products, arithmetic and copies ran while one was open for 5% of the time, Pallas kernels for 24%

commit v1 on v0

--- a/solution.py
+++ b/solution.py
@@ -456,26 +456,30 @@
     return jnp.concatenate([near[k] for k in range(4)], axis=0)
 
 
-def gather_plane(line):
+def gather_plane(line, later=None):
     plane = {0: line}
     for k in ORDER:
+        if later is not None and k == ORDER[-1]:
+            line, later = tie(line, later)
         plane[k] = shift_by(line, 1, k)
-    return [plane[k] for k in range(4)]
+    own = [plane[k] for k in range(4)]
+    return own if later is None else (own, later)
 
 
 def swapped(own):
     return list(own) + [swap_core(block) for block in own]
 
 
-def scatter_far(parts):
+def scatter_far(parts, later):
     half16 = jnp.float16
-    summed = {}
-    for k in ORDER + (0,):
-        summed[k] = parts[k] + swap_core(parts[4 + k])
-    line = summed[0]
+    sent = {}
     for k in ORDER:
-        line = line + shift_by(summed[k].astype(half16), 1, -k).astype(f32)
-    return line
+        sent[k] = (parts[k] + swap_core(parts[4 + k])).astype(half16)
+    line = parts[0] + swap_core(parts[4])
+    sent[3], later = tie(sent[3], later)
+    for k in ORDER:
+        line = line + shift_by(sent[k], 1, -k).astype(f32)
+    return line, later
 
 
 def scatter_near(line):
@@ -499,17 +503,15 @@
 
 
 def exchange_views(colors):
-    def step(value, r):
-        return lax.ppermute(value, "view", [(v, v ^ r) for v in range(N_VIEW)])
-
-    handed = step(colors[4:], 4)
-    pairs = [jnp.concatenate([colors[r : r + 1], handed[r : r + 1]], axis=0) for r in range(4)]
-    return jnp.concatenate([pairs[0]] + [step(pairs[r], r) for r in (1, 2, 3)], axis=0)
+    def step(r):
+        return lax.ppermute(colors[r : r + 1], "view", [(v, v ^ r) for v in range(N_VIEW)])
+
+    got = {r: step(r) for r in (4, 5, 3, 6, 2, 7, 1)}
+    return jnp.concatenate([colors[0:1]] + [got[r] for r in range(1, N_VIEW)], axis=0)
 
 
 def place_of(view):
-    r = view ^ lax.axis_index("view")
-    return (r % 4) * 2 + r // 4
+    return view ^ lax.axis_index("view")
 
 
 def across_view(value):
@@ -541,22 +543,22 @@
     positions = jnp.transpose(positions, (1, 0, 2))
     colors, screen, geometry = prep(cameras_first, owner_after, features, positions, scales, opacity)
     screen = across_tile(screen)
-    line, screen, geometry = tie(gather_line(colors), screen, geometry)
-    geometry = across_view(geometry)
-    own = gather_plane(line)
+    own, screen = gather_plane(gather_line(colors), screen)
     w_first, token = weights(lists_first[0], loads_first[0], shift_first[0], screen, "weights_first")
-    *own, token, geometry = tie(*own, token, geometry)
+    *own, token = tie(*own, token)
     slots = color_slots(lists_first[0], lists_first[0] % BINS)
     parts = first_render(slots, loads_first[0], token, w_first, target[0], swapped(own))
-    screen = across_tile(screen_again(cameras_second[0], geometry))
-    *parts, screen = tie(*parts, screen)
+    line, geometry = scatter_far(parts, geometry)
+    screen = screen_again(cameras_second[0], across_view(geometry))
+    line, screen = tie(line, screen)
+    gradient, screen = tie(scatter_near(line), across_tile(screen))
     w_second, token = weights(lists_second[0], loads_second[0], shift_second[0], screen, "weights_second")
-    line, token = tie(scatter_far(parts), token)
     me = lax.axis_index("view").reshape(1)
-    colors, packed = adam(owner_after, me, scatter_near(line), features, moment_first, moment_second)
+    colors, packed = adam(owner_after, me, gradient, features, moment_first, moment_second)
     colors, packed = tie(exchange_views(colors), packed)
     packed = across_view(packed)
-    blocks = swapped(gather_plane(gather_line(colors)))
+    *own, token = tie(*gather_plane(gather_line(colors)), token)
+    blocks = swapped(own)
     slots = color_slots(lists_second[0], place_of(lists_second[0] % BINS))
     image = second_render(slots, loads_second[0], token, w_second, blocks)
     new_features, new_first, new_second = (packed[:, i * C : i * C + C] for i in range(3))

time: 171 us -> 161 us (0.942)
  starting transfers between devices: 87.8 us -> 62.3 us
  blocking collectives: 0 us -> 15.2 us
  Pallas kernels: 45.4 us -> 50.7 us
  other arithmetic: 10.3 us -> 6.1 us
    ppermute x12, starting transfers between devices: 27.6 us -> 8.54 us  [swap_core(): return lax.ppermute(value, 'tile', pairs)]
    all_to_all x0 -> x1, blocking collectives: none -> 15.2 us  [across_view(): lax.all_to_all(value, 'view', split_axis=0, concat_axis=0, tiled=True)]
    all_to_all x2 -> x1, starting transfers between devices: 12.9 us -> 4.71 us  [across_view(): lax.all_to_all(value, 'view', split_axis=0, concat_axis=0, tiled=True)]
    ppermute x4 -> x7, waiting for transfers between devices: 7.34 us -> 1.23 us  [step(): lax.ppermute(colors[r:r + 1], 'view', [(v, v ^ r) for v in range(N_VIEW)])]
    ppermute x18, starting transfers between devices: 26.8 us -> 21.2 us  [shift_by(): return lax.ppermute(value, 'tile', pairs)]
    all_to_all x2, waiting for transfers between devices: 7.97 us -> 13.2 us  [across_tile(): lax.all_to_all(value, 'tile', split_axis=0, concat_axis=0, tiled=True)]
    ppermute x4 -> x7, starting transfers between devices: 6.85 us -> 11.7 us  [step(): lax.ppermute(colors[r:r + 1], 'view', [(v, v ^ r) for v in range(N_VIEW)])]
    pallas_call x2, Pallas kernels: 19.6 us -> 23.9 us  [weights(): pl.pallas_call(weights_kernel, out_shape=(jax.ShapeDtypeStruct((TILES, LB...]
  transfers between devices with their start and end apart: 38 -> 40, of which waited for: 11 -> 14; matrix products, arithmetic and copies ran while one was open for 5% -> 4% of each run, Pallas kernels for 24% -> 21%
where the time goes in v1:
time: 161 us; the launch traced here: 160 us
  starting transfers between devices  62.3 us (39%)
  Pallas kernels  50.7 us (31%)
  waiting for transfers between devices  22.2 us (14%)
  blocking collectives  15.2 us (9%)
  other arithmetic  6.1 us (4%)
  local copies, waits for them, and re-layouts  2.53 us (2%)
    pallas_call x2, Pallas kernels, weights(): pl.pallas_call(weights_kernel, out_shape=(jax.ShapeDtypeStruct((TILES, LB...  23.9 us
    ppermute x18, starting transfers between devices, shift_by(): return lax.ppermute(value, 'tile', pairs)  21.2 us
    all_to_all x2, starting transfers between devices, across_tile(): lax.all_to_all(value, 'tile', split_axis=0, concat_axis=0, tiled=True)  16.2 us
    all_to_all x1, blocking collectives, across_view(): lax.all_to_all(value, 'view', split_axis=0, concat_axis=0, tiled=True)  15.2 us
    pallas_call x1, Pallas kernels, first_render(): pl.pallas_call(first_kernel, out_shape=(jax.ShapeDtypeStruct((32, C, GB),...  14 us
    all_to_all x2, waiting for transfers between devices, across_tile(): lax.all_to_all(value, 'tile', split_axis=0, concat_axis=0, tiled=True)  13.2 us
    ppermute x7, starting transfers between devices, step(): lax.ppermute(colors[r:r + 1], 'view', [(v, v ^ r) for v in range(N_VIEW)])  11.7 us
    ppermute x12, starting transfers between devices, swap_core(): return lax.ppermute(value, 'tile', pairs)  8.54 us
  transfers between devices with their start and end apart: 40, of which 14 were waited for; matrix products, arithmetic and copies ran while one was open for 4% of the time, Pallas kernels for 21%

profile of v1, /device:TPU:1, one launch (start us, length us, event | category | flops | bytes accessed | tf_op | source)
XLA Modules:
  0.0 160.2 jit_solution(4212647495547961565)
XLA Ops:
  0.6 2.0 %prep.1 = (bf16[8,64,128]{2,1,0:T(8,128)(2,1)}, bf16[32,32,128]{2,1,0:T(8,128)(2,1)}, f32[8,8,128]{2,1,0:T(8,128)}) custom-call(f32[1,2,4]{2,1,0:T(2,128)} %camera_hbm.1, s32[8]{0:T(128)} %owner.1, f32[8,64,128]{2,1,0:T(8,128)} %feat.1, f32[3,8,128]{2,1,0:T(8,128)} %bitcast.22, f32[8,128]{1,0:T(8,128)} %scales_hbm.1, f32[8,128]{1,0:T(8,128)} %opacity_hbm.1), custom_call_target="tpu_custom_call" | custom-call | tf_op jit(solution)/shard_map/prep/pallas_call | solution.py:116
  2.6 2.2 %collective-permute-start = (bf16[8,64,128]{2,1,0:T(8,128)(2,1)}, bf16[8,64,128]{2,1,0:T(8,128)(2,1)S(1)}, u32[]{:S(2)}, u32[]{:S(2)}) collective-permute-start(bf16[8,64,128]{2,1,0:T(8,128)(2,1)} %get-tuple-element.41), channel_id=1, source_target_pairs={{0,8},{1,3},{2,10},{3,5},{4,12},{5,7},{6,14},{7,1},{8,16},{9,11},{... | collective-permute-start | bytes 393224 | tf_op jit(solution)/shard_map/ppermute | solution.py:437
  4.8 2.6 %collective-permute-start.1 = (bf16[8,64,128]{2,1,0:T(8,128)(2,1)}, bf16[8,64,128]{2,1,0:T(8,128)(2,1)S(1)}, u32[]{:S(2)}, u32[]{:S(2)}) collective-permute-start(bf16[8,64,128]{2,1,0:T(8,128)(2,1)} %get-tuple-element.41), channel_id=1, source_target_pairs={{0,16},{1,5},{2,18},{3,7},{4,20},{5,1},{6,22},{7,3},{8,24},{9,13},... | collective-permute-start | bytes 393224 | tf_op jit(solution)/shard_map/ppermute | solution.py:437
  7.4 1.1 collective-permute-start.2
  8.5 6.0 %all-to-all-start = ((bf16[32,32,128]{2,1,0:T(8,128)(2,1)}), bf16[32,32,128]{2,1,0:T(8,128)(2,1)S(1)}, u32[]{:S(2)}, u32[]{:S(2)}) async-start(bf16[32,32,128]{2,1,0:T(8,128)(2,1)} %get-tuple-element.42), calls=%async_computation | async-start | bytes 524288 | tf_op jit(solution)/shard_map/all_to_all | solution.py:522
  14.5 0.9 constant_dynamic-update-slice_fusion.3
  15.6 1.5 collective-permute-start.3
  17.0 2.4 %collective-permute-start.4 = (bf16[32,64,128]{2,1,0:T(8,128)(2,1)S(1)}, bf16[32,64,128]{2,1,0:T(8,128)(2,1)S(1)}, u32[]{:S(2)}, u32[]{:S(2)}) collective-permute-start(bf16[32,64,128]{2,1,0:T(8,128)(2,1)S(1)} %constant_dynamic-update-slice_fusion.rest_0_), channel_id=1, source_target_pairs={{0,4},{1,17},{2,6},{3,19},{4,0},{5,21},{6,2},{7,23},{8,12},{9,25},... | collective-permute-start | bytes 1572872 | tf_op jit(solution)/shard_map/ppermute | solution.py:437
  19.5 4.3 %all-to-all-done.screen_hbm = bf16[32,32,128]{2,1,0:T(8,128)(2,1)S(1)} async-done(((bf16[32,32,128]{2,1,0:T(8,128)(2,1)}), bf16[32,32,128]{2,1,0:T(8,128)(2,1)S(1)}, u32[]{:S(2)}, u32[]{:S(2)}) %all-to-all-start) | async-done | bytes 262176 | tf_op jit(solution)/shard_map/all_to_all | solution.py:522
  23.8 0.5 collective-permute-start.5
  24.5 11.9 %weights_first.1 = (bf16[16,8,128,256]{3,2,1,0:T(8,128)(2,1)}, f32[8,128]{1,0:T(8,128)}) custom-call(s32[8,16]{1,0:T(8,128)} %bitcast.23, s32[16]{0:T(128)} %bitcast.27, f32[2,16]{1,0:T(2,128)} %bitcast.31, bf16[32,32,128]{2,1,0:T(8,128)(2,1)} %copy-done.18), custom_call_target="tpu_custom_call" | custom-call | flops 58720256 | bytes 10000000 | tf_op jit(solution)/shard_map/weights_first/pallas_call | solution.py:256
  37.6 0.6 fusion.14.slots
  38.5 1.5 collective-permute-done.7.rest_5_
  40.1 0.8 collective-permute-done.9.rest_7_
  40.9 14.0 %first_render.1 = (f32[32,64,128]{2,1,0:T(8,128)}, f32[32,64,128]{2,1,0:T(8,128)}, f32[32,64,128]{2,1,0:T(8,128)}, f32[32,64,128]{2,1,0:T(8,128)}, f32[32,64,128...) custom-call(s32[16,8]{1,0:T(8,128)} %fusion.14.slots, s32[16]{0:T(128)} %bitcast.28, ...), custom_call_target="tpu_custom_call" | custom-call | flops 1073741824 | bytes 25000000 | tf_op jit(solution)/shard_map/first_render/pallas_call | solution.py:346
  55.0 0.5 collective-permute-start.13
  56.1 1.8 %collective-permute-done.11 = f32[32,64,128]{2,1,0:T(8,128)S(1)} collective-permute-done((f32[32,64,128]{2,1,0:T(8,128)}, f32[32,64,128]{2,1,0:T(8,128)S(1)}, u32[]{:S(2)}, u32[]{:S(2)}) %collective-permute-start.11) | collective-permute-done | bytes 1048608 | tf_op jit(solution)/shard_map/ppermute | solution.py:442
  57.9 1.4 add_convert_fusion.2
  59.6 1.4 add_convert_fusion.1
  61.0 2.4 %collective-permute-start.14 = (f16[32,64,128]{2,1,0:T(8,128)(2,1)S(1)}, f16[32,64,128]{2,1,0:T(8,128)(2,1)S(1)}, u32[]{:S(2)}, u32[]{:S(2)}) collective-permute-start(f16[32,64,128]{2,1,0:T(8,128)(2,1)S(1)} %add_convert_fusion.1), channel_id=1, source_target_pairs={{0,6},{1,25},{2,0},{3,27},{4,2},{5,29},{6,4},{7,31},{8,14},{9,1},{... | collective-permute-start | bytes 1572872 | tf_op jit(solution)/shard_map/ppermute | solution.py:437
  63.4 1.4 add_convert_fusion
  64.9 15.2 %all_to_all.20.geometry = f32[8,8,128]{2,1,0:T(8,128)S(1)} all-to-all(f32[8,8,128]{2,1,0:T(8,128)S(1)} %copy-done.19), channel_id=1, replica_groups=mesh['view'=8,'tile'=32] {'view'}, dimensions={0} | all-to-all | bytes 65536 | tf_op jit(solution)/shard_map/all_to_all | solution.py:518
  80.1 1.4 screen_again.1
  82.7 1.3 collective-permute-start.18
  84.2 10.2 %all-to-all-start.2 = ((bf16[32,32,128]{2,1,0:T(8,128)(2,1)}), bf16[32,32,128]{2,1,0:T(8,128)(2,1)S(1)}, u32[]{:S(2)}, u32[]{:S(2)}) async-start(bf16[32,32,128]{2,1,0:T(8,128)(2,1)} %screen_again.1), calls=%async_computation.2 | async-start | bytes 524288 | tf_op jit(solution)/shard_map/all_to_all | solution.py:522
  94.4 8.9 %all-to-all-done.2.screen_hbm = bf16[32,32,128]{2,1,0:T(8,128)(2,1)S(1)} async-done(((bf16[32,32,128]{2,1,0:T(8,128)(2,1)}), bf16[32,32,128]{2,1,0:T(8,128)(2,1)S(1)}, u32[]{:S(2)}, u32[]{:S(2)}) %all-to-all-start.2) | async-done | bytes 262176 | tf_op jit(solution)/shard_map/all_to_all | solution.py:522
  103.3 1.9 %adam.1 = (bf16[8,64,128]{2,1,0:T(8,128)(2,1)S(1)}, f32[8,192,128]{2,1,0:T(8,128)}) custom-call(s32[8]{0:T(128)S(1)} %copy-done.3, s32[1]{0:T(128)} %bitcast.2.me, f32[8,64,128]{2,1,0:T(8,128)S(1)} %convert_add_fusion.1.gradient, f32[8,64,128]{2,1,0:T(8,128)S(1)} %copy-done, f32[8,64,128]{2,1,0:T(8,128)S(1)} %copy-done.1, f32[8,64,128]{2,1,0:T(8,128)S(1)} %copy-done.2), custom_call_target="tpu_custom_call" | custom-call | tf_op jit(solution)/shard_map/adam/pallas_call | solution.py:413
  105.9 3.0 %collective-permute-start.22 = (bf16[1,64,128]{2,1,0:T(8,128)(2,1)S(1)}, bf16[1,64,128]{2,1,0:T(8,128)(2,1)S(1)}, u32[]{:S(2)}, u32[]{:S(2)}) collective-permute-start(bf16[1,64,128]{2,1,0:T(8,128)(2,1)S(1)} %get-tuple-element.88), channel_id=1, source_target_pairs={{0,96},{32,64},{64,32},{96,0},{128,224},{160,192},{192,160},{224,1... | collective-permute-start | bytes 49160 | tf_op jit(solution)/shard_map/ppermute | solution.py:507
  109.1 3.3 %collective-permute-start.24 = (bf16[1,64,128]{2,1,0:T(8,128)(2,1)S(1)}, bf16[1,64,128]{2,1,0:T(8,128)(2,1)S(1)}, u32[]{:S(2)}, u32[]{:S(2)}) collective-permute-start(bf16[1,64,128]{2,1,0:T(8,128)(2,1)S(1)} %get-tuple-element.86), channel_id=1, source_target_pairs={{0,160},{32,128},{64,224},{96,192},{128,32},{160,0},{192,96},{224,... | collective-permute-start | bytes 49160 | tf_op jit(solution)/shard_map/ppermute | solution.py:507
  112.5 1.9 %collective-permute-start.25 = (bf16[1,64,128]{2,1,0:T(8,128)(2,1)S(1)}, bf16[1,64,128]{2,1,0:T(8,128)(2,1)S(1)}, u32[]{:S(2)}, u32[]{:S(2)}) collective-permute-start(bf16[1,64,128]{2,1,0:T(8,128)(2,1)S(1)} %get-tuple-element.85), channel_id=1, source_target_pairs={{0,192},{32,224},{64,128},{96,160},{128,64},{160,96},{192,0},{224,... | collective-permute-start | bytes 49160 | tf_op jit(solution)/shard_map/ppermute | solution.py:507
  114.4 2.6 %collective-permute-start.26 = (bf16[1,64,128]{2,1,0:T(8,128)(2,1)S(1)}, bf16[1,64,128]{2,1,0:T(8,128)(2,1)S(1)}, u32[]{:S(2)}, u32[]{:S(2)}) collective-permute-start(bf16[1,64,128]{2,1,0:T(8,128)(2,1)S(1)} %get-tuple-element.84), channel_id=1, source_target_pairs={{0,224},{32,192},{64,160},{96,128},{128,96},{160,64},{192,32},{224... | collective-permute-start | bytes 49160 | tf_op jit(solution)/shard_map/ppermute | solution.py:507
  117.2 1.0 collective-permute-done.26
  118.5 1.9 %collective-permute-start.28 = (bf16[8,64,128]{2,1,0:T(8,128)(2,1)S(1)}, bf16[8,64,128]{2,1,0:T(8,128)(2,1)S(1)}, u32[]{:S(2)}, u32[]{:S(2)}) collective-permute-start(bf16[8,64,128]{2,1,0:T(8,128)(2,1)S(1)} %constant_dynamic-update-slice_fusion.4), channel_id=1, source_target_pairs={{0,16},{1,5},{2,18},{3,7},{4,20},{5,1},{6,22},{7,3},{8,24},{9,13},... | collective-permute-start | bytes 393224 | tf_op jit(solution)/shard_map/ppermute | solution.py:437
  120.4 0.6 collective-permute-start.29
  121.0 4.7 %all-to-all-start.3 = ((f32[8,192,128]{2,1,0:T(8,128)}), f32[8,192,128]{2,1,0:T(8,128)S(1)}, u32[]{:S(2)}, u32[]{:S(2)}) async-start(f32[8,192,128]{2,1,0:T(8,128)} %get-tuple-element.77), calls=%async_computation.3 | async-start | bytes 1572864 | tf_op jit(solution)/shard_map/all_to_all | solution.py:518
  125.9 0.7 collective-permute-start.30
  126.6 1.7 %collective-permute-start.31 = (bf16[32,64,128]{2,1,0:T(8,128)(2,1)S(1)}, bf16[32,64,128]{2,1,0:T(8,128)(2,1)S(1)}, u32[]{:S(2)}, u32[]{:S(2)}) collective-permute-start(bf16[32,64,128]{2,1,0:T(8,128)(2,1)S(1)} %constant_dynamic-update-slice_fusion.12.rest_0_), channel_id=1, source_target_pairs={{0,4},{1,17},{2,6},{3,19},{4,0},{5,21},{6,2},{7,23},{8,12},{9,25},... | collective-permute-start | bytes 1572872 | tf_op jit(solution)/shard_map/ppermute | solution.py:437
  128.3 1.1 collective-permute-start.32
  129.3 12.0 %weights_second.1 = (bf16[16,8,128,256]{3,2,1,0:T(8,128)(2,1)}, f32[8,128]{1,0:T(8,128)}) custom-call(s32[8,16]{1,0:T(8,128)} %bitcast.25, s32[16]{0:T(128)} %bitcast.29, f32[2,16]{1,0:T(2,128)} %bitcast.32, bf16[32,32,128]{2,1,0:T(8,128)(2,1)} %copy-done.17), custom_call_target="tpu_custom_call" | custom-call | flops 58720256 | bytes 10000000 | tf_op jit(solution)/shard_map/weights_second/pallas_call | solution.py:256
  141.4 0.6 collective-permute-done.32.rest_3_
  141.9 5.8 %collective-permute-start.33 = (bf16[32,64,128]{2,1,0:T(8,128)(2,1)S(1)}, bf16[32,64,128]{2,1,0:T(8,128)(2,1)S(1)}, u32[]{:S(2)}, u32[]{:S(2)}) collective-permute-start(bf16[32,64,128]{2,1,0:T(8,128)(2,1)S(1)} %constant_dynamic-update-slice_fusion.12.rest_0_), channel_id=1, source_target_pairs={{0,1},{1,0},{2,3},{3,2},{4,5},{5,4},{6,7},{7,6},{8,9},{9,8},{10,11... | collective-permute-start | bytes 1572872 | tf_op jit(solution)/shard_map/ppermute | solution.py:442
  147.8 0.5 collective-permute-start.35
  148.4 0.6 fusion.7.slots
  149.0 1.0 collective-permute-done.33.rest_4_
  150.2 0.7 collective-permute-done.35.rest_6_
  150.9 0.7 collective-permute-done.36.rest_7_
  151.7 7.6 %second_render.1 = f32[16,64,256]{2,1,0:T(8,128)} custom-call(s32[16,8]{1,0:T(8,128)} %fusion.7.slots, s32[16]{0:T(128)} %bitcast.30, f32[8,128]{1,0:T(8,128)} %get-tuple-element.71.token, bf16[16,8,128,256]{3,2,1,0:T(8,128)(2,1)} %get-tuple-element.72.w_hbm, bf16[32,64,128]{2,1,0:T(8,128)(2,1)} %copy-done.6, bf16[32,64,128]{2,1,0:T(8,128)(2,1)} %copy-done.13, ...), custom_call_target="tpu_custom_call" | custom-call | flops 536870912 | bytes 14000000 | tf_op jit(solution)/shard_map/second_render/pallas_call | solution.py:380
  159.3 0.9 fusion.21
  (112 shorter events, 5.8 us)
Async XLA Ops:
  0.6 36.9 %copy-start.20 = (s32[1,16,8]{1,2,0:T(8,128)S(1)}, s32[1,16,8]{1,2,0:T(8,128)}, u32[]{:S(2)}) copy-start(s32[1,16,8]{1,2,0:T(8,128)} %param.24) | copy-start | bytes 1540
  2.6 12.8 %collective-permute-start = (bf16[8,64,128]{2,1,0:T(8,128)(2,1)}, bf16[8,64,128]{2,1,0:T(8,128)(2,1)S(1)}, u32[]{:S(2)}, u32[]{:S(2)}) collective-permute-start(bf16[8,64,128]{2,1,0:T(8,128)(2,1)} %get-tuple-element.41), channel_id=1, source_target_pairs={{0,8},{1,3},{2,10},{3,5},{4,12},{5,7},{6,14},{7,1},{8,16},{9,11},{... | collective-permute-start | bytes 393224 | tf_op jit(solution)/shard_map/ppermute | solution.py:437
  4.8 10.7 %collective-permute-start.1 = (bf16[8,64,128]{2,1,0:T(8,128)(2,1)}, bf16[8,64,128]{2,1,0:T(8,128)(2,1)S(1)}, u32[]{:S(2)}, u32[]{:S(2)}) collective-permute-start(bf16[8,64,128]{2,1,0:T(8,128)(2,1)} %get-tuple-element.41), channel_id=1, source_target_pairs={{0,16},{1,5},{2,18},{3,7},{4,20},{5,1},{6,22},{7,3},{8,24},{9,13},... | collective-permute-start | bytes 393224 | tf_op jit(solution)/shard_map/ppermute | solution.py:437
  7.4 8.1 %collective-permute-start.2 = (bf16[8,64,128]{2,1,0:T(8,128)(2,1)}, bf16[8,64,128]{2,1,0:T(8,128)(2,1)S(1)}, u32[]{:S(2)}, u32[]{:S(2)}) collective-permute-start(bf16[8,64,128]{2,1,0:T(8,128)(2,1)} %get-tuple-element.41), channel_id=1, source_target_pairs={{0,24},{1,7},{2,26},{3,1},{4,28},{5,3},{6,30},{7,5},{8,0},{9,15},{... | collective-permute-start | bytes 393224 | tf_op jit(solution)/shard_map/ppermute | solution.py:437
  8.5 15.3 %all-to-all-start = ((bf16[32,32,128]{2,1,0:T(8,128)(2,1)}), bf16[32,32,128]{2,1,0:T(8,128)(2,1)S(1)}, u32[]{:S(2)}, u32[]{:S(2)}) async-start(bf16[32,32,128]{2,1,0:T(8,128)(2,1)} %get-tuple-element.42), calls=%async_computation | async-start | bytes 524288 | tf_op jit(solution)/shard_map/all_to_all | solution.py:522
  15.6 20.9 %collective-permute-start.3 = (bf16[32,64,128]{2,1,0:T(8,128)(2,1)S(1)}, bf16[32,64,128]{2,1,0:T(8,128)(2,1)S(1)}, u32[]{:S(2)}, u32[]{:S(2)}) collective-permute-start(bf16[32,64,128]{2,1,0:T(8,128)(2,1)S(1)} %constant_dynamic-update-slice_fusion.rest_0_), channel_id=1, source_target_pairs={{0,2},{1,9},{2,4},{3,11},{4,6},{5,13},{6,0},{7,15},{8,10},{9,17},{... | collective-permute-start | bytes 1572872 | tf_op jit(solution)/shard_map/ppermute | solution.py:437
  17.0 19.4 %collective-permute-start.4 = (bf16[32,64,128]{2,1,0:T(8,128)(2,1)S(1)}, bf16[32,64,128]{2,1,0:T(8,128)(2,1)S(1)}, u32[]{:S(2)}, u32[]{:S(2)}) collective-permute-start(bf16[32,64,128]{2,1,0:T(8,128)(2,1)S(1)} %constant_dynamic-update-slice_fusion.rest_0_), channel_id=1, source_target_pairs={{0,4},{1,17},{2,6},{3,19},{4,0},{5,21},{6,2},{7,23},{8,12},{9,25},... | collective-permute-start | bytes 1572872 | tf_op jit(solution)/shard_map/ppermute | solution.py:437
  23.8 12.6 %collective-permute-start.5 = (bf16[32,64,128]{2,1,0:T(8,128)(2,1)S(1)}, bf16[32,64,128]{2,1,0:T(8,128)(2,1)S(1)}, u32[]{:S(2)}, u32[]{:S(2)}) collective-permute-start(bf16[32,64,128]{2,1,0:T(8,128)(2,1)S(1)} %constant_dynamic-update-slice_fusion.rest_0_), channel_id=1, source_target_pairs={{0,6},{1,25},{2,0},{3,27},{4,2},{5,29},{6,4},{7,31},{8,14},{9,1},{... | collective-permute-start | bytes 1572872 | tf_op jit(solution)/shard_map/ppermute | solution.py:437
  36.5 2.0 %collective-permute-start.6 = (bf16[32,64,128]{2,1,0:T(8,128)(2,1)S(1)}, bf16[32,64,128]{2,1,0:T(8,128)(2,1)S(1)}, u32[]{:S(2)}, u32[]{:S(2)}) collective-permute-start(bf16[32,64,128]{2,1,0:T(8,128)(2,1)S(1)} %constant_dynamic-update-slice_fusion.rest_0_), channel_id=1, source_target_pairs={{0,1},{1,0},{2,3},{3,2},{4,5},{5,4},{6,7},{7,6},{8,9},{9,8},{10,11... | collective-permute-start | bytes 1572872 | tf_op jit(solution)/shard_map/ppermute | solution.py:442
  36.6 3.4 %collective-permute-start.7 = (bf16[32,64,128]{2,1,0:T(8,128)(2,1)S(1)}, bf16[32,64,128]{2,1,0:T(8,128)(2,1)S(1)}, u32[]{:S(2)}, u32[]{:S(2)}) collective-permute-start(bf16[32,64,128]{2,1,0:T(8,128)(2,1)S(1)} %collective-permute-done.3.rest_1_), channel_id=1, source_target_pairs={{0,1},{1,0},{2,3},{3,2},{4,5},{5,4},{6,7},{7,6},{8,9},{9,8},{10,11... | collective-permute-start | bytes 1572872 | tf_op jit(solution)/shard_map/ppermute | solution.py:442
  37.1 3.0 %collective-permute-start.8 = (bf16[32,64,128]{2,1,0:T(8,128)(2,1)S(1)}, bf16[32,64,128]{2,1,0:T(8,128)(2,1)}, u32[]{:S(2)}, u32[]{:S(2)}) collective-permute-start(bf16[32,64,128]{2,1,0:T(8,128)(2,1)S(1)} %collective-permute-done.4.rest_2_), channel_id=1, source_target_pairs={{0,1},{1,0},{2,3},{3,2},{4,5},{5,4},{6,7},{7,6},{8,9},{9,8},{10,11... | collective-permute-start | bytes 1572872 | tf_op jit(solution)/shard_map/ppermute | solution.py:442
  37.2 3.7 %collective-permute-start.9 = (bf16[32,64,128]{2,1,0:T(8,128)(2,1)S(1)}, bf16[32,64,128]{2,1,0:T(8,128)(2,1)}, u32[]{:S(2)}, u32[]{:S(2)}) collective-permute-start(bf16[32,64,128]{2,1,0:T(8,128)(2,1)S(1)} %collective-permute-done.5.rest_3_), channel_id=1, source_target_pairs={{0,1},{1,0},{2,3},{3,2},{4,5},{5,4},{6,7},{7,6},{8,9},{9,8},{10,11... | collective-permute-start | bytes 1572872 | tf_op jit(solution)/shard_map/ppermute | solution.py:442
  40.9 39.2 %copy-start.4 = (f32[1,2,4]{2,1,0:T(2,128)S(1)}, f32[1,2,4]{2,1,0:T(2,128)}, u32[]{:S(2)}) copy-start(f32[1,2,4]{2,1,0:T(2,128)} %param.28) | copy-start | bytes 100
  54.9 26.7 %copy-start.5 = (f32[32,64,128]{2,1,0:T(8,128)S(1)}, f32[32,64,128]{2,1,0:T(8,128)}, u32[]{:S(2)}) copy-start(f32[32,64,128]{2,1,0:T(8,128)} %get-tuple-element.52) | copy-start | bytes 3145732
  54.9 48.4 %copy-start = (f32[8,64,128]{2,1,0:T(8,128)S(1)}, f32[8,64,128]{2,1,0:T(8,128)}, u32[]{:S(2)}) copy-start(f32[8,64,128]{2,1,0:T(8,128)} %feat.1) | copy-start | bytes 786436
  54.9 48.4 %copy-start.1 = (f32[8,64,128]{2,1,0:T(8,128)S(1)}, f32[8,64,128]{2,1,0:T(8,128)}, u32[]{:S(2)}) copy-start(f32[8,64,128]{2,1,0:T(8,128)} %m1.1) | copy-start | bytes 786436
  54.9 48.4 %copy-start.2 = (f32[8,64,128]{2,1,0:T(8,128)S(1)}, f32[8,64,128]{2,1,0:T(8,128)}, u32[]{:S(2)}) copy-start(f32[8,64,128]{2,1,0:T(8,128)} %m2.1) | copy-start | bytes 786436
  54.9 48.4 %copy-start.3 = (s32[8]{0:T(128)S(1)}, s32[8]{0:T(128)}, u32[]{:S(2)}) copy-start(s32[8]{0:T(128)} %owner.1) | copy-start | bytes 100
  55.0 3.0 %collective-permute-start.11 = (f32[32,64,128]{2,1,0:T(8,128)}, f32[32,64,128]{2,1,0:T(8,128)S(1)}, u32[]{:S(2)}, u32[]{:S(2)}) collective-permute-start(f32[32,64,128]{2,1,0:T(8,128)} %get-tuple-element.55), channel_id=1, source_target_pairs={{0,1},{1,0},{2,3},{3,2},{4,5},{5,4},{6,7},{7,6},{8,9},{9,8},{10,11... | collective-permute-start | bytes 3145736 | tf_op jit(solution)/shard_map/ppermute | solution.py:442
  55.0 4.6 %collective-permute-start.13 = (f32[32,64,128]{2,1,0:T(8,128)}, f32[32,64,128]{2,1,0:T(8,128)S(1)}, u32[]{:S(2)}, u32[]{:S(2)}) collective-permute-start(f32[32,64,128]{2,1,0:T(8,128)} %get-tuple-element.57), channel_id=1, source_target_pairs={{0,1},{1,0},{2,3},{3,2},{4,5},{5,4},{6,7},{7,6},{8,9},{9,8},{10,11... | collective-permute-start | bytes 3145736 | tf_op jit(solution)/shard_map/ppermute | solution.py:442
  55.5 7.8 %collective-permute-start.15 = (f32[32,64,128]{2,1,0:T(8,128)}, f32[32,64,128]{2,1,0:T(8,128)S(1)}, u32[]{:S(2)}, u32[]{:S(2)}) collective-permute-start(f32[32,64,128]{2,1,0:T(8,128)} %get-tuple-element.59), channel_id=1, source_target_pairs={{0,1},{1,0},{2,3},{3,2},{4,5},{5,4},{6,7},{7,6},{8,9},{9,8},{10,11... | collective-permute-start | bytes 3145736 | tf_op jit(solution)/shard_map/ppermute | solution.py:442
  55.6 25.9 %collective-permute-start.10 = (f32[32,64,128]{2,1,0:T(8,128)}, f32[32,64,128]{2,1,0:T(8,128)S(1)}, u32[]{:S(2)}, u32[]{:S(2)}) collective-permute-start(f32[32,64,128]{2,1,0:T(8,128)} %get-tuple-element.53), channel_id=1, source_target_pairs={{0,1},{1,0},{2,3},{3,2},{4,5},{5,4},{6,7},{7,6},{8,9},{9,8},{10,11... | collective-permute-start | bytes 3145736 | tf_op jit(solution)/shard_map/ppermute | solution.py:442
  59.3 22.2 %collective-permute-start.12 = (f16[32,64,128]{2,1,0:T(8,128)(2,1)S(1)}, f16[32,64,128]{2,1,0:T(8,128)(2,1)S(1)}, u32[]{:S(2)}, u32[]{:S(2)}) collective-permute-start(f16[32,64,128]{2,1,0:T(8,128)(2,1)S(1)} %add_convert_fusion.2), channel_id=1, source_target_pairs={{0,4},{1,17},{2,6},{3,19},{4,0},{5,21},{6,2},{7,23},{8,12},{9,25},... | collective-permute-start | bytes 1572872 | tf_op jit(solution)/shard_map/ppermute | solution.py:437
  61.0 20.5 %collective-permute-start.14 = (f16[32,64,128]{2,1,0:T(8,128)(2,1)S(1)}, f16[32,64,128]{2,1,0:T(8,128)(2,1)S(1)}, u32[]{:S(2)}, u32[]{:S(2)}) collective-permute-start(f16[32,64,128]{2,1,0:T(8,128)(2,1)S(1)} %add_convert_fusion.1), channel_id=1, source_target_pairs={{0,6},{1,25},{2,0},{3,27},{4,2},{5,29},{6,4},{7,31},{8,14},{9,1},{... | collective-permute-start | bytes 1572872 | tf_op jit(solution)/shard_map/ppermute | solution.py:437
  64.8 16.8 %collective-permute-start.16 = (f16[32,64,128]{2,1,0:T(8,128)(2,1)S(1)}, f16[32,64,128]{2,1,0:T(8,128)(2,1)S(1)}, u32[]{:S(2)}, u32[]{:S(2)}) collective-permute-start(f16[32,64,128]{2,1,0:T(8,128)(2,1)S(1)} %add_convert_fusion), channel_id=1, source_target_pairs={{0,2},{1,9},{2,4},{3,11},{4,6},{5,13},{6,0},{7,15},{8,10},{9,17},{... | collective-permute-start | bytes 1572872 | tf_op jit(solution)/shard_map/ppermute | solution.py:437
  82.0 66.2 %copy-start.21 = (s32[1,16,8]{1,2,0:T(8,128)S(1)}, s32[1,16,8]{1,2,0:T(8,128)}, u32[]{:S(2)}) copy-start(s32[1,16,8]{1,2,0:T(8,128)} %param.30) | copy-start | bytes 1540
  82.2 12.1 %collective-permute-start.17 = (f16[8,64,128]{2,1,0:T(8,128)(2,1)S(1)}, f16[8,64,128]{2,1,0:T(8,128)(2,1)S(1)}, u32[]{:S(2)}, u32[]{:S(2)}) collective-permute-start(f16[8,64,128]{2,1,0:T(8,128)(2,1)S(1)} %get-tuple-element.81), channel_id=1, source_target_pairs={{0,16},{1,5},{2,18},{3,7},{4,20},{5,1},{6,22},{7,3},{8,24},{9,13},... | collective-permute-start | bytes 393224 | tf_op jit(solution)/shard_map/ppermute | solution.py:437
  82.7 11.7 %collective-permute-start.18 = (f16[8,64,128]{2,1,0:T(8,128)(2,1)S(1)}, f16[8,64,128]{2,1,0:T(8,128)(2,1)S(1)}, u32[]{:S(2)}, u32[]{:S(2)}) collective-permute-start(f16[8,64,128]{2,1,0:T(8,128)(2,1)S(1)} %get-tuple-element.83), channel_id=1, source_target_pairs={{0,24},{1,7},{2,26},{3,1},{4,28},{5,3},{6,30},{7,5},{8,0},{9,15},{... | collective-permute-start | bytes 393224 | tf_op jit(solution)/shard_map/ppermute | solution.py:437
  84.0 10.4 %collective-permute-start.19 = (f16[8,64,128]{2,1,0:T(8,128)(2,1)S(1)}, f16[8,64,128]{2,1,0:T(8,128)(2,1)S(1)}, u32[]{:S(2)}, u32[]{:S(2)}) collective-permute-start(f16[8,64,128]{2,1,0:T(8,128)(2,1)S(1)} %get-tuple-element.82), channel_id=1, source_target_pairs={{0,8},{1,3},{2,10},{3,5},{4,12},{5,7},{6,14},{7,1},{8,16},{9,11},{... | collective-permute-start | bytes 393224 | tf_op jit(solution)/shard_map/ppermute | solution.py:437
  84.2 19.2 %all-to-all-start.2 = ((bf16[32,32,128]{2,1,0:T(8,128)(2,1)}), bf16[32,32,128]{2,1,0:T(8,128)(2,1)S(1)}, u32[]{:S(2)}, u32[]{:S(2)}) async-start(bf16[32,32,128]{2,1,0:T(8,128)(2,1)} %screen_again.1), calls=%async_computation.2 | async-start | bytes 524288 | tf_op jit(solution)/shard_map/all_to_all | solution.py:522
  105.3 7.2 %collective-permute-start.20 = (bf16[1,64,128]{2,1,0:T(8,128)(2,1)S(1)}, bf16[1,64,128]{2,1,0:T(8,128)(2,1)S(1)}, u32[]{:S(2)}, u32[]{:S(2)}) collective-permute-start(bf16[1,64,128]{2,1,0:T(8,128)(2,1)S(1)} %get-tuple-element.90), channel_id=1, source_target_pairs={{0,32},{32,0},{64,96},{96,64},{128,160},{160,128},{192,224},{224,1... | collective-permute-start | bytes 49160 | tf_op jit(solution)/shard_map/ppermute | solution.py:507
  105.6 8.8 %collective-permute-start.21 = (bf16[1,64,128]{2,1,0:T(8,128)(2,1)S(1)}, bf16[1,64,128]{2,1,0:T(8,128)(2,1)S(1)}, u32[]{:S(2)}, u32[]{:S(2)}) collective-permute-start(bf16[1,64,128]{2,1,0:T(8,128)(2,1)S(1)} %get-tuple-element.89), channel_id=1, source_target_pairs={{0,64},{32,96},{64,0},{96,32},{128,192},{160,224},{192,128},{224,1... | collective-permute-start | bytes 49160 | tf_op jit(solution)/shard_map/ppermute | solution.py:507
  105.9 11.1 %collective-permute-start.22 = (bf16[1,64,128]{2,1,0:T(8,128)(2,1)S(1)}, bf16[1,64,128]{2,1,0:T(8,128)(2,1)S(1)}, u32[]{:S(2)}, u32[]{:S(2)}) collective-permute-start(bf16[1,64,128]{2,1,0:T(8,128)(2,1)S(1)} %get-tuple-element.88), channel_id=1, source_target_pairs={{0,96},{32,64},{64,32},{96,0},{128,224},{160,192},{192,160},{224,1... | collective-permute-start | bytes 49160 | tf_op jit(solution)/shard_map/ppermute | solution.py:507
  108.9 8.1 %collective-permute-start.23 = (bf16[1,64,128]{2,1,0:T(8,128)(2,1)S(1)}, bf16[1,64,128]{2,1,0:T(8,128)(2,1)S(1)}, u32[]{:S(2)}, u32[]{:S(2)}) collective-permute-start(bf16[1,64,128]{2,1,0:T(8,128)(2,1)S(1)} %get-tuple-element.87), channel_id=1, source_target_pairs={{0,128},{32,160},{64,192},{96,224},{128,0},{160,32},{192,64},{224,... | collective-permute-start | bytes 49160 | tf_op jit(solution)/shard_map/ppermute | solution.py:507
  109.1 7.9 %collective-permute-start.24 = (bf16[1,64,128]{2,1,0:T(8,128)(2,1)S(1)}, bf16[1,64,128]{2,1,0:T(8,128)(2,1)S(1)}, u32[]{:S(2)}, u32[]{:S(2)}) collective-permute-start(bf16[1,64,128]{2,1,0:T(8,128)(2,1)S(1)} %get-tuple-element.86), channel_id=1, source_target_pairs={{0,160},{32,128},{64,224},{96,192},{128,32},{160,0},{192,96},{224,... | collective-permute-start | bytes 49160 | tf_op jit(solution)/shard_map/ppermute | solution.py:507
  112.5 4.8 %collective-permute-start.25 = (bf16[1,64,128]{2,1,0:T(8,128)(2,1)S(1)}, bf16[1,64,128]{2,1,0:T(8,128)(2,1)S(1)}, u32[]{:S(2)}, u32[]{:S(2)}) collective-permute-start(bf16[1,64,128]{2,1,0:T(8,128)(2,1)S(1)} %get-tuple-element.85), channel_id=1, source_target_pairs={{0,192},{32,224},{64,128},{96,160},{128,64},{160,96},{192,0},{224,... | collective-permute-start | bytes 49160 | tf_op jit(solution)/shard_map/ppermute | solution.py:507
  114.4 3.9 %collective-permute-start.26 = (bf16[1,64,128]{2,1,0:T(8,128)(2,1)S(1)}, bf16[1,64,128]{2,1,0:T(8,128)(2,1)S(1)}, u32[]{:S(2)}, u32[]{:S(2)}) collective-permute-start(bf16[1,64,128]{2,1,0:T(8,128)(2,1)S(1)} %get-tuple-element.84), channel_id=1, source_target_pairs={{0,224},{32,192},{64,160},{96,128},{128,96},{160,64},{192,32},{224... | collective-permute-start | bytes 49160 | tf_op jit(solution)/shard_map/ppermute | solution.py:507
  118.3 7.5 %collective-permute-start.27 = (bf16[8,64,128]{2,1,0:T(8,128)(2,1)S(1)}, bf16[8,64,128]{2,1,0:T(8,128)(2,1)S(1)}, u32[]{:S(2)}, u32[]{:S(2)}) collective-permute-start(bf16[8,64,128]{2,1,0:T(8,128)(2,1)S(1)} %constant_dynamic-update-slice_fusion.4), channel_id=1, source_target_pairs={{0,8},{1,3},{2,10},{3,5},{4,12},{5,7},{6,14},{7,1},{8,16},{9,11},{... | collective-permute-start | bytes 393224 | tf_op jit(solution)/shard_map/ppermute | solution.py:437
  118.5 7.3 %collective-permute-start.28 = (bf16[8,64,128]{2,1,0:T(8,128)(2,1)S(1)}, bf16[8,64,128]{2,1,0:T(8,128)(2,1)S(1)}, u32[]{:S(2)}, u32[]{:S(2)}) collective-permute-start(bf16[8,64,128]{2,1,0:T(8,128)(2,1)S(1)} %constant_dynamic-update-slice_fusion.4), channel_id=1, source_target_pairs={{0,16},{1,5},{2,18},{3,7},{4,20},{5,1},{6,22},{7,3},{8,24},{9,13},... | collective-permute-start | bytes 393224 | tf_op jit(solution)/shard_map/ppermute | solution.py:437
  120.4 5.4 %collective-permute-start.29 = (bf16[8,64,128]{2,1,0:T(8,128)(2,1)S(1)}, bf16[8,64,128]{2,1,0:T(8,128)(2,1)S(1)}, u32[]{:S(2)}, u32[]{:S(2)}) collective-permute-start(bf16[8,64,128]{2,1,0:T(8,128)(2,1)S(1)} %constant_dynamic-update-slice_fusion.4), channel_id=1, source_target_pairs={{0,24},{1,7},{2,26},{3,1},{4,28},{5,3},{6,30},{7,5},{8,0},{9,15},{... | collective-permute-start | bytes 393224 | tf_op jit(solution)/shard_map/ppermute | solution.py:437
  121.0 38.3 %all-to-all-start.3 = ((f32[8,192,128]{2,1,0:T(8,128)}), f32[8,192,128]{2,1,0:T(8,128)S(1)}, u32[]{:S(2)}, u32[]{:S(2)}) async-start(f32[8,192,128]{2,1,0:T(8,128)} %get-tuple-element.77), calls=%async_computation.3 | async-start | bytes 1572864 | tf_op jit(solution)/shard_map/all_to_all | solution.py:518
  125.9 15.5 %collective-permute-start.30 = (bf16[32,64,128]{2,1,0:T(8,128)(2,1)S(1)}, bf16[32,64,128]{2,1,0:T(8,128)(2,1)S(1)}, u32[]{:S(2)}, u32[]{:S(2)}) collective-permute-start(bf16[32,64,128]{2,1,0:T(8,128)(2,1)S(1)} %constant_dynamic-update-slice_fusion.12.rest_0_), channel_id=1, source_target_pairs={{0,2},{1,9},{2,4},{3,11},{4,6},{5,13},{6,0},{7,15},{8,10},{9,17},{... | collective-permute-start | bytes 1572872 | tf_op jit(solution)/shard_map/ppermute | solution.py:437
  126.6 14.8 %collective-permute-start.31 = (bf16[32,64,128]{2,1,0:T(8,128)(2,1)S(1)}, bf16[32,64,128]{2,1,0:T(8,128)(2,1)S(1)}, u32[]{:S(2)}, u32[]{:S(2)}) collective-permute-start(bf16[32,64,128]{2,1,0:T(8,128)(2,1)S(1)} %constant_dynamic-update-slice_fusion.12.rest_0_), channel_id=1, source_target_pairs={{0,4},{1,17},{2,6},{3,19},{4,0},{5,21},{6,2},{7,23},{8,12},{9,25},... | collective-permute-start | bytes 1572872 | tf_op jit(solution)/shard_map/ppermute | solution.py:437
  128.3 13.6 %collective-permute-start.32 = (bf16[32,64,128]{2,1,0:T(8,128)(2,1)S(1)}, bf16[32,64,128]{2,1,0:T(8,128)(2,1)S(1)}, u32[]{:S(2)}, u32[]{:S(2)}) collective-permute-start(bf16[32,64,128]{2,1,0:T(8,128)(2,1)S(1)} %constant_dynamic-update-slice_fusion.12.rest_0_), channel_id=1, source_target_pairs={{0,6},{1,25},{2,0},{3,27},{4,2},{5,29},{6,4},{7,31},{8,14},{9,1},{... | collective-permute-start | bytes 1572872 | tf_op jit(solution)/shard_map/ppermute | solution.py:437
  141.9 8.1 %collective-permute-start.33 = (bf16[32,64,128]{2,1,0:T(8,128)(2,1)S(1)}, bf16[32,64,128]{2,1,0:T(8,128)(2,1)S(1)}, u32[]{:S(2)}, u32[]{:S(2)}) collective-permute-start(bf16[32,64,128]{2,1,0:T(8,128)(2,1)S(1)} %constant_dynamic-update-slice_fusion.12.rest_0_), channel_id=1, source_target_pairs={{0,1},{1,0},{2,3},{3,2},{4,5},{5,4},{6,7},{7,6},{8,9},{9,8},{10,11... | collective-permute-start | bytes 1572872 | tf_op jit(solution)/shard_map/ppermute | solution.py:442
  147.8 2.4 %collective-permute-start.34 = (bf16[32,64,128]{2,1,0:T(8,128)(2,1)S(1)}, bf16[32,64,128]{2,1,0:T(8,128)(2,1)}, u32[]{:S(2)}, u32[]{:S(2)}) collective-permute-start(bf16[32,64,128]{2,1,0:T(8,128)(2,1)S(1)} %collective-permute-done.30.rest_1_), channel_id=1, source_target_pairs={{0,1},{1,0},{2,3},{3,2},{4,5},{5,4},{6,7},{7,6},{8,9},{9,8},{10,11... | collective-permute-start | bytes 1572872 | tf_op jit(solution)/shard_map/ppermute | solution.py:442
  147.8 3.2 %collective-permute-start.35 = (bf16[32,64,128]{2,1,0:T(8,128)(2,1)S(1)}, bf16[32,64,128]{2,1,0:T(8,128)(2,1)}, u32[]{:S(2)}, u32[]{:S(2)}) collective-permute-start(bf16[32,64,128]{2,1,0:T(8,128)(2,1)S(1)} %collective-permute-done.31.rest_2_), channel_id=1, source_target_pairs={{0,1},{1,0},{2,3},{3,2},{4,5},{5,4},{6,7},{7,6},{8,9},{9,8},{10,11... | collective-permute-start | bytes 1572872 | tf_op jit(solution)/shard_map/ppermute | solution.py:442
  148.3 3.4 %collective-permute-start.36 = (bf16[32,64,128]{2,1,0:T(8,128)(2,1)S(1)}, bf16[32,64,128]{2,1,0:T(8,128)(2,1)}, u32[]{:S(2)}, u32[]{:S(2)}) collective-permute-start(bf16[32,64,128]{2,1,0:T(8,128)(2,1)S(1)} %collective-permute-done.32.rest_3_), channel_id=1, source_target_pairs={{0,1},{1,0},{2,3},{3,2},{4,5},{5,4},{6,7},{7,6},{8,9},{9,8},{10,11... | collective-permute-start | bytes 1572872 | tf_op jit(solution)/shard_map/ppermute | solution.py:442
  (14 other events, 150.6 us)

commit v2 on v1

--- a/solution.py
+++ b/solution.py
@@ -30,7 +30,8 @@
 ANY = pl.BlockSpec(memory_space=pl.ANY)
 GROUP = 8
 WEIGHTS_MIB = 60
-RENDER_MIB = 60
+RENDER_MIB = 34
+SECOND_MIB = 48
 LOG2E = 1.4426950408889634
 f32 = jnp.float32
 bf16 = jnp.bfloat16
@@ -155,7 +156,7 @@
 def weights_kernel(lists_hbm, loads_hbm, shift_hbm, screen_hbm, out_hbm, token, *scratch):
     lists, loads, shift, screen, bins, out, work, sem, sems = scratch
     copies = fetch([(lists_hbm, lists), (loads_hbm, loads), (shift_hbm, shift), (screen_hbm, screen)], sems)
-    token[...] = jnp.zeros((8, GB), f32)
+    token[...] = jnp.zeros((8, GB), jnp.int32)
     row = lax.broadcasted_iota(jnp.int32, (8, GB), 0)
     lane = lax.broadcasted_iota(jnp.int32, (8, GB), 1)
     pixel_x = (lane % SIDE).astype(f32) + 0.5
@@ -255,7 +256,7 @@
 def weights(lists, loads, shift, screen, name):
     return pl.pallas_call(
         weights_kernel,
-        out_shape=(jax.ShapeDtypeStruct((TILES, LBLK, GB, PIX), bf16), jax.ShapeDtypeStruct((8, GB), f32)),
+        out_shape=(jax.ShapeDtypeStruct((TILES, LBLK, GB, PIX), bf16), jax.ShapeDtypeStruct((8, GB), jnp.int32)),
         in_specs=[ANY] * 4,
         out_specs=(ANY, VM),
         scratch_shapes=[
@@ -316,7 +317,7 @@
     return jnp.dot(row, w, preferred_element_type=f32)
 
 
-def first_kernel(slots, loads, token, w_hbm, target_hbm, *rest):
+def first_kernel(slots, loads, w_hbm, target_hbm, *rest):
     blocks, outs, (colors, w, target, total, sems, w_sems, t_sem) = rest[:8], rest[8:16], rest[16:]
     copies = load_colors(blocks, colors, sems) + fetch([(target_hbm, target)], t_sem)
     fetch_weights(loads, w_hbm, w, w_sems)
@@ -342,11 +343,11 @@
         copy.wait()
 
 
-def first_render(slots, loads, token, w, target, blocks):
+def first_render(slots, loads, w, target, blocks):
     return pl.pallas_call(
         first_kernel,
         out_shape=(jax.ShapeDtypeStruct((32, C, GB), f32),) * 8,
-        in_specs=[SM, SM, ANY, ANY, ANY] + [ANY] * 8,
+        in_specs=[SM, SM, ANY, ANY] + [ANY] * 8,
         out_specs=(ANY,) * 8,
         scratch_shapes=[
             pltpu.VMEM((N_TILE * BINS, C, GB), bf16),
@@ -360,10 +361,10 @@
         compiler_params=params(RENDER_MIB),
         cost_estimate=pl.CostEstimate(flops=TILES * LBLK * C * GB * PIX * 4, bytes_accessed=25_000_000, transcendentals=0),
         name="first_render",
-    )(slots, loads, token, w, target, *blocks)
-
-
-def second_kernel(slots, loads, token, w_hbm, *rest):
+    )(slots, loads, w, target, *blocks)
+
+
+def second_kernel(slots, loads, w_hbm, *rest):
     blocks, image, (colors, w, sems, w_sems) = rest[:8], rest[8], rest[9:]
     copies = load_colors(blocks, colors, sems)
     fetch_weights(loads, w_hbm, w, w_sems)
@@ -376,11 +377,11 @@
     over_tiles(loads, w_hbm, w, w_sems, body)
 
 
-def second_render(slots, loads, token, w, blocks):
+def second_render(slots, loads, w, blocks):
     return pl.pallas_call(
         second_kernel,
         out_shape=jax.ShapeDtypeStruct((TILES, C, PIX), f32),
-        in_specs=[SM, SM, ANY, ANY] + [ANY] * 8,
+        in_specs=[SM, SM, ANY] + [ANY] * 8,
         out_specs=VM,
         scratch_shapes=[
             pltpu.VMEM((N_TILE * BINS, C, GB), bf16),
@@ -388,13 +389,13 @@
             pltpu.SemaphoreType.DMA((8,)),
             pltpu.SemaphoreType.DMA((TILES,)),
         ],
-        compiler_params=params(RENDER_MIB),
+        compiler_params=params(SECOND_MIB),
         cost_estimate=pl.CostEstimate(flops=TILES * LBLK * C * GB * PIX * 2, bytes_accessed=14_000_000, transcendentals=0),
         name="second_render",
-    )(slots, loads, token, w, *blocks)
-
-
-def adam_kernel(owner, me, gradient, feat, m1, m2, colors, packed):
+    )(slots, loads, w, *blocks)
+
+
+def adam_kernel(owner, me, gradient, feat, m1, m2, close, away, packed, colors):
     g = reorder_wide(gradient[...].reshape(BINS * C, GB), True).reshape(BINS, C, GB)
     first_new = beta_first * m1[...] + (1.0 - beta_first) * g
     second_new = beta_second * m2[...] + (1.0 - beta_second) * g * g
@@ -407,17 +408,21 @@
         packed[w, 0:C] = stepped[s]
         packed[w, C : 2 * C] = first_new[s]
         packed[w, 2 * C : 3 * C] = second_new[s]
+    close[...] = colors[0:4]
+    away[...] = colors[4:]
 
 
 def adam(owner, me, gradient, feat, m1, m2):
     return pl.pallas_call(
         adam_kernel,
         out_shape=(
-            jax.ShapeDtypeStruct((N_VIEW, C, GB), bf16),
+            jax.ShapeDtypeStruct((N_VIEW // 2, C, GB), bf16),
+            jax.ShapeDtypeStruct((N_VIEW // 2, C, GB), bf16),
             jax.ShapeDtypeStruct((N_VIEW, 3 * C, GB), f32),
         ),
         in_specs=[SM, SM, VM, VM, VM, VM],
-        out_specs=(VM, VM),
+        out_specs=(VM, VM, VM),
+        scratch_shapes=[pltpu.VMEM((N_VIEW, C, GB), bf16)],
         compiler_params=params(16),
         name="adam",
     )(owner, me, gradient, feat, m1, m2)
@@ -502,12 +507,14 @@
     return (((core ^ c) * 4 + far) * 4 + near) * BINS + within
 
 
-def exchange_views(colors):
-    def step(r):
-        return lax.ppermute(colors[r : r + 1], "view", [(v, v ^ r) for v in range(N_VIEW)])
-
-    got = {r: step(r) for r in (4, 5, 3, 6, 2, 7, 1)}
-    return jnp.concatenate([colors[0:1]] + [got[r] for r in range(1, N_VIEW)], axis=0)
+def exchange_views(close, away, later):
+    def step(value, r):
+        return lax.ppermute(value, "view", [(v, v ^ r) for v in range(N_VIEW)])
+
+    got = {r: step(away[r - 4 : r - 3], r) for r in (4, 5, 6, 7)}
+    close, later = tie(close, later)
+    got.update({r: step(close[r : r + 1], r) for r in (3, 2, 1)})
+    return jnp.concatenate([close[0:1]] + [got[r] for r in range(1, N_VIEW)], axis=0), later
 
 
 def place_of(view):
@@ -546,21 +553,23 @@
     own, screen = gather_plane(gather_line(colors), screen)
     w_first, token = weights(lists_first[0], loads_first[0], shift_first[0], screen, "weights_first")
     *own, token = tie(*own, token)
-    slots = color_slots(lists_first[0], lists_first[0] % BINS)
-    parts = first_render(slots, loads_first[0], token, w_first, target[0], swapped(own))
+    slots = color_slots(lists_first[0], lists_first[0] % BINS) + token[0, 0]
+    parts = first_render(slots, loads_first[0], w_first, target[0], swapped(own))
     line, geometry = scatter_far(parts, geometry)
     screen = screen_again(cameras_second[0], across_view(geometry))
     line, screen = tie(line, screen)
-    gradient, screen = tie(scatter_near(line), across_tile(screen))
+    screen = across_tile(screen)
+    gradient = scatter_near(line)
+    me = lax.axis_index("view").reshape(1)
+    close, away, packed = adam(owner_after, me, gradient, features, moment_first, moment_second)
+    colors, screen = exchange_views(close, away, screen)
+    colors, packed = tie(colors, packed)
     w_second, token = weights(lists_second[0], loads_second[0], shift_second[0], screen, "weights_second")
-    me = lax.axis_index("view").reshape(1)
-    colors, packed = adam(owner_after, me, gradient, features, moment_first, moment_second)
-    colors, packed = tie(exchange_views(colors), packed)
     packed = across_view(packed)
     *own, token = tie(*gather_plane(gather_line(colors)), token)
     blocks = swapped(own)
-    slots = color_slots(lists_second[0], place_of(lists_second[0] % BINS))
-    image = second_render(slots, loads_second[0], token, w_second, blocks)
+    slots = color_slots(lists_second[0], place_of(lists_second[0] % BINS)) + token[0, 0]
+    image = second_render(slots, loads_second[0], w_second, blocks)
     new_features, new_first, new_second = (packed[:, i * C : i * C + C] for i in range(3))
     return (image[None], new_features, new_first, new_second)
 

time: 161 us -> 156 us (0.969)
  Pallas kernels: 50.7 us -> 42.7 us
  starting transfers between devices: 62.3 us -> 58.5 us
  waiting for transfers between devices: 22.2 us -> 25.9 us
  other arithmetic: 6.1 us -> 2.58 us
  local copies, waits for them, and re-layouts: 2.53 us -> 6.02 us
  blocking collectives: 15.2 us -> 18.1 us
    ppermute x7, waiting for transfers between devices: 1.23 us -> 5.41 us  [step(): return lax.ppermute(value, 'view', [(v, v ^ r) for v in range(N_VIEW)])]
    pallas_call x1, Pallas kernels: 14 us -> 10.2 us  [first_render(): pl.pallas_call(first_kernel, out_shape=(jax.ShapeDtypeStruct((32, C, GB),...]
    convert_element_type x3, other arithmetic: 4.21 us -> 0.59 us  [scatter_far(): sent[k] = (parts[k] + swap_core(parts[4 + k])).astype(half16)]
    pallas_call x2, Pallas kernels: 23.9 us -> 20.6 us  [weights(): pl.pallas_call(weights_kernel, out_shape=(jax.ShapeDtypeStruct((TILES, LB...]
    all_to_all x1, blocking collectives: 15.2 us -> 18.1 us  [across_view(): lax.all_to_all(value, 'view', split_axis=0, concat_axis=0, tiled=True)]
    ppermute x18, waiting for transfers between devices: 0.62 us -> 3.33 us  [shift_by(): return lax.ppermute(value, 'tile', pairs)]
    slice x1 -> x4, local copies, waits for them, and re-layouts: 0.01 us -> 2.41 us  [the longest x1 1.2 us: local(): token[0, 0]]
    all_to_all x2, waiting for transfers between devices: 13.2 us -> 11.2 us  [across_tile(): lax.all_to_all(value, 'tile', split_axis=0, concat_axis=0, tiled=True)]
  transfers between devices with their start and end apart: 40 -> 40, of which waited for: 14 -> 14; matrix products, arithmetic and copies ran while one was open for 4% -> 4% of each run, Pallas kernels for 21% -> 20%
where the time goes in v2:
time: 156 us; the launch traced here: 155 us
  starting transfers between devices  58.5 us (38%)
  Pallas kernels  42.7 us (27%)
  waiting for transfers between devices  25.9 us (17%)
  blocking collectives  18.1 us (12%)
  local copies, waits for them, and re-layouts  6.02 us (4%)
  other arithmetic  2.58 us (2%)
    pallas_call x2, Pallas kernels, weights(): pl.pallas_call(weights_kernel, out_shape=(jax.ShapeDtypeStruct((TILES, LB...  20.6 us
    ppermute x18, starting transfers between devices, shift_by(): return lax.ppermute(value, 'tile', pairs)  19.4 us
    all_to_all x1, blocking collectives, across_view(): lax.all_to_all(value, 'view', split_axis=0, concat_axis=0, tiled=True)  18.1 us
    all_to_all x2, starting transfers between devices, across_tile(): lax.all_to_all(value, 'tile', split_axis=0, concat_axis=0, tiled=True)  14.8 us
    all_to_all x2, waiting for transfers between devices, across_tile(): lax.all_to_all(value, 'tile', split_axis=0, concat_axis=0, tiled=True)  11.2 us
    ppermute x7, starting transfers between devices, step(): return lax.ppermute(value, 'view', [(v, v ^ r) for v in range(N_VIEW)])  11.2 us
    pallas_call x1, Pallas kernels, first_render(): pl.pallas_call(first_kernel, out_shape=(jax.ShapeDtypeStruct((32, C, GB),...  10.2 us
    ppermute x12, starting transfers between devices, swap_core(): return lax.ppermute(value, 'tile', pairs)  8.64 us
  transfers between devices with their start and end apart: 40, of which 14 were waited for; matrix products, arithmetic and copies ran while one was open for 4% of the time, Pallas kernels for 20%

profile of v2, /device:TPU:1, one launch (start us, length us, event | category | flops | bytes accessed | tf_op | source)
XLA Modules:
  0.0 154.9 jit_solution(12781916471865886035)
XLA Ops:
  0.7 2.0 %prep.1 = (bf16[8,64,128]{2,1,0:T(8,128)(2,1)}, bf16[32,32,128]{2,1,0:T(8,128)(2,1)}, f32[8,8,128]{2,1,0:T(8,128)}) custom-call(f32[1,2,4]{2,1,0:T(2,128)} %camera_hbm.1, s32[8]{0:T(128)} %owner.1, f32[8,64,128]{2,1,0:T(8,128)} %feat.1, f32[3,8,128]{2,1,0:T(8,128)} %bitcast.28, f32[8,128]{1,0:T(8,128)} %scales_hbm.1, f32[8,128]{1,0:T(8,128)} %opacity_hbm.1), custom_call_target="tpu_custom_call" | custom-call | tf_op jit(solution)/shard_map/prep/pallas_call | solution.py:117
  2.7 2.2 %collective-permute-start = (bf16[8,64,128]{2,1,0:T(8,128)(2,1)}, bf16[8,64,128]{2,1,0:T(8,128)(2,1)S(1)}, u32[]{:S(2)}, u32[]{:S(2)}) collective-permute-start(bf16[8,64,128]{2,1,0:T(8,128)(2,1)} %get-tuple-element.42), channel_id=1, source_target_pairs={{0,8},{1,3},{2,10},{3,5},{4,12},{5,7},{6,14},{7,1},{8,16},{9,11},{... | collective-permute-start | bytes 393224 | tf_op jit(solution)/shard_map/ppermute | solution.py:442
  4.9 2.6 %collective-permute-start.1 = (bf16[8,64,128]{2,1,0:T(8,128)(2,1)}, bf16[8,64,128]{2,1,0:T(8,128)(2,1)S(1)}, u32[]{:S(2)}, u32[]{:S(2)}) collective-permute-start(bf16[8,64,128]{2,1,0:T(8,128)(2,1)} %get-tuple-element.42), channel_id=1, source_target_pairs={{0,16},{1,5},{2,18},{3,7},{4,20},{5,1},{6,22},{7,3},{8,24},{9,13},... | collective-permute-start | bytes 393224 | tf_op jit(solution)/shard_map/ppermute | solution.py:442
  7.5 1.1 collective-permute-start.2
  8.6 6.0 %all-to-all-start = ((bf16[32,32,128]{2,1,0:T(8,128)(2,1)}), bf16[32,32,128]{2,1,0:T(8,128)(2,1)S(1)}, u32[]{:S(2)}, u32[]{:S(2)}) async-start(bf16[32,32,128]{2,1,0:T(8,128)(2,1)} %get-tuple-element.43), calls=%async_computation | async-start | bytes 524288 | tf_op jit(solution)/shard_map/all_to_all | solution.py:529
  14.6 0.9 constant_dynamic-update-slice_fusion.3
  15.6 1.5 collective-permute-start.3
  17.1 2.4 %collective-permute-start.4 = (bf16[32,64,128]{2,1,0:T(8,128)(2,1)S(1)}, bf16[32,64,128]{2,1,0:T(8,128)(2,1)S(1)}, u32[]{:S(2)}, u32[]{:S(2)}) collective-permute-start(bf16[32,64,128]{2,1,0:T(8,128)(2,1)S(1)} %constant_dynamic-update-slice_fusion.rest_0_), channel_id=1, source_target_pairs={{0,4},{1,17},{2,6},{3,19},{4,0},{5,21},{6,2},{7,23},{8,12},{9,25},... | collective-permute-start | bytes 1572872 | tf_op jit(solution)/shard_map/ppermute | solution.py:442
  19.5 4.4 %all-to-all-done.screen_hbm = bf16[32,32,128]{2,1,0:T(8,128)(2,1)S(1)} async-done(((bf16[32,32,128]{2,1,0:T(8,128)(2,1)}), bf16[32,32,128]{2,1,0:T(8,128)(2,1)S(1)}, u32[]{:S(2)}, u32[]{:S(2)}) %all-to-all-start) | async-done | bytes 262176 | tf_op jit(solution)/shard_map/all_to_all | solution.py:529
  24.6 11.2 %weights_first.1 = (bf16[16,8,128,256]{3,2,1,0:T(8,128)(2,1)}, s32[8,128]{1,0:T(8,128)}) custom-call(s32[8,16]{1,0:T(8,128)} %bitcast.29, s32[16]{0:T(128)} %bitcast.23, f32[2,16]{1,0:T(2,128)} %bitcast.33, bf16[32,32,128]{2,1,0:T(8,128)(2,1)} %copy-done.9), custom_call_target="tpu_custom_call" | custom-call | flops 58720256 | bytes 10000000 | tf_op jit(solution)/shard_map/weights_first/pallas_call | solution.py:257
  37.0 1.2 slice.54
  38.2 0.7 fusion.16.slots
  38.9 0.5 collective-permute-done.8.rest_6_
  39.4 0.7 collective-permute-done.9.rest_7_
  40.2 10.2 %first_render.1 = (f32[32,64,128]{2,1,0:T(8,128)S(1)}, f32[32,64,128]{2,1,0:T(8,128)S(1)}, f32[32,64,128]{2,1,0:T(8,128)S(1)}, f32[32,64,128]{2,1,0:T(8,128)S(1)...) custom-call(s32[16,8]{1,0:T(8,128)S(1)} %fusion.16.slots, ...), custom_call_target="tpu_custom_call" | custom-call | flops 1073741824 | bytes 25000000 | tf_op jit(solution)/shard_map/first_render/pallas_call | solution.py:347
  51.6 1.6 %collective-permute-done.11 = f32[32,64,128]{2,1,0:T(8,128)S(1)} collective-permute-done((f32[32,64,128]{2,1,0:T(8,128)S(1)}, f32[32,64,128]{2,1,0:T(8,128)S(1)}, u32[]{:S(2)}, u32[]{:S(2)}) %collective-permute-start.11) | collective-permute-done | bytes 1048608 | tf_op jit(solution)/shard_map/ppermute | solution.py:447
  53.8 1.0 collective-permute-done.13
  54.9 0.7 collective-permute-start.14
  55.7 0.6 collective-permute-done.15
  56.8 18.1 %all_to_all.20.geometry = f32[8,8,128]{2,1,0:T(8,128)S(1)} all-to-all(f32[8,8,128]{2,1,0:T(8,128)S(1)} %copy-done.10), channel_id=1, replica_groups=mesh['view'=8,'tile'=32] {'view'}, dimensions={0} | all-to-all | bytes 65536 | tf_op jit(solution)/shard_map/all_to_all | solution.py:525
  74.8 1.4 screen_again.1
  77.1 0.6 collective-permute-start.18
  77.7 0.9 collective-permute-start.19
  78.6 8.8 %all-to-all-start.2 = ((bf16[32,32,128]{2,1,0:T(8,128)(2,1)}), bf16[32,32,128]{2,1,0:T(8,128)(2,1)S(1)}, u32[]{:S(2)}, u32[]{:S(2)}) async-start(bf16[32,32,128]{2,1,0:T(8,128)(2,1)} %screen_again.1), calls=%async_computation.2 | async-start | bytes 524288 | tf_op jit(solution)/shard_map/all_to_all | solution.py:529
  87.6 2.0 %adam.1 = (bf16[4,64,128]{2,1,0:T(8,128)(2,1)S(1)}, bf16[4,64,128]{2,1,0:T(8,128)(2,1)S(1)}, f32[8,192,128]{2,1,0:T(8,128)}) custom-call(s32[8]{0:T(128)S(1)} %copy-done.4, s32[1]{0:T(128)} %bitcast.1.me, f32[8,64,128]{2,1,0:T(8,128)S(1)} %convert_add_fusion.1.gradient, f32[8,64,128]{2,1,0:T(8,128)S(1)} %copy-done, f32[8,64,128]{2,1,0:T(8,128)S(1)} %copy-done.2, ...), custom_call_target="tpu_custom_call" | custom-call | tf_op jit(solution)/shard_map/adam/pallas_call | solution.py:416
  89.6 6.9 %all-to-all-done.2.screen_hbm = bf16[32,32,128]{2,1,0:T(8,128)(2,1)S(1)} async-done(((bf16[32,32,128]{2,1,0:T(8,128)(2,1)}), bf16[32,32,128]{2,1,0:T(8,128)(2,1)S(1)}, u32[]{:S(2)}, u32[]{:S(2)}) %all-to-all-start.2) | async-done | bytes 262176 | tf_op jit(solution)/shard_map/all_to_all | solution.py:529
  96.8 1.5 collective-permute-start.23
  98.3 3.9 %collective-permute-start.24 = (bf16[1,64,128]{2,1,0:T(8,128)(2,1)S(1)}, bf16[1,64,128]{2,1,0:T(8,128)(2,1)S(1)}, u32[]{:S(2)}, u32[]{:S(2)}) collective-permute-start(bf16[1,64,128]{2,1,0:T(8,128)(2,1)S(1)} %get-tuple-element.88), channel_id=1, source_target_pairs={{0,160},{32,128},{64,224},{96,192},{128,32},{160,0},{192,96},{224,... | collective-permute-start | bytes 49160 | tf_op jit(solution)/shard_map/ppermute | solution.py:512
  102.7 2.2 %collective-permute-start.26 = (bf16[1,64,128]{2,1,0:T(8,128)(2,1)S(1)}, bf16[1,64,128]{2,1,0:T(8,128)(2,1)S(1)}, u32[]{:S(2)}, u32[]{:S(2)}) collective-permute-start(bf16[1,64,128]{2,1,0:T(8,128)(2,1)S(1)} %get-tuple-element.86), channel_id=1, source_target_pairs={{0,224},{32,192},{64,160},{96,128},{128,96},{160,64},{192,32},{224... | collective-permute-start | bytes 49160 | tf_op jit(solution)/shard_map/ppermute | solution.py:512
  104.9 1.2 collective-permute-start.21
  106.1 2.6 %collective-permute-done.21 = bf16[1,64,128]{2,1,0:T(8,128)(2,1)S(1)} collective-permute-done((bf16[1,64,128]{2,1,0:T(8,128)(2,1)S(1)}, bf16[1,64,128]{2,1,0:T(8,128)(2,1)S(1)}, u32[]{:S(2)}, u32[]{:S(2)}) %collective-permute-start.21) | collective-permute-done | bytes 16416 | tf_op jit(solution)/shard_map/ppermute | solution.py:512
  108.7 1.6 %collective-permute-start.22 = (bf16[1,64,128]{2,1,0:T(8,128)(2,1)S(1)}, bf16[1,64,128]{2,1,0:T(8,128)(2,1)S(1)}, u32[]{:S(2)}, u32[]{:S(2)}) collective-permute-start(bf16[1,64,128]{2,1,0:T(8,128)(2,1)S(1)} %get-tuple-element.90), channel_id=1, source_target_pairs={{0,96},{32,64},{64,32},{96,0},{128,224},{160,192},{192,160},{224,1... | collective-permute-start | bytes 49160 | tf_op jit(solution)/shard_map/ppermute | solution.py:512
  110.3 2.8 %collective-permute-done.22 = bf16[1,64,128]{2,1,0:T(8,128)(2,1)S(1)} collective-permute-done((bf16[1,64,128]{2,1,0:T(8,128)(2,1)S(1)}, bf16[1,64,128]{2,1,0:T(8,128)(2,1)S(1)}, u32[]{:S(2)}, u32[]{:S(2)}) %collective-permute-start.22) | collective-permute-done | bytes 16416 | tf_op jit(solution)/shard_map/ppermute | solution.py:512
  113.3 2.0 %collective-permute-start.28 = (bf16[8,64,128]{2,1,0:T(8,128)(2,1)S(1)}, bf16[8,64,128]{2,1,0:T(8,128)(2,1)S(1)}, u32[]{:S(2)}, u32[]{:S(2)}) collective-permute-start(bf16[8,64,128]{2,1,0:T(8,128)(2,1)S(1)} %constant_dynamic-update-slice_fusion.4), channel_id=1, source_target_pairs={{0,16},{1,5},{2,18},{3,7},{4,20},{5,1},{6,22},{7,3},{8,24},{9,13},... | collective-permute-start | bytes 393224 | tf_op jit(solution)/shard_map/ppermute | solution.py:442
  115.3 0.8 collective-permute-start.29
  116.0 4.4 %all-to-all-start.3 = ((f32[8,192,128]{2,1,0:T(8,128)}), f32[8,192,128]{2,1,0:T(8,128)}, u32[]{:S(2)}, u32[]{:S(2)}) async-start(f32[8,192,128]{2,1,0:T(8,128)} %get-tuple-element.79), calls=%async_computation.3 | async-start | bytes 1572864 | tf_op jit(solution)/shard_map/all_to_all | solution.py:525
  121.0 1.7 %collective-permute-start.31 = (bf16[32,64,128]{2,1,0:T(8,128)(2,1)S(1)}, bf16[32,64,128]{2,1,0:T(8,128)(2,1)S(1)}, u32[]{:S(2)}, u32[]{:S(2)}) collective-permute-start(bf16[32,64,128]{2,1,0:T(8,128)(2,1)S(1)} %constant_dynamic-update-slice_fusion.12.rest_0_), channel_id=1, source_target_pairs={{0,4},{1,17},{2,6},{3,19},{4,0},{5,21},{6,2},{7,23},{8,12},{9,25},... | collective-permute-start | bytes 1572872 | tf_op jit(solution)/shard_map/ppermute | solution.py:442
  122.7 1.1 collective-permute-start.32
  123.8 9.4 %weights_second.1 = (bf16[16,8,128,256]{3,2,1,0:T(8,128)(2,1)}, s32[8,128]{1,0:T(8,128)}) custom-call(s32[8,16]{1,0:T(8,128)} %bitcast.31, s32[16]{0:T(128)} %bitcast.25, f32[2,16]{1,0:T(2,128)} %bitcast.34, bf16[32,32,128]{2,1,0:T(8,128)(2,1)} %copy-done.8), custom_call_target="tpu_custom_call" | custom-call | flops 58720256 | bytes 10000000 | tf_op jit(solution)/shard_map/weights_second/pallas_call | solution.py:257
  133.3 2.7 %collective-permute-done.30.rest_1_ = bf16[32,64,128]{2,1,0:T(8,128)(2,1)S(1)} collective-permute-done((bf16[32,64,128]{2,1,0:T(8,128)(2,1)S(1)}, bf16[32,64,128]{2,1,0:T(8,128)(2,1)S(1)}, u32[]{:S(2)}, u32[]{:S(2)}) %collective-permute-start.30) | collective-permute-done | bytes 524320 | tf_op jit(solution)/shard_map/ppermute | solution.py:442
  135.9 0.6 collective-permute-done.32.rest_3_
  136.6 5.9 %collective-permute-start.33 = (bf16[32,64,128]{2,1,0:T(8,128)(2,1)S(1)}, bf16[32,64,128]{2,1,0:T(8,128)(2,1)S(1)}, u32[]{:S(2)}, u32[]{:S(2)}) collective-permute-start(bf16[32,64,128]{2,1,0:T(8,128)(2,1)S(1)} %constant_dynamic-update-slice_fusion.12.rest_0_), channel_id=1, source_target_pairs={{0,1},{1,0},{2,3},{3,2},{4,5},{5,4},{6,7},{7,6},{8,9},{9,8},{10,11... | collective-permute-start | bytes 1572872 | tf_op jit(solution)/shard_map/ppermute | solution.py:447
  143.1 1.2 slice.67
  144.3 0.7 fusion.8.slots
  145.0 0.5 collective-permute-done.34.rest_5_
  145.7 0.8 collective-permute-done.36.rest_7_
  146.4 6.5 %second_render.1 = f32[16,64,256]{2,1,0:T(8,128)} custom-call(s32[16,8]{1,0:T(8,128)S(1)} %fusion.8.slots, s32[16]{0:T(128)S(1)} %bitcast.26, bf16[16,8,128,256]{3,2,1,0:T(8,128)(2,1)} %get-tuple-element.74.w_hbm, bf16[32,64,128]{2,1,0:T(8,128)(2,1)S(1)} %constant_dynamic-update-slice_fusion.12.rest_0_, ...), custom_call_target="tpu_custom_call" | custom-call | flops 536870912 | bytes 14000000 | tf_op jit(solution)/shard_map/second_render/pallas_call | solution.py:381
  152.9 2.0 %fusion.23 = (f32[8,64,128]{2,1,0:T(8,128)}, f32[8,64,128]{2,1,0:T(8,128)}, f32[8,64,128]{2,1,0:T(8,128)}) fusion(f32[8,192,128]{2,1,0:T(8,128)} %all-to-all-done.3), kind=kLoop, calls=%fused_computation.92 | loop fusion | bytes 1572864 | tf_op jit(solution)/shard_map/slice | solution.py:573
  (97 shorter events, 7.4 us)
Async XLA Ops:
  0.6 39.5 %copy-start.6 = (s32[1,16]{1,0:T(1,128)S(1)}, s32[1,16]{1,0:T(1,128)}, u32[]{:S(2)}) copy-start(s32[1,16]{1,0:T(1,128)} %param.25) | copy-start | bytes 196
  0.7 39.5 %copy-start.1 = (bf16[1,16,64,256]{3,2,1,0:T(8,128)(2,1)S(1)}, bf16[1,16,64,256]{3,2,1,0:T(8,128)(2,1)}, u32[]{:S(2)}) copy-start(bf16[1,16,64,256]{3,2,1,0:T(8,128)(2,1)} %param.26) | copy-start | bytes 1572868
  2.7 12.8 %collective-permute-start = (bf16[8,64,128]{2,1,0:T(8,128)(2,1)}, bf16[8,64,128]{2,1,0:T(8,128)(2,1)S(1)}, u32[]{:S(2)}, u32[]{:S(2)}) collective-permute-start(bf16[8,64,128]{2,1,0:T(8,128)(2,1)} %get-tuple-element.42), channel_id=1, source_target_pairs={{0,8},{1,3},{2,10},{3,5},{4,12},{5,7},{6,14},{7,1},{8,16},{9,11},{... | collective-permute-start | bytes 393224 | tf_op jit(solution)/shard_map/ppermute | solution.py:442
  4.9 10.7 %collective-permute-start.1 = (bf16[8,64,128]{2,1,0:T(8,128)(2,1)}, bf16[8,64,128]{2,1,0:T(8,128)(2,1)S(1)}, u32[]{:S(2)}, u32[]{:S(2)}) collective-permute-start(bf16[8,64,128]{2,1,0:T(8,128)(2,1)} %get-tuple-element.42), channel_id=1, source_target_pairs={{0,16},{1,5},{2,18},{3,7},{4,20},{5,1},{6,22},{7,3},{8,24},{9,13},... | collective-permute-start | bytes 393224 | tf_op jit(solution)/shard_map/ppermute | solution.py:442
  7.5 8.1 %collective-permute-start.2 = (bf16[8,64,128]{2,1,0:T(8,128)(2,1)}, bf16[8,64,128]{2,1,0:T(8,128)(2,1)S(1)}, u32[]{:S(2)}, u32[]{:S(2)}) collective-permute-start(bf16[8,64,128]{2,1,0:T(8,128)(2,1)} %get-tuple-element.42), channel_id=1, source_target_pairs={{0,24},{1,7},{2,26},{3,1},{4,28},{5,3},{6,30},{7,5},{8,0},{9,15},{... | collective-permute-start | bytes 393224 | tf_op jit(solution)/shard_map/ppermute | solution.py:442
  8.6 15.3 %all-to-all-start = ((bf16[32,32,128]{2,1,0:T(8,128)(2,1)}), bf16[32,32,128]{2,1,0:T(8,128)(2,1)S(1)}, u32[]{:S(2)}, u32[]{:S(2)}) async-start(bf16[32,32,128]{2,1,0:T(8,128)(2,1)} %get-tuple-element.43), calls=%async_computation | async-start | bytes 524288 | tf_op jit(solution)/shard_map/all_to_all | solution.py:529
  15.6 20.2 %collective-permute-start.3 = (bf16[32,64,128]{2,1,0:T(8,128)(2,1)S(1)}, bf16[32,64,128]{2,1,0:T(8,128)(2,1)S(1)}, u32[]{:S(2)}, u32[]{:S(2)}) collective-permute-start(bf16[32,64,128]{2,1,0:T(8,128)(2,1)S(1)} %constant_dynamic-update-slice_fusion.rest_0_), channel_id=1, source_target_pairs={{0,2},{1,9},{2,4},{3,11},{4,6},{5,13},{6,0},{7,15},{8,10},{9,17},{... | collective-permute-start | bytes 1572872 | tf_op jit(solution)/shard_map/ppermute | solution.py:442
  17.1 18.7 %collective-permute-start.4 = (bf16[32,64,128]{2,1,0:T(8,128)(2,1)S(1)}, bf16[32,64,128]{2,1,0:T(8,128)(2,1)S(1)}, u32[]{:S(2)}, u32[]{:S(2)}) collective-permute-start(bf16[32,64,128]{2,1,0:T(8,128)(2,1)S(1)} %constant_dynamic-update-slice_fusion.rest_0_), channel_id=1, source_target_pairs={{0,4},{1,17},{2,6},{3,19},{4,0},{5,21},{6,2},{7,23},{8,12},{9,25},... | collective-permute-start | bytes 1572872 | tf_op jit(solution)/shard_map/ppermute | solution.py:442
  23.9 11.9 %collective-permute-start.5 = (bf16[32,64,128]{2,1,0:T(8,128)(2,1)S(1)}, bf16[32,64,128]{2,1,0:T(8,128)(2,1)S(1)}, u32[]{:S(2)}, u32[]{:S(2)}) collective-permute-start(bf16[32,64,128]{2,1,0:T(8,128)(2,1)S(1)} %constant_dynamic-update-slice_fusion.rest_0_), channel_id=1, source_target_pairs={{0,6},{1,25},{2,0},{3,27},{4,2},{5,29},{6,4},{7,31},{8,14},{9,1},{... | collective-permute-start | bytes 1572872 | tf_op jit(solution)/shard_map/ppermute | solution.py:442
  35.8 3.1 %collective-permute-start.6 = (bf16[32,64,128]{2,1,0:T(8,128)(2,1)S(1)}, bf16[32,64,128]{2,1,0:T(8,128)(2,1)S(1)}, u32[]{:S(2)}, u32[]{:S(2)}) collective-permute-start(bf16[32,64,128]{2,1,0:T(8,128)(2,1)S(1)} %constant_dynamic-update-slice_fusion.rest_0_), channel_id=1, source_target_pairs={{0,1},{1,0},{2,3},{3,2},{4,5},{5,4},{6,7},{7,6},{8,9},{9,8},{10,11... | collective-permute-start | bytes 1572872 | tf_op jit(solution)/shard_map/ppermute | solution.py:447
  35.9 3.0 %collective-permute-start.7 = (bf16[32,64,128]{2,1,0:T(8,128)(2,1)S(1)}, bf16[32,64,128]{2,1,0:T(8,128)(2,1)}, u32[]{:S(2)}, u32[]{:S(2)}) collective-permute-start(bf16[32,64,128]{2,1,0:T(8,128)(2,1)S(1)} %collective-permute-done.3.rest_1_), channel_id=1, source_target_pairs={{0,1},{1,0},{2,3},{3,2},{4,5},{5,4},{6,7},{7,6},{8,9},{9,8},{10,11... | collective-permute-start | bytes 1572872 | tf_op jit(solution)/shard_map/ppermute | solution.py:447
  36.4 3.0 %collective-permute-start.8 = (bf16[32,64,128]{2,1,0:T(8,128)(2,1)S(1)}, bf16[32,64,128]{2,1,0:T(8,128)(2,1)}, u32[]{:S(2)}, u32[]{:S(2)}) collective-permute-start(bf16[32,64,128]{2,1,0:T(8,128)(2,1)S(1)} %collective-permute-done.4.rest_2_), channel_id=1, source_target_pairs={{0,1},{1,0},{2,3},{3,2},{4,5},{5,4},{6,7},{7,6},{8,9},{9,8},{10,11... | collective-permute-start | bytes 1572872 | tf_op jit(solution)/shard_map/ppermute | solution.py:447
  36.5 3.7 %collective-permute-start.9 = (bf16[32,64,128]{2,1,0:T(8,128)(2,1)S(1)}, bf16[32,64,128]{2,1,0:T(8,128)(2,1)}, u32[]{:S(2)}, u32[]{:S(2)}) collective-permute-start(bf16[32,64,128]{2,1,0:T(8,128)(2,1)S(1)} %collective-permute-done.5.rest_3_), channel_id=1, source_target_pairs={{0,1},{1,0},{2,3},{3,2},{4,5},{5,4},{6,7},{7,6},{8,9},{9,8},{10,11... | collective-permute-start | bytes 1572872 | tf_op jit(solution)/shard_map/ppermute | solution.py:447
  50.4 37.2 %copy-start = (f32[8,64,128]{2,1,0:T(8,128)S(1)}, f32[8,64,128]{2,1,0:T(8,128)}, u32[]{:S(2)}) copy-start(f32[8,64,128]{2,1,0:T(8,128)} %feat.1) | copy-start | bytes 786436
  50.4 37.2 %copy-start.2 = (f32[8,64,128]{2,1,0:T(8,128)S(1)}, f32[8,64,128]{2,1,0:T(8,128)}, u32[]{:S(2)}) copy-start(f32[8,64,128]{2,1,0:T(8,128)} %m1.1) | copy-start | bytes 786436
  50.4 37.2 %copy-start.3 = (f32[8,64,128]{2,1,0:T(8,128)S(1)}, f32[8,64,128]{2,1,0:T(8,128)}, u32[]{:S(2)}) copy-start(f32[8,64,128]{2,1,0:T(8,128)} %m2.1) | copy-start | bytes 786436
  50.5 37.2 %copy-start.4 = (s32[8]{0:T(128)S(1)}, s32[8]{0:T(128)}, u32[]{:S(2)}) copy-start(s32[8]{0:T(128)} %owner.1) | copy-start | bytes 100
  50.5 2.7 %collective-permute-start.11 = (f32[32,64,128]{2,1,0:T(8,128)S(1)}, f32[32,64,128]{2,1,0:T(8,128)S(1)}, u32[]{:S(2)}, u32[]{:S(2)}) collective-permute-start(f32[32,64,128]{2,1,0:T(8,128)S(1)} %get-tuple-element.56), channel_id=1, source_target_pairs={{0,1},{1,0},{2,3},{3,2},{4,5},{5,4},{6,7},{7,6},{8,9},{9,8},{10,11... | collective-permute-start | bytes 3145736 | tf_op jit(solution)/shard_map/ppermute | solution.py:447
  50.6 4.1 %collective-permute-start.13 = (f32[32,64,128]{2,1,0:T(8,128)S(1)}, f32[32,64,128]{2,1,0:T(8,128)S(1)}, u32[]{:S(2)}, u32[]{:S(2)}) collective-permute-start(f32[32,64,128]{2,1,0:T(8,128)S(1)} %get-tuple-element.58), channel_id=1, source_target_pairs={{0,1},{1,0},{2,3},{3,2},{4,5},{5,4},{6,7},{7,6},{8,9},{9,8},{10,11... | collective-permute-start | bytes 3145736 | tf_op jit(solution)/shard_map/ppermute | solution.py:447
  51.1 5.1 %collective-permute-start.15 = (f32[32,64,128]{2,1,0:T(8,128)S(1)}, f32[32,64,128]{2,1,0:T(8,128)S(1)}, u32[]{:S(2)}, u32[]{:S(2)}) collective-permute-start(f32[32,64,128]{2,1,0:T(8,128)S(1)} %get-tuple-element.60), channel_id=1, source_target_pairs={{0,1},{1,0},{2,3},{3,2},{4,5},{5,4},{6,7},{7,6},{8,9},{9,8},{10,11... | collective-permute-start | bytes 3145736 | tf_op jit(solution)/shard_map/ppermute | solution.py:447
  51.2 25.1 %collective-permute-start.10 = (f32[32,64,128]{2,1,0:T(8,128)S(1)}, f32[32,64,128]{2,1,0:T(8,128)S(1)}, u32[]{:S(2)}, u32[]{:S(2)}) collective-permute-start(f32[32,64,128]{2,1,0:T(8,128)S(1)} %get-tuple-element.54), channel_id=1, source_target_pairs={{0,1},{1,0},{2,3},{3,2},{4,5},{5,4},{6,7},{7,6},{8,9},{9,8},{10,11... | collective-permute-start | bytes 3145736 | tf_op jit(solution)/shard_map/ppermute | solution.py:447
  53.4 22.9 %collective-permute-start.12 = (f16[32,64,128]{2,1,0:T(8,128)(2,1)S(1)}, f16[32,64,128]{2,1,0:T(8,128)(2,1)S(1)}, u32[]{:S(2)}, u32[]{:S(2)}) collective-permute-start(f16[32,64,128]{2,1,0:T(8,128)(2,1)S(1)} %add_convert_fusion.2), channel_id=1, source_target_pairs={{0,4},{1,17},{2,6},{3,19},{4,0},{5,21},{6,2},{7,23},{8,12},{9,25},... | collective-permute-start | bytes 1572872 | tf_op jit(solution)/shard_map/ppermute | solution.py:442
  54.9 21.4 %collective-permute-start.14 = (f16[32,64,128]{2,1,0:T(8,128)(2,1)S(1)}, f16[32,64,128]{2,1,0:T(8,128)(2,1)S(1)}, u32[]{:S(2)}, u32[]{:S(2)}) collective-permute-start(f16[32,64,128]{2,1,0:T(8,128)(2,1)S(1)} %add_convert_fusion.1), channel_id=1, source_target_pairs={{0,6},{1,25},{2,0},{3,27},{4,2},{5,29},{6,4},{7,31},{8,14},{9,1},{... | collective-permute-start | bytes 1572872 | tf_op jit(solution)/shard_map/ppermute | solution.py:442
  56.4 19.9 %collective-permute-start.16 = (f16[32,64,128]{2,1,0:T(8,128)(2,1)S(1)}, f16[32,64,128]{2,1,0:T(8,128)(2,1)S(1)}, u32[]{:S(2)}, u32[]{:S(2)}) collective-permute-start(f16[32,64,128]{2,1,0:T(8,128)(2,1)S(1)} %add_convert_fusion), channel_id=1, source_target_pairs={{0,2},{1,9},{2,4},{3,11},{4,6},{5,13},{6,0},{7,15},{8,10},{9,17},{... | collective-permute-start | bytes 1572872 | tf_op jit(solution)/shard_map/ppermute | solution.py:442
  76.8 66.2 %copy-start.12 = (s32[1,16,8]{1,2,0:T(8,128)S(1)}, s32[1,16,8]{1,2,0:T(8,128)}, u32[]{:S(2)}) copy-start(s32[1,16,8]{1,2,0:T(8,128)} %param.30) | copy-start | bytes 1540
  76.8 69.6 %copy-start.7 = (s32[1,16]{1,0:T(1,128)S(1)}, s32[1,16]{1,0:T(1,128)}, u32[]{:S(2)}) copy-start(s32[1,16]{1,0:T(1,128)} %param.31) | copy-start | bytes 196
  77.0 10.5 %collective-permute-start.17 = (f16[8,64,128]{2,1,0:T(8,128)(2,1)S(1)}, f16[8,64,128]{2,1,0:T(8,128)(2,1)S(1)}, u32[]{:S(2)}, u32[]{:S(2)}) collective-permute-start(f16[8,64,128]{2,1,0:T(8,128)(2,1)S(1)} %get-tuple-element.83), channel_id=1, source_target_pairs={{0,16},{1,5},{2,18},{3,7},{4,20},{5,1},{6,22},{7,3},{8,24},{9,13},... | collective-permute-start | bytes 393224 | tf_op jit(solution)/shard_map/ppermute | solution.py:442
  77.1 10.4 %collective-permute-start.18 = (f16[8,64,128]{2,1,0:T(8,128)(2,1)S(1)}, f16[8,64,128]{2,1,0:T(8,128)(2,1)S(1)}, u32[]{:S(2)}, u32[]{:S(2)}) collective-permute-start(f16[8,64,128]{2,1,0:T(8,128)(2,1)S(1)} %get-tuple-element.85), channel_id=1, source_target_pairs={{0,24},{1,7},{2,26},{3,1},{4,28},{5,3},{6,30},{7,5},{8,0},{9,15},{... | collective-permute-start | bytes 393224 | tf_op jit(solution)/shard_map/ppermute | solution.py:442
  77.7 9.8 %collective-permute-start.19 = (f16[8,64,128]{2,1,0:T(8,128)(2,1)S(1)}, f16[8,64,128]{2,1,0:T(8,128)(2,1)S(1)}, u32[]{:S(2)}, u32[]{:S(2)}) collective-permute-start(f16[8,64,128]{2,1,0:T(8,128)(2,1)S(1)} %get-tuple-element.84), channel_id=1, source_target_pairs={{0,8},{1,3},{2,10},{3,5},{4,12},{5,7},{6,14},{7,1},{8,16},{9,11},{... | collective-permute-start | bytes 393224 | tf_op jit(solution)/shard_map/ppermute | solution.py:442
  78.6 17.8 %all-to-all-start.2 = ((bf16[32,32,128]{2,1,0:T(8,128)(2,1)}), bf16[32,32,128]{2,1,0:T(8,128)(2,1)S(1)}, u32[]{:S(2)}, u32[]{:S(2)}) async-start(bf16[32,32,128]{2,1,0:T(8,128)(2,1)} %screen_again.1), calls=%async_computation.2 | async-start | bytes 524288 | tf_op jit(solution)/shard_map/all_to_all | solution.py:529
  96.5 8.4 %collective-permute-start.20 = (bf16[1,64,128]{2,1,0:T(8,128)(2,1)S(1)}, bf16[1,64,128]{2,1,0:T(8,128)(2,1)S(1)}, u32[]{:S(2)}, u32[]{:S(2)}) collective-permute-start(bf16[1,64,128]{2,1,0:T(8,128)(2,1)S(1)} %get-tuple-element.92), channel_id=1, source_target_pairs={{0,32},{32,0},{64,96},{96,64},{128,160},{160,128},{192,224},{224,1... | collective-permute-start | bytes 49160 | tf_op jit(solution)/shard_map/ppermute | solution.py:512
  96.8 16.3 %collective-permute-start.23 = (bf16[1,64,128]{2,1,0:T(8,128)(2,1)S(1)}, bf16[1,64,128]{2,1,0:T(8,128)(2,1)S(1)}, u32[]{:S(2)}, u32[]{:S(2)}) collective-permute-start(bf16[1,64,128]{2,1,0:T(8,128)(2,1)S(1)} %get-tuple-element.89), channel_id=1, source_target_pairs={{0,128},{32,160},{64,192},{96,224},{128,0},{160,32},{192,64},{224,... | collective-permute-start | bytes 49160 | tf_op jit(solution)/shard_map/ppermute | solution.py:512
  98.3 14.8 %collective-permute-start.24 = (bf16[1,64,128]{2,1,0:T(8,128)(2,1)S(1)}, bf16[1,64,128]{2,1,0:T(8,128)(2,1)S(1)}, u32[]{:S(2)}, u32[]{:S(2)}) collective-permute-start(bf16[1,64,128]{2,1,0:T(8,128)(2,1)S(1)} %get-tuple-element.88), channel_id=1, source_target_pairs={{0,160},{32,128},{64,224},{96,192},{128,32},{160,0},{192,96},{224,... | collective-permute-start | bytes 49160 | tf_op jit(solution)/shard_map/ppermute | solution.py:512
  102.2 10.9 %collective-permute-start.25 = (bf16[1,64,128]{2,1,0:T(8,128)(2,1)S(1)}, bf16[1,64,128]{2,1,0:T(8,128)(2,1)S(1)}, u32[]{:S(2)}, u32[]{:S(2)}) collective-permute-start(bf16[1,64,128]{2,1,0:T(8,128)(2,1)S(1)} %get-tuple-element.87), channel_id=1, source_target_pairs={{0,192},{32,224},{64,128},{96,160},{128,64},{160,96},{192,0},{224,... | collective-permute-start | bytes 49160 | tf_op jit(solution)/shard_map/ppermute | solution.py:512
  102.7 10.5 %collective-permute-start.26 = (bf16[1,64,128]{2,1,0:T(8,128)(2,1)S(1)}, bf16[1,64,128]{2,1,0:T(8,128)(2,1)S(1)}, u32[]{:S(2)}, u32[]{:S(2)}) collective-permute-start(bf16[1,64,128]{2,1,0:T(8,128)(2,1)S(1)} %get-tuple-element.86), channel_id=1, source_target_pairs={{0,224},{32,192},{64,160},{96,128},{128,96},{160,64},{192,32},{224... | collective-permute-start | bytes 49160 | tf_op jit(solution)/shard_map/ppermute | solution.py:512
  104.9 3.8 %collective-permute-start.21 = (bf16[1,64,128]{2,1,0:T(8,128)(2,1)S(1)}, bf16[1,64,128]{2,1,0:T(8,128)(2,1)S(1)}, u32[]{:S(2)}, u32[]{:S(2)}) collective-permute-start(bf16[1,64,128]{2,1,0:T(8,128)(2,1)S(1)} %get-tuple-element.91), channel_id=1, source_target_pairs={{0,64},{32,96},{64,0},{96,32},{128,192},{160,224},{192,128},{224,1... | collective-permute-start | bytes 49160 | tf_op jit(solution)/shard_map/ppermute | solution.py:512
  108.7 4.4 %collective-permute-start.22 = (bf16[1,64,128]{2,1,0:T(8,128)(2,1)S(1)}, bf16[1,64,128]{2,1,0:T(8,128)(2,1)S(1)}, u32[]{:S(2)}, u32[]{:S(2)}) collective-permute-start(bf16[1,64,128]{2,1,0:T(8,128)(2,1)S(1)} %get-tuple-element.90), channel_id=1, source_target_pairs={{0,96},{32,64},{64,32},{96,0},{128,224},{160,192},{192,160},{224,1... | collective-permute-start | bytes 49160 | tf_op jit(solution)/shard_map/ppermute | solution.py:512
  113.2 7.3 %collective-permute-start.27 = (bf16[8,64,128]{2,1,0:T(8,128)(2,1)S(1)}, bf16[8,64,128]{2,1,0:T(8,128)(2,1)S(1)}, u32[]{:S(2)}, u32[]{:S(2)}) collective-permute-start(bf16[8,64,128]{2,1,0:T(8,128)(2,1)S(1)} %constant_dynamic-update-slice_fusion.4), channel_id=1, source_target_pairs={{0,8},{1,3},{2,10},{3,5},{4,12},{5,7},{6,14},{7,1},{8,16},{9,11},{... | collective-permute-start | bytes 393224 | tf_op jit(solution)/shard_map/ppermute | solution.py:442
  113.3 7.2 %collective-permute-start.28 = (bf16[8,64,128]{2,1,0:T(8,128)(2,1)S(1)}, bf16[8,64,128]{2,1,0:T(8,128)(2,1)S(1)}, u32[]{:S(2)}, u32[]{:S(2)}) collective-permute-start(bf16[8,64,128]{2,1,0:T(8,128)(2,1)S(1)} %constant_dynamic-update-slice_fusion.4), channel_id=1, source_target_pairs={{0,16},{1,5},{2,18},{3,7},{4,20},{5,1},{6,22},{7,3},{8,24},{9,13},... | collective-permute-start | bytes 393224 | tf_op jit(solution)/shard_map/ppermute | solution.py:442
  115.3 5.3 %collective-permute-start.29 = (bf16[8,64,128]{2,1,0:T(8,128)(2,1)S(1)}, bf16[8,64,128]{2,1,0:T(8,128)(2,1)S(1)}, u32[]{:S(2)}, u32[]{:S(2)}) collective-permute-start(bf16[8,64,128]{2,1,0:T(8,128)(2,1)S(1)} %constant_dynamic-update-slice_fusion.4), channel_id=1, source_target_pairs={{0,24},{1,7},{2,26},{3,1},{4,28},{5,3},{6,30},{7,5},{8,0},{9,15},{... | collective-permute-start | bytes 393224 | tf_op jit(solution)/shard_map/ppermute | solution.py:442
  116.0 36.9 %all-to-all-start.3 = ((f32[8,192,128]{2,1,0:T(8,128)}), f32[8,192,128]{2,1,0:T(8,128)}, u32[]{:S(2)}, u32[]{:S(2)}) async-start(f32[8,192,128]{2,1,0:T(8,128)} %get-tuple-element.79), calls=%async_computation.3 | async-start | bytes 1572864 | tf_op jit(solution)/shard_map/all_to_all | solution.py:525
  120.6 15.3 %collective-permute-start.30 = (bf16[32,64,128]{2,1,0:T(8,128)(2,1)S(1)}, bf16[32,64,128]{2,1,0:T(8,128)(2,1)S(1)}, u32[]{:S(2)}, u32[]{:S(2)}) collective-permute-start(bf16[32,64,128]{2,1,0:T(8,128)(2,1)S(1)} %constant_dynamic-update-slice_fusion.12.rest_0_), channel_id=1, source_target_pairs={{0,2},{1,9},{2,4},{3,11},{4,6},{5,13},{6,0},{7,15},{8,10},{9,17},{... | collective-permute-start | bytes 1572872 | tf_op jit(solution)/shard_map/ppermute | solution.py:442
  121.0 15.0 %collective-permute-start.31 = (bf16[32,64,128]{2,1,0:T(8,128)(2,1)S(1)}, bf16[32,64,128]{2,1,0:T(8,128)(2,1)S(1)}, u32[]{:S(2)}, u32[]{:S(2)}) collective-permute-start(bf16[32,64,128]{2,1,0:T(8,128)(2,1)S(1)} %constant_dynamic-update-slice_fusion.12.rest_0_), channel_id=1, source_target_pairs={{0,4},{1,17},{2,6},{3,19},{4,0},{5,21},{6,2},{7,23},{8,12},{9,25},... | collective-permute-start | bytes 1572872 | tf_op jit(solution)/shard_map/ppermute | solution.py:442
  122.7 13.9 %collective-permute-start.32 = (bf16[32,64,128]{2,1,0:T(8,128)(2,1)S(1)}, bf16[32,64,128]{2,1,0:T(8,128)(2,1)S(1)}, u32[]{:S(2)}, u32[]{:S(2)}) collective-permute-start(bf16[32,64,128]{2,1,0:T(8,128)(2,1)S(1)} %constant_dynamic-update-slice_fusion.12.rest_0_), channel_id=1, source_target_pairs={{0,6},{1,25},{2,0},{3,27},{4,2},{5,29},{6,4},{7,31},{8,14},{9,1},{... | collective-permute-start | bytes 1572872 | tf_op jit(solution)/shard_map/ppermute | solution.py:442
  136.6 8.4 %collective-permute-start.33 = (bf16[32,64,128]{2,1,0:T(8,128)(2,1)S(1)}, bf16[32,64,128]{2,1,0:T(8,128)(2,1)S(1)}, u32[]{:S(2)}, u32[]{:S(2)}) collective-permute-start(bf16[32,64,128]{2,1,0:T(8,128)(2,1)S(1)} %constant_dynamic-update-slice_fusion.12.rest_0_), channel_id=1, source_target_pairs={{0,1},{1,0},{2,3},{3,2},{4,5},{5,4},{6,7},{7,6},{8,9},{9,8},{10,11... | collective-permute-start | bytes 1572872 | tf_op jit(solution)/shard_map/ppermute | solution.py:447
  142.5 3.0 %collective-permute-start.34 = (bf16[32,64,128]{2,1,0:T(8,128)(2,1)S(1)}, bf16[32,64,128]{2,1,0:T(8,128)(2,1)S(1)}, u32[]{:S(2)}, u32[]{:S(2)}) collective-permute-start(bf16[32,64,128]{2,1,0:T(8,128)(2,1)S(1)} %collective-permute-done.30.rest_1_), channel_id=1, source_target_pairs={{0,1},{1,0},{2,3},{3,2},{4,5},{5,4},{6,7},{7,6},{8,9},{9,8},{10,11... | collective-permute-start | bytes 1572872 | tf_op jit(solution)/shard_map/ppermute | solution.py:447
  142.5 3.2 %collective-permute-start.35 = (bf16[32,64,128]{2,1,0:T(8,128)(2,1)S(1)}, bf16[32,64,128]{2,1,0:T(8,128)(2,1)}, u32[]{:S(2)}, u32[]{:S(2)}) collective-permute-start(bf16[32,64,128]{2,1,0:T(8,128)(2,1)S(1)} %collective-permute-done.31.rest_2_), channel_id=1, source_target_pairs={{0,1},{1,0},{2,3},{3,2},{4,5},{5,4},{6,7},{7,6},{8,9},{9,8},{10,11... | collective-permute-start | bytes 1572872 | tf_op jit(solution)/shard_map/ppermute | solution.py:447
  143.0 3.4 %collective-permute-start.36 = (bf16[32,64,128]{2,1,0:T(8,128)(2,1)S(1)}, bf16[32,64,128]{2,1,0:T(8,128)(2,1)}, u32[]{:S(2)}, u32[]{:S(2)}) collective-permute-start(bf16[32,64,128]{2,1,0:T(8,128)(2,1)S(1)} %collective-permute-done.32.rest_3_), channel_id=1, source_target_pairs={{0,1},{1,0},{2,3},{3,2},{4,5},{5,4},{6,7},{7,6},{8,9},{9,8},{10,11... | collective-permute-start | bytes 1572872 | tf_op jit(solution)/shard_map/ppermute | solution.py:447
  (5 other events, 115.6 us)

commit v3 on v2

--- a/solution.py
+++ b/solution.py
@@ -29,6 +29,7 @@
 SM = pl.BlockSpec(memory_space=pltpu.SMEM)
 ANY = pl.BlockSpec(memory_space=pl.ANY)
 GROUP = 8
+LATER = 4
 WEIGHTS_MIB = 60
 RENDER_MIB = 34
 SECOND_MIB = 48
@@ -395,7 +396,8 @@
     )(slots, loads, w, *blocks)
 
 
-def adam_kernel(owner, me, gradient, feat, m1, m2, close, away, packed, colors):
+def adam_kernel(owner, me, gradient, feat, m1, m2, *rest):
+    outs, packed, colors = rest[:N_VIEW], rest[N_VIEW], rest[N_VIEW + 1]
     g = reorder_wide(gradient[...].reshape(BINS * C, GB), True).reshape(BINS, C, GB)
     first_new = beta_first * m1[...] + (1.0 - beta_first) * g
     second_new = beta_second * m2[...] + (1.0 - beta_second) * g * g
@@ -408,20 +410,19 @@
         packed[w, 0:C] = stepped[s]
         packed[w, C : 2 * C] = first_new[s]
         packed[w, 2 * C : 3 * C] = second_new[s]
-    close[...] = colors[0:4]
-    away[...] = colors[4:]
+    for r, out in enumerate(outs):
+        out[...] = colors[r : r + 1]
 
 
 def adam(owner, me, gradient, feat, m1, m2):
     return pl.pallas_call(
         adam_kernel,
         out_shape=(
-            jax.ShapeDtypeStruct((N_VIEW // 2, C, GB), bf16),
-            jax.ShapeDtypeStruct((N_VIEW // 2, C, GB), bf16),
+            *(jax.ShapeDtypeStruct((1, C, GB), bf16),) * N_VIEW,
             jax.ShapeDtypeStruct((N_VIEW, 3 * C, GB), f32),
         ),
         in_specs=[SM, SM, VM, VM, VM, VM],
-        out_specs=(VM, VM, VM),
+        out_specs=(VM,) * (N_VIEW + 1),
         scratch_shapes=[pltpu.VMEM((N_VIEW, C, GB), bf16)],
         compiler_params=params(16),
         name="adam",
@@ -507,14 +508,14 @@
     return (((core ^ c) * 4 + far) * 4 + near) * BINS + within
 
 
-def exchange_views(close, away, later):
-    def step(value, r):
-        return lax.ppermute(value, "view", [(v, v ^ r) for v in range(N_VIEW)])
-
-    got = {r: step(away[r - 4 : r - 3], r) for r in (4, 5, 6, 7)}
-    close, later = tie(close, later)
-    got.update({r: step(close[r : r + 1], r) for r in (3, 2, 1)})
-    return jnp.concatenate([close[0:1]] + [got[r] for r in range(1, N_VIEW)], axis=0), later
+def exchange_views(colors, later):
+    got = {0: colors[0]}
+    for i, r in enumerate((4, 5, 3, 6, 2, 7, 1)):
+        value = colors[r]
+        if i == LATER:
+            value, later = tie(value, later)
+        got[r] = lax.ppermute(value, "view", [(v, v ^ r) for v in range(N_VIEW)])
+    return jnp.concatenate([got[r] for r in range(N_VIEW)], axis=0), later
 
 
 def place_of(view):
@@ -561,8 +562,8 @@
     screen = across_tile(screen)
     gradient = scatter_near(line)
     me = lax.axis_index("view").reshape(1)
-    close, away, packed = adam(owner_after, me, gradient, features, moment_first, moment_second)
-    colors, screen = exchange_views(close, away, screen)
+    *colors, packed = adam(owner_after, me, gradient, features, moment_first, moment_second)
+    colors, screen = exchange_views(colors, screen)
     colors, packed = tie(colors, packed)
     w_second, token = weights(lists_second[0], loads_second[0], shift_second[0], screen, "weights_second")
     packed = across_view(packed)

time: 156 us -> 151 us (0.968); the launches traced: 155 us -> 152 us
  waiting for transfers between devices: 25.9 us -> 14.4 us
  starting transfers between devices: 58.5 us -> 66.8 us
    all_to_all x2, waiting for transfers between devices: 11.2 us -> 4.36 us  [across_tile(): lax.all_to_all(value, 'tile', split_axis=0, concat_axis=0, tiled=True)]
    ppermute x18, starting transfers between devices: 19.4 us -> 24.4 us  [shift_by(): return lax.ppermute(value, 'tile', pairs)]
    ppermute x18, waiting for transfers between devices: 3.33 us -> 1.19 us  [shift_by(): return lax.ppermute(value, 'tile', pairs)]
    all_to_all x2, starting transfers between devices: 14.8 us -> 16.4 us  [across_tile(): lax.all_to_all(value, 'tile', split_axis=0, concat_axis=0, tiled=True)]
    all_to_all x1, starting transfers between devices: 4.44 us -> 6.02 us  [across_view(): lax.all_to_all(value, 'view', split_axis=0, concat_axis=0, tiled=True)]
  transfers between devices with their start and end apart: 40 -> 40, of which waited for: 14 -> 11; matrix products, arithmetic and copies ran while one was open for 4% -> 4% of each run, Pallas kernels for 20% -> 21%
where the time goes in v3:
time: 151 us; the launch traced here: 152 us
  starting transfers between devices  66.8 us (44%)
  Pallas kernels  43.1 us (29%)
  blocking collectives  17.9 us (12%)
  waiting for transfers between devices  14.4 us (10%)
  local copies, waits for them, and re-layouts  6.01 us (4%)
  other arithmetic  2.58 us (2%)
    ppermute x18, starting transfers between devices, shift_by(): return lax.ppermute(value, 'tile', pairs)  24.4 us
    pallas_call x2, Pallas kernels, weights(): pl.pallas_call(weights_kernel, out_shape=(jax.ShapeDtypeStruct((TILES, LB...  21.3 us
    all_to_all x1, blocking collectives, across_view(): lax.all_to_all(value, 'view', split_axis=0, concat_axis=0, tiled=True)  17.9 us
    all_to_all x2, starting transfers between devices, across_tile(): lax.all_to_all(value, 'tile', split_axis=0, concat_axis=0, tiled=True)  16.4 us
    ppermute x7, starting transfers between devices, exchange_views(): got[r] = lax.ppermute(value, 'view', [(v, v ^ r) for v in range(N_VIEW)])  10.7 us
    pallas_call x1, Pallas kernels, first_render(): pl.pallas_call(first_kernel, out_shape=(jax.ShapeDtypeStruct((32, C, GB),...  9.86 us
    ppermute x12, starting transfers between devices, swap_core(): return lax.ppermute(value, 'tile', pairs)  9.13 us
    pallas_call x1, Pallas kernels, second_render(): pl.pallas_call(second_kernel, out_shape=jax.ShapeDtypeStruct((TILES, C, P...  6.55 us
  transfers between devices with their start and end apart: 40, of which 11 were waited for; matrix products, arithmetic and copies ran while one was open for 4% of the time, Pallas kernels for 21%

profile of v3, /device:TPU:1, one launch (start us, length us, event | category | flops | bytes accessed | tf_op | source)
XLA Modules:
  0.0 151.8 jit_solution(7489654370432670760)
XLA Ops:
  0.7 2.0 %prep.1 = (bf16[8,64,128]{2,1,0:T(8,128)(2,1)}, bf16[32,32,128]{2,1,0:T(8,128)(2,1)}, f32[8,8,128]{2,1,0:T(8,128)}) custom-call(f32[1,2,4]{2,1,0:T(2,128)} %camera_hbm.1, s32[8]{0:T(128)} %owner.1, f32[8,64,128]{2,1,0:T(8,128)} %feat.1, f32[3,8,128]{2,1,0:T(8,128)} %bitcast.28, f32[8,128]{1,0:T(8,128)} %scales_hbm.1, f32[8,128]{1,0:T(8,128)} %opacity_hbm.1), custom_call_target="tpu_custom_call" | custom-call | tf_op jit(solution)/shard_map/prep/pallas_call | solution.py:118
  2.7 2.2 %collective-permute-start = (bf16[8,64,128]{2,1,0:T(8,128)(2,1)}, bf16[8,64,128]{2,1,0:T(8,128)(2,1)S(1)}, u32[]{:S(2)}, u32[]{:S(2)}) collective-permute-start(bf16[8,64,128]{2,1,0:T(8,128)(2,1)} %get-tuple-element.48), channel_id=1, source_target_pairs={{0,8},{1,3},{2,10},{3,5},{4,12},{5,7},{6,14},{7,1},{8,16},{9,11},{... | collective-permute-start | bytes 393224 | tf_op jit(solution)/shard_map/ppermute | solution.py:443
  4.9 2.6 %collective-permute-start.1 = (bf16[8,64,128]{2,1,0:T(8,128)(2,1)}, bf16[8,64,128]{2,1,0:T(8,128)(2,1)S(1)}, u32[]{:S(2)}, u32[]{:S(2)}) collective-permute-start(bf16[8,64,128]{2,1,0:T(8,128)(2,1)} %get-tuple-element.48), channel_id=1, source_target_pairs={{0,16},{1,5},{2,18},{3,7},{4,20},{5,1},{6,22},{7,3},{8,24},{9,13},... | collective-permute-start | bytes 393224 | tf_op jit(solution)/shard_map/ppermute | solution.py:443
  7.5 1.1 collective-permute-start.2
  8.6 6.0 %all-to-all-start = ((bf16[32,32,128]{2,1,0:T(8,128)(2,1)}), bf16[32,32,128]{2,1,0:T(8,128)(2,1)S(1)}, u32[]{:S(2)}, u32[]{:S(2)}) async-start(bf16[32,32,128]{2,1,0:T(8,128)(2,1)} %get-tuple-element.49), calls=%async_computation | async-start | bytes 524288 | tf_op jit(solution)/shard_map/all_to_all | solution.py:530
  14.6 0.9 constant_dynamic-update-slice_fusion.3
  15.6 1.5 collective-permute-start.3
  17.1 2.4 %collective-permute-start.4 = (bf16[32,64,128]{2,1,0:T(8,128)(2,1)S(1)}, bf16[32,64,128]{2,1,0:T(8,128)(2,1)S(1)}, u32[]{:S(2)}, u32[]{:S(2)}) collective-permute-start(bf16[32,64,128]{2,1,0:T(8,128)(2,1)S(1)} %constant_dynamic-update-slice_fusion.rest_0_), channel_id=1, source_target_pairs={{0,4},{1,17},{2,6},{3,19},{4,0},{5,21},{6,2},{7,23},{8,12},{9,25},... | collective-permute-start | bytes 1572872 | tf_op jit(solution)/shard_map/ppermute | solution.py:443
  19.5 4.4 %all-to-all-done.screen_hbm = bf16[32,32,128]{2,1,0:T(8,128)(2,1)S(1)} async-done(((bf16[32,32,128]{2,1,0:T(8,128)(2,1)}), bf16[32,32,128]{2,1,0:T(8,128)(2,1)S(1)}, u32[]{:S(2)}, u32[]{:S(2)}) %all-to-all-start) | async-done | bytes 262176 | tf_op jit(solution)/shard_map/all_to_all | solution.py:530
  24.6 11.0 %weights_first.1 = (bf16[16,8,128,256]{3,2,1,0:T(8,128)(2,1)}, s32[8,128]{1,0:T(8,128)}) custom-call(s32[8,16]{1,0:T(8,128)} %bitcast.29, s32[16]{0:T(128)} %bitcast.23, f32[2,16]{1,0:T(2,128)} %bitcast.33, bf16[32,32,128]{2,1,0:T(8,128)(2,1)} %copy-done.9), custom_call_target="tpu_custom_call" | custom-call | flops 58720256 | bytes 10000000 | tf_op jit(solution)/shard_map/weights_first/pallas_call | solution.py:258
  35.6 0.9 collective-permute-start.6
  37.2 1.2 slice.30
  38.4 0.7 fusion.16.slots
  39.1 0.6 collective-permute-done.8.rest_6_
  39.7 0.7 collective-permute-done.9.rest_7_
  40.4 9.9 %first_render.1 = (f32[32,64,128]{2,1,0:T(8,128)S(1)}, f32[32,64,128]{2,1,0:T(8,128)S(1)}, f32[32,64,128]{2,1,0:T(8,128)S(1)}, f32[32,64,128]{2,1,0:T(8,128)S(1)...) custom-call(s32[16,8]{1,0:T(8,128)S(1)} %fusion.16.slots, ...), custom_call_target="tpu_custom_call" | custom-call | flops 1073741824 | bytes 25000000 | tf_op jit(solution)/shard_map/first_render/pallas_call | solution.py:348
  50.4 0.6 collective-permute-start.11
  51.6 1.7 %collective-permute-done.11 = f32[32,64,128]{2,1,0:T(8,128)S(1)} collective-permute-done((f32[32,64,128]{2,1,0:T(8,128)S(1)}, f32[32,64,128]{2,1,0:T(8,128)S(1)}, u32[]{:S(2)}, u32[]{:S(2)}) %collective-permute-start.11) | collective-permute-done | bytes 1048608 | tf_op jit(solution)/shard_map/ppermute | solution.py:448
  53.5 0.9 collective-permute-start.12
  55.0 1.5 collective-permute-start.14
  56.8 17.9 %all_to_all.20.geometry = f32[8,8,128]{2,1,0:T(8,128)S(1)} all-to-all(f32[8,8,128]{2,1,0:T(8,128)S(1)} %copy-done.10), channel_id=1, replica_groups=mesh['view'=8,'tile'=32] {'view'}, dimensions={0} | all-to-all | bytes 65536 | tf_op jit(solution)/shard_map/all_to_all | solution.py:526
  74.7 1.4 screen_again.1
  77.3 1.1 collective-permute-start.19
  78.5 10.4 %all-to-all-start.2 = ((bf16[32,32,128]{2,1,0:T(8,128)(2,1)}), bf16[32,32,128]{2,1,0:T(8,128)(2,1)S(1)}, u32[]{:S(2)}, u32[]{:S(2)}) async-start(bf16[32,32,128]{2,1,0:T(8,128)(2,1)} %screen_again.1), calls=%async_computation.2 | async-start | bytes 524288 | tf_op jit(solution)/shard_map/all_to_all | solution.py:530
  89.1 1.9 %adam.1 = (bf16[1,64,128]{2,1,0:T(8,128)(2,1)S(1)}, bf16[1,64,128]{2,1,0:T(8,128)(2,1)S(1)}, bf16[1,64,128]{2,1,0:T(8,128)(2,1)S(1)}, bf16[1,64,128]{2,1,0:T(8,1...) custom-call(s32[8]{0:T(128)S(1)} %copy-done.4, ...), custom_call_target="tpu_custom_call" | custom-call | tf_op jit(solution)/shard_map/adam/pallas_call | solution.py:418
  91.3 1.0 collective-permute-start.22
  92.3 2.2 %collective-permute-start.23 = (bf16[1,64,128]{2,1,0:T(8,128)(2,1)S(1)}, bf16[1,64,128]{2,1,0:T(8,128)(2,1)S(1)}, u32[]{:S(2)}, u32[]{:S(2)}) collective-permute-start(bf16[1,64,128]{2,1,0:T(8,128)(2,1)S(1)} %get-tuple-element.77), channel_id=1, source_target_pairs={{0,128},{32,160},{64,192},{96,224},{128,0},{160,32},{192,64},{224,... | collective-permute-start | bytes 49160 | tf_op jit(solution)/shard_map/ppermute | solution.py:517
  94.5 2.1 %collective-permute-start.24 = (bf16[1,64,128]{2,1,0:T(8,128)(2,1)S(1)}, bf16[1,64,128]{2,1,0:T(8,128)(2,1)S(1)}, u32[]{:S(2)}, u32[]{:S(2)}) collective-permute-start(bf16[1,64,128]{2,1,0:T(8,128)(2,1)S(1)} %get-tuple-element.78), channel_id=1, source_target_pairs={{0,160},{32,128},{64,224},{96,192},{128,32},{160,0},{192,96},{224,... | collective-permute-start | bytes 49160 | tf_op jit(solution)/shard_map/ppermute | solution.py:517
  96.7 1.4 collective-permute-start.25
  98.1 1.2 collective-permute-start.21
  99.2 2.7 %collective-permute-done.21 = bf16[1,64,128]{2,1,0:T(8,128)(2,1)S(1)} collective-permute-done((bf16[1,64,128]{2,1,0:T(8,128)(2,1)S(1)}, bf16[1,64,128]{2,1,0:T(8,128)(2,1)S(1)}, u32[]{:S(2)}, u32[]{:S(2)}) %collective-permute-start.21) | collective-permute-done | bytes 16416 | tf_op jit(solution)/shard_map/ppermute | solution.py:517
  102.0 2.5 %collective-permute-start.26 = (bf16[1,64,128]{2,1,0:T(8,128)(2,1)S(1)}, bf16[1,64,128]{2,1,0:T(8,128)(2,1)S(1)}, u32[]{:S(2)}, u32[]{:S(2)}) collective-permute-start(bf16[1,64,128]{2,1,0:T(8,128)(2,1)S(1)} %get-tuple-element.80), channel_id=1, source_target_pairs={{0,224},{32,192},{64,160},{96,128},{128,96},{160,64},{192,32},{224... | collective-permute-start | bytes 49160 | tf_op jit(solution)/shard_map/ppermute | solution.py:517
  104.6 1.2 collective-permute-done.26
  105.8 1.5 collective-permute-start.27
  107.3 2.4 %collective-permute-start.28 = (bf16[8,64,128]{2,1,0:T(8,128)(2,1)S(1)}, bf16[8,64,128]{2,1,0:T(8,128)(2,1)S(1)}, u32[]{:S(2)}, u32[]{:S(2)}) collective-permute-start(bf16[8,64,128]{2,1,0:T(8,128)(2,1)S(1)} %constant_dynamic-update-slice_fusion.4), channel_id=1, source_target_pairs={{0,16},{1,5},{2,18},{3,7},{4,20},{5,1},{6,22},{7,3},{8,24},{9,13},... | collective-permute-start | bytes 393224 | tf_op jit(solution)/shard_map/ppermute | solution.py:443
  109.7 1.3 collective-permute-start.29
  110.9 6.0 %all-to-all-start.3 = ((f32[8,192,128]{2,1,0:T(8,128)}), f32[8,192,128]{2,1,0:T(8,128)}, u32[]{:S(2)}, u32[]{:S(2)}) async-start(f32[8,192,128]{2,1,0:T(8,128)} %get-tuple-element.91), calls=%async_computation.3 | async-start | bytes 1572864 | tf_op jit(solution)/shard_map/all_to_all | solution.py:526
  117.1 1.3 collective-permute-start.30
  118.3 2.5 %collective-permute-start.31 = (bf16[32,64,128]{2,1,0:T(8,128)(2,1)S(1)}, bf16[32,64,128]{2,1,0:T(8,128)(2,1)S(1)}, u32[]{:S(2)}, u32[]{:S(2)}) collective-permute-start(bf16[32,64,128]{2,1,0:T(8,128)(2,1)S(1)} %constant_dynamic-update-slice_fusion.12.rest_0_), channel_id=1, source_target_pairs={{0,4},{1,17},{2,6},{3,19},{4,0},{5,21},{6,2},{7,23},{8,12},{9,25},... | collective-permute-start | bytes 1572872 | tf_op jit(solution)/shard_map/ppermute | solution.py:443
  120.8 1.1 collective-permute-start.32
  121.9 10.3 %weights_second.1 = (bf16[16,8,128,256]{3,2,1,0:T(8,128)(2,1)}, s32[8,128]{1,0:T(8,128)}) custom-call(s32[8,16]{1,0:T(8,128)} %bitcast.31, s32[16]{0:T(128)} %bitcast.25, f32[2,16]{1,0:T(2,128)} %bitcast.34, bf16[32,32,128]{2,1,0:T(8,128)(2,1)} %copy-done.8), custom_call_target="tpu_custom_call" | custom-call | flops 58720256 | bytes 10000000 | tf_op jit(solution)/shard_map/weights_second/pallas_call | solution.py:258
  132.2 1.1 collective-permute-done.31.rest_2_
  133.4 5.9 %collective-permute-start.33 = (bf16[32,64,128]{2,1,0:T(8,128)(2,1)S(1)}, bf16[32,64,128]{2,1,0:T(8,128)(2,1)S(1)}, u32[]{:S(2)}, u32[]{:S(2)}) collective-permute-start(bf16[32,64,128]{2,1,0:T(8,128)(2,1)S(1)} %constant_dynamic-update-slice_fusion.12.rest_0_), channel_id=1, source_target_pairs={{0,1},{1,0},{2,3},{3,2},{4,5},{5,4},{6,7},{7,6},{8,9},{9,8},{10,11... | collective-permute-start | bytes 1572872 | tf_op jit(solution)/shard_map/ppermute | solution.py:448
  139.9 1.2 slice.35
  141.1 0.7 fusion.8.slots
  142.4 0.8 collective-permute-done.36.rest_7_
  143.2 6.6 %second_render.1 = f32[16,64,256]{2,1,0:T(8,128)} custom-call(s32[16,8]{1,0:T(8,128)S(1)} %fusion.8.slots, s32[16]{0:T(128)S(1)} %bitcast.26, bf16[16,8,128,256]{3,2,1,0:T(8,128)(2,1)} %get-tuple-element.86.w_hbm, bf16[32,64,128]{2,1,0:T(8,128)(2,1)S(1)} %constant_dynamic-update-slice_fusion.12.rest_0_, ...), custom_call_target="tpu_custom_call" | custom-call | flops 536870912 | bytes 14000000 | tf_op jit(solution)/shard_map/second_render/pallas_call | solution.py:382
  149.8 2.0 %fusion.23 = (f32[8,64,128]{2,1,0:T(8,128)}, f32[8,64,128]{2,1,0:T(8,128)}, f32[8,64,128]{2,1,0:T(8,128)}) fusion(f32[8,192,128]{2,1,0:T(8,128)} %all-to-all-done.3), kind=kLoop, calls=%fused_computation.92 | loop fusion | bytes 1572864 | tf_op jit(solution)/shard_map/slice | solution.py:574
  (96 shorter events, 6.3 us)
Async XLA Ops:
  0.6 39.8 %copy-start.6 = (s32[1,16]{1,0:T(1,128)S(1)}, s32[1,16]{1,0:T(1,128)}, u32[]{:S(2)}) copy-start(s32[1,16]{1,0:T(1,128)} %param.25) | copy-start | bytes 196
  0.7 39.8 %copy-start.1 = (bf16[1,16,64,256]{3,2,1,0:T(8,128)(2,1)S(1)}, bf16[1,16,64,256]{3,2,1,0:T(8,128)(2,1)}, u32[]{:S(2)}) copy-start(bf16[1,16,64,256]{3,2,1,0:T(8,128)(2,1)} %param.26) | copy-start | bytes 1572868
  2.7 12.8 %collective-permute-start = (bf16[8,64,128]{2,1,0:T(8,128)(2,1)}, bf16[8,64,128]{2,1,0:T(8,128)(2,1)S(1)}, u32[]{:S(2)}, u32[]{:S(2)}) collective-permute-start(bf16[8,64,128]{2,1,0:T(8,128)(2,1)} %get-tuple-element.48), channel_id=1, source_target_pairs={{0,8},{1,3},{2,10},{3,5},{4,12},{5,7},{6,14},{7,1},{8,16},{9,11},{... | collective-permute-start | bytes 393224 | tf_op jit(solution)/shard_map/ppermute | solution.py:443
  4.9 10.7 %collective-permute-start.1 = (bf16[8,64,128]{2,1,0:T(8,128)(2,1)}, bf16[8,64,128]{2,1,0:T(8,128)(2,1)S(1)}, u32[]{:S(2)}, u32[]{:S(2)}) collective-permute-start(bf16[8,64,128]{2,1,0:T(8,128)(2,1)} %get-tuple-element.48), channel_id=1, source_target_pairs={{0,16},{1,5},{2,18},{3,7},{4,20},{5,1},{6,22},{7,3},{8,24},{9,13},... | collective-permute-start | bytes 393224 | tf_op jit(solution)/shard_map/ppermute | solution.py:443
  7.5 8.1 %collective-permute-start.2 = (bf16[8,64,128]{2,1,0:T(8,128)(2,1)}, bf16[8,64,128]{2,1,0:T(8,128)(2,1)S(1)}, u32[]{:S(2)}, u32[]{:S(2)}) collective-permute-start(bf16[8,64,128]{2,1,0:T(8,128)(2,1)} %get-tuple-element.48), channel_id=1, source_target_pairs={{0,24},{1,7},{2,26},{3,1},{4,28},{5,3},{6,30},{7,5},{8,0},{9,15},{... | collective-permute-start | bytes 393224 | tf_op jit(solution)/shard_map/ppermute | solution.py:443
  8.6 15.3 %all-to-all-start = ((bf16[32,32,128]{2,1,0:T(8,128)(2,1)}), bf16[32,32,128]{2,1,0:T(8,128)(2,1)S(1)}, u32[]{:S(2)}, u32[]{:S(2)}) async-start(bf16[32,32,128]{2,1,0:T(8,128)(2,1)} %get-tuple-element.49), calls=%async_computation | async-start | bytes 524288 | tf_op jit(solution)/shard_map/all_to_all | solution.py:530
  15.6 20.0 %collective-permute-start.3 = (bf16[32,64,128]{2,1,0:T(8,128)(2,1)S(1)}, bf16[32,64,128]{2,1,0:T(8,128)(2,1)S(1)}, u32[]{:S(2)}, u32[]{:S(2)}) collective-permute-start(bf16[32,64,128]{2,1,0:T(8,128)(2,1)S(1)} %constant_dynamic-update-slice_fusion.rest_0_), channel_id=1, source_target_pairs={{0,2},{1,9},{2,4},{3,11},{4,6},{5,13},{6,0},{7,15},{8,10},{9,17},{... | collective-permute-start | bytes 1572872 | tf_op jit(solution)/shard_map/ppermute | solution.py:443
  17.1 18.5 %collective-permute-start.4 = (bf16[32,64,128]{2,1,0:T(8,128)(2,1)S(1)}, bf16[32,64,128]{2,1,0:T(8,128)(2,1)S(1)}, u32[]{:S(2)}, u32[]{:S(2)}) collective-permute-start(bf16[32,64,128]{2,1,0:T(8,128)(2,1)S(1)} %constant_dynamic-update-slice_fusion.rest_0_), channel_id=1, source_target_pairs={{0,4},{1,17},{2,6},{3,19},{4,0},{5,21},{6,2},{7,23},{8,12},{9,25},... | collective-permute-start | bytes 1572872 | tf_op jit(solution)/shard_map/ppermute | solution.py:443
  23.9 11.7 %collective-permute-start.5 = (bf16[32,64,128]{2,1,0:T(8,128)(2,1)S(1)}, bf16[32,64,128]{2,1,0:T(8,128)(2,1)S(1)}, u32[]{:S(2)}, u32[]{:S(2)}) collective-permute-start(bf16[32,64,128]{2,1,0:T(8,128)(2,1)S(1)} %constant_dynamic-update-slice_fusion.rest_0_), channel_id=1, source_target_pairs={{0,6},{1,25},{2,0},{3,27},{4,2},{5,29},{6,4},{7,31},{8,14},{9,1},{... | collective-permute-start | bytes 1572872 | tf_op jit(solution)/shard_map/ppermute | solution.py:443
  35.6 3.5 %collective-permute-start.6 = (bf16[32,64,128]{2,1,0:T(8,128)(2,1)S(1)}, bf16[32,64,128]{2,1,0:T(8,128)(2,1)S(1)}, u32[]{:S(2)}, u32[]{:S(2)}) collective-permute-start(bf16[32,64,128]{2,1,0:T(8,128)(2,1)S(1)} %constant_dynamic-update-slice_fusion.rest_0_), channel_id=1, source_target_pairs={{0,1},{1,0},{2,3},{3,2},{4,5},{5,4},{6,7},{7,6},{8,9},{9,8},{10,11... | collective-permute-start | bytes 1572872 | tf_op jit(solution)/shard_map/ppermute | solution.py:448
  36.5 2.6 %collective-permute-start.7 = (bf16[32,64,128]{2,1,0:T(8,128)(2,1)S(1)}, bf16[32,64,128]{2,1,0:T(8,128)(2,1)}, u32[]{:S(2)}, u32[]{:S(2)}) collective-permute-start(bf16[32,64,128]{2,1,0:T(8,128)(2,1)S(1)} %collective-permute-done.3.rest_1_), channel_id=1, source_target_pairs={{0,1},{1,0},{2,3},{3,2},{4,5},{5,4},{6,7},{7,6},{8,9},{9,8},{10,11... | collective-permute-start | bytes 1572872 | tf_op jit(solution)/shard_map/ppermute | solution.py:448
  36.6 3.1 %collective-permute-start.8 = (bf16[32,64,128]{2,1,0:T(8,128)(2,1)S(1)}, bf16[32,64,128]{2,1,0:T(8,128)(2,1)}, u32[]{:S(2)}, u32[]{:S(2)}) collective-permute-start(bf16[32,64,128]{2,1,0:T(8,128)(2,1)S(1)} %collective-permute-done.4.rest_2_), channel_id=1, source_target_pairs={{0,1},{1,0},{2,3},{3,2},{4,5},{5,4},{6,7},{7,6},{8,9},{9,8},{10,11... | collective-permute-start | bytes 1572872 | tf_op jit(solution)/shard_map/ppermute | solution.py:448
  37.0 3.4 %collective-permute-start.9 = (bf16[32,64,128]{2,1,0:T(8,128)(2,1)S(1)}, bf16[32,64,128]{2,1,0:T(8,128)(2,1)}, u32[]{:S(2)}, u32[]{:S(2)}) collective-permute-start(bf16[32,64,128]{2,1,0:T(8,128)(2,1)S(1)} %collective-permute-done.5.rest_3_), channel_id=1, source_target_pairs={{0,1},{1,0},{2,3},{3,2},{4,5},{5,4},{6,7},{7,6},{8,9},{9,8},{10,11... | collective-permute-start | bytes 1572872 | tf_op jit(solution)/shard_map/ppermute | solution.py:448
  50.3 38.7 %copy-start = (f32[8,64,128]{2,1,0:T(8,128)S(1)}, f32[8,64,128]{2,1,0:T(8,128)}, u32[]{:S(2)}) copy-start(f32[8,64,128]{2,1,0:T(8,128)} %feat.1) | copy-start | bytes 786436
  50.3 38.7 %copy-start.2 = (f32[8,64,128]{2,1,0:T(8,128)S(1)}, f32[8,64,128]{2,1,0:T(8,128)}, u32[]{:S(2)}) copy-start(f32[8,64,128]{2,1,0:T(8,128)} %m1.1) | copy-start | bytes 786436
  50.3 38.7 %copy-start.3 = (f32[8,64,128]{2,1,0:T(8,128)S(1)}, f32[8,64,128]{2,1,0:T(8,128)}, u32[]{:S(2)}) copy-start(f32[8,64,128]{2,1,0:T(8,128)} %m2.1) | copy-start | bytes 786436
  50.3 38.7 %copy-start.4 = (s32[8]{0:T(128)S(1)}, s32[8]{0:T(128)}, u32[]{:S(2)}) copy-start(s32[8]{0:T(128)} %owner.1) | copy-start | bytes 100
  50.4 2.9 %collective-permute-start.11 = (f32[32,64,128]{2,1,0:T(8,128)S(1)}, f32[32,64,128]{2,1,0:T(8,128)S(1)}, u32[]{:S(2)}, u32[]{:S(2)}) collective-permute-start(f32[32,64,128]{2,1,0:T(8,128)S(1)} %get-tuple-element.62), channel_id=1, source_target_pairs={{0,1},{1,0},{2,3},{3,2},{4,5},{5,4},{6,7},{7,6},{8,9},{9,8},{10,11... | collective-permute-start | bytes 3145736 | tf_op jit(solution)/shard_map/ppermute | solution.py:448
  51.0 3.8 %collective-permute-start.13 = (f32[32,64,128]{2,1,0:T(8,128)S(1)}, f32[32,64,128]{2,1,0:T(8,128)S(1)}, u32[]{:S(2)}, u32[]{:S(2)}) collective-permute-start(f32[32,64,128]{2,1,0:T(8,128)S(1)} %get-tuple-element.64), channel_id=1, source_target_pairs={{0,1},{1,0},{2,3},{3,2},{4,5},{5,4},{6,7},{7,6},{8,9},{9,8},{10,11... | collective-permute-start | bytes 3145736 | tf_op jit(solution)/shard_map/ppermute | solution.py:448
  51.1 5.4 %collective-permute-start.15 = (f32[32,64,128]{2,1,0:T(8,128)S(1)}, f32[32,64,128]{2,1,0:T(8,128)S(1)}, u32[]{:S(2)}, u32[]{:S(2)}) collective-permute-start(f32[32,64,128]{2,1,0:T(8,128)S(1)} %get-tuple-element.66), channel_id=1, source_target_pairs={{0,1},{1,0},{2,3},{3,2},{4,5},{5,4},{6,7},{7,6},{8,9},{9,8},{10,11... | collective-permute-start | bytes 3145736 | tf_op jit(solution)/shard_map/ppermute | solution.py:448
  51.5 24.6 %collective-permute-start.10 = (f32[32,64,128]{2,1,0:T(8,128)S(1)}, f32[32,64,128]{2,1,0:T(8,128)S(1)}, u32[]{:S(2)}, u32[]{:S(2)}) collective-permute-start(f32[32,64,128]{2,1,0:T(8,128)S(1)} %get-tuple-element.60), channel_id=1, source_target_pairs={{0,1},{1,0},{2,3},{3,2},{4,5},{5,4},{6,7},{7,6},{8,9},{9,8},{10,11... | collective-permute-start | bytes 3145736 | tf_op jit(solution)/shard_map/ppermute | solution.py:448
  53.5 22.7 %collective-permute-start.12 = (f16[32,64,128]{2,1,0:T(8,128)(2,1)S(1)}, f16[32,64,128]{2,1,0:T(8,128)(2,1)S(1)}, u32[]{:S(2)}, u32[]{:S(2)}) collective-permute-start(f16[32,64,128]{2,1,0:T(8,128)(2,1)S(1)} %add_convert_fusion.2), channel_id=1, source_target_pairs={{0,4},{1,17},{2,6},{3,19},{4,0},{5,21},{6,2},{7,23},{8,12},{9,25},... | collective-permute-start | bytes 1572872 | tf_op jit(solution)/shard_map/ppermute | solution.py:443
  55.0 21.1 %collective-permute-start.14 = (f16[32,64,128]{2,1,0:T(8,128)(2,1)S(1)}, f16[32,64,128]{2,1,0:T(8,128)(2,1)S(1)}, u32[]{:S(2)}, u32[]{:S(2)}) collective-permute-start(f16[32,64,128]{2,1,0:T(8,128)(2,1)S(1)} %add_convert_fusion.1), channel_id=1, source_target_pairs={{0,6},{1,25},{2,0},{3,27},{4,2},{5,29},{6,4},{7,31},{8,14},{9,1},{... | collective-permute-start | bytes 1572872 | tf_op jit(solution)/shard_map/ppermute | solution.py:443
  56.7 19.5 %collective-permute-start.16 = (f16[32,64,128]{2,1,0:T(8,128)(2,1)S(1)}, f16[32,64,128]{2,1,0:T(8,128)(2,1)S(1)}, u32[]{:S(2)}, u32[]{:S(2)}) collective-permute-start(f16[32,64,128]{2,1,0:T(8,128)(2,1)S(1)} %add_convert_fusion), channel_id=1, source_target_pairs={{0,2},{1,9},{2,4},{3,11},{4,6},{5,13},{6,0},{7,15},{8,10},{9,17},{... | collective-permute-start | bytes 1572872 | tf_op jit(solution)/shard_map/ppermute | solution.py:443
  76.6 63.2 %copy-start.12 = (s32[1,16,8]{1,2,0:T(8,128)S(1)}, s32[1,16,8]{1,2,0:T(8,128)}, u32[]{:S(2)}) copy-start(s32[1,16,8]{1,2,0:T(8,128)} %param.30) | copy-start | bytes 1540
  76.6 66.6 %copy-start.7 = (s32[1,16]{1,0:T(1,128)S(1)}, s32[1,16]{1,0:T(1,128)}, u32[]{:S(2)}) copy-start(s32[1,16]{1,0:T(1,128)} %param.31) | copy-start | bytes 196
  76.8 12.1 %collective-permute-start.17 = (f16[8,64,128]{2,1,0:T(8,128)(2,1)S(1)}, f16[8,64,128]{2,1,0:T(8,128)(2,1)S(1)}, u32[]{:S(2)}, u32[]{:S(2)}) collective-permute-start(f16[8,64,128]{2,1,0:T(8,128)(2,1)S(1)} %get-tuple-element.95), channel_id=1, source_target_pairs={{0,16},{1,5},{2,18},{3,7},{4,20},{5,1},{6,22},{7,3},{8,24},{9,13},... | collective-permute-start | bytes 393224 | tf_op jit(solution)/shard_map/ppermute | solution.py:443
  76.9 12.0 %collective-permute-start.18 = (f16[8,64,128]{2,1,0:T(8,128)(2,1)S(1)}, f16[8,64,128]{2,1,0:T(8,128)(2,1)S(1)}, u32[]{:S(2)}, u32[]{:S(2)}) collective-permute-start(f16[8,64,128]{2,1,0:T(8,128)(2,1)S(1)} %get-tuple-element.97), channel_id=1, source_target_pairs={{0,24},{1,7},{2,26},{3,1},{4,28},{5,3},{6,30},{7,5},{8,0},{9,15},{... | collective-permute-start | bytes 393224 | tf_op jit(solution)/shard_map/ppermute | solution.py:443
  77.3 11.6 %collective-permute-start.19 = (f16[8,64,128]{2,1,0:T(8,128)(2,1)S(1)}, f16[8,64,128]{2,1,0:T(8,128)(2,1)S(1)}, u32[]{:S(2)}, u32[]{:S(2)}) collective-permute-start(f16[8,64,128]{2,1,0:T(8,128)(2,1)S(1)} %get-tuple-element.96), channel_id=1, source_target_pairs={{0,8},{1,3},{2,10},{3,5},{4,12},{5,7},{6,14},{7,1},{8,16},{9,11},{... | collective-permute-start | bytes 393224 | tf_op jit(solution)/shard_map/ppermute | solution.py:443
  78.5 19.6 %all-to-all-start.2 = ((bf16[32,32,128]{2,1,0:T(8,128)(2,1)}), bf16[32,32,128]{2,1,0:T(8,128)(2,1)S(1)}, u32[]{:S(2)}, u32[]{:S(2)}) async-start(bf16[32,32,128]{2,1,0:T(8,128)(2,1)} %screen_again.1), calls=%async_computation.2 | async-start | bytes 524288 | tf_op jit(solution)/shard_map/all_to_all | solution.py:530
  91.0 7.1 %collective-permute-start.20 = (bf16[1,64,128]{2,1,0:T(8,128)(2,1)S(1)}, bf16[1,64,128]{2,1,0:T(8,128)(2,1)S(1)}, u32[]{:S(2)}, u32[]{:S(2)}) collective-permute-start(bf16[1,64,128]{2,1,0:T(8,128)(2,1)S(1)} %get-tuple-element.72), channel_id=1, source_target_pairs={{0,32},{32,0},{64,96},{96,64},{128,160},{160,128},{192,224},{224,1... | collective-permute-start | bytes 49160 | tf_op jit(solution)/shard_map/ppermute | solution.py:517
  91.3 13.2 %collective-permute-start.22 = (bf16[1,64,128]{2,1,0:T(8,128)(2,1)S(1)}, bf16[1,64,128]{2,1,0:T(8,128)(2,1)S(1)}, u32[]{:S(2)}, u32[]{:S(2)}) collective-permute-start(bf16[1,64,128]{2,1,0:T(8,128)(2,1)S(1)} %get-tuple-element.76), channel_id=1, source_target_pairs={{0,96},{32,64},{64,32},{96,0},{128,224},{160,192},{192,160},{224,1... | collective-permute-start | bytes 49160 | tf_op jit(solution)/shard_map/ppermute | solution.py:517
  92.3 12.2 %collective-permute-start.23 = (bf16[1,64,128]{2,1,0:T(8,128)(2,1)S(1)}, bf16[1,64,128]{2,1,0:T(8,128)(2,1)S(1)}, u32[]{:S(2)}, u32[]{:S(2)}) collective-permute-start(bf16[1,64,128]{2,1,0:T(8,128)(2,1)S(1)} %get-tuple-element.77), channel_id=1, source_target_pairs={{0,128},{32,160},{64,192},{96,224},{128,0},{160,32},{192,64},{224,... | collective-permute-start | bytes 49160 | tf_op jit(solution)/shard_map/ppermute | solution.py:517
  94.5 10.0 %collective-permute-start.24 = (bf16[1,64,128]{2,1,0:T(8,128)(2,1)S(1)}, bf16[1,64,128]{2,1,0:T(8,128)(2,1)S(1)}, u32[]{:S(2)}, u32[]{:S(2)}) collective-permute-start(bf16[1,64,128]{2,1,0:T(8,128)(2,1)S(1)} %get-tuple-element.78), channel_id=1, source_target_pairs={{0,160},{32,128},{64,224},{96,192},{128,32},{160,0},{192,96},{224,... | collective-permute-start | bytes 49160 | tf_op jit(solution)/shard_map/ppermute | solution.py:517
  96.7 7.9 %collective-permute-start.25 = (bf16[1,64,128]{2,1,0:T(8,128)(2,1)S(1)}, bf16[1,64,128]{2,1,0:T(8,128)(2,1)S(1)}, u32[]{:S(2)}, u32[]{:S(2)}) collective-permute-start(bf16[1,64,128]{2,1,0:T(8,128)(2,1)S(1)} %get-tuple-element.79), channel_id=1, source_target_pairs={{0,192},{32,224},{64,128},{96,160},{128,64},{160,96},{192,0},{224,... | collective-permute-start | bytes 49160 | tf_op jit(solution)/shard_map/ppermute | solution.py:517
  98.1 3.9 %collective-permute-start.21 = (bf16[1,64,128]{2,1,0:T(8,128)(2,1)S(1)}, bf16[1,64,128]{2,1,0:T(8,128)(2,1)S(1)}, u32[]{:S(2)}, u32[]{:S(2)}) collective-permute-start(bf16[1,64,128]{2,1,0:T(8,128)(2,1)S(1)} %get-tuple-element.75), channel_id=1, source_target_pairs={{0,64},{32,96},{64,0},{96,32},{128,192},{160,224},{192,128},{224,1... | collective-permute-start | bytes 49160 | tf_op jit(solution)/shard_map/ppermute | solution.py:517
  102.0 3.8 %collective-permute-start.26 = (bf16[1,64,128]{2,1,0:T(8,128)(2,1)S(1)}, bf16[1,64,128]{2,1,0:T(8,128)(2,1)S(1)}, u32[]{:S(2)}, u32[]{:S(2)}) collective-permute-start(bf16[1,64,128]{2,1,0:T(8,128)(2,1)S(1)} %get-tuple-element.80), channel_id=1, source_target_pairs={{0,224},{32,192},{64,160},{96,128},{128,96},{160,64},{192,32},{224... | collective-permute-start | bytes 49160 | tf_op jit(solution)/shard_map/ppermute | solution.py:517
  105.8 11.2 %collective-permute-start.27 = (bf16[8,64,128]{2,1,0:T(8,128)(2,1)S(1)}, bf16[8,64,128]{2,1,0:T(8,128)(2,1)S(1)}, u32[]{:S(2)}, u32[]{:S(2)}) collective-permute-start(bf16[8,64,128]{2,1,0:T(8,128)(2,1)S(1)} %constant_dynamic-update-slice_fusion.4), channel_id=1, source_target_pairs={{0,8},{1,3},{2,10},{3,5},{4,12},{5,7},{6,14},{7,1},{8,16},{9,11},{... | collective-permute-start | bytes 393224 | tf_op jit(solution)/shard_map/ppermute | solution.py:443
  107.3 9.7 %collective-permute-start.28 = (bf16[8,64,128]{2,1,0:T(8,128)(2,1)S(1)}, bf16[8,64,128]{2,1,0:T(8,128)(2,1)S(1)}, u32[]{:S(2)}, u32[]{:S(2)}) collective-permute-start(bf16[8,64,128]{2,1,0:T(8,128)(2,1)S(1)} %constant_dynamic-update-slice_fusion.4), channel_id=1, source_target_pairs={{0,16},{1,5},{2,18},{3,7},{4,20},{5,1},{6,22},{7,3},{8,24},{9,13},... | collective-permute-start | bytes 393224 | tf_op jit(solution)/shard_map/ppermute | solution.py:443
  109.7 7.4 %collective-permute-start.29 = (bf16[8,64,128]{2,1,0:T(8,128)(2,1)S(1)}, bf16[8,64,128]{2,1,0:T(8,128)(2,1)S(1)}, u32[]{:S(2)}, u32[]{:S(2)}) collective-permute-start(bf16[8,64,128]{2,1,0:T(8,128)(2,1)S(1)} %constant_dynamic-update-slice_fusion.4), channel_id=1, source_target_pairs={{0,24},{1,7},{2,26},{3,1},{4,28},{5,3},{6,30},{7,5},{8,0},{9,15},{... | collective-permute-start | bytes 393224 | tf_op jit(solution)/shard_map/ppermute | solution.py:443
  110.9 38.8 %all-to-all-start.3 = ((f32[8,192,128]{2,1,0:T(8,128)}), f32[8,192,128]{2,1,0:T(8,128)}, u32[]{:S(2)}, u32[]{:S(2)}) async-start(f32[8,192,128]{2,1,0:T(8,128)} %get-tuple-element.91), calls=%async_computation.3 | async-start | bytes 1572864 | tf_op jit(solution)/shard_map/all_to_all | solution.py:526
  117.1 15.2 %collective-permute-start.30 = (bf16[32,64,128]{2,1,0:T(8,128)(2,1)S(1)}, bf16[32,64,128]{2,1,0:T(8,128)(2,1)S(1)}, u32[]{:S(2)}, u32[]{:S(2)}) collective-permute-start(bf16[32,64,128]{2,1,0:T(8,128)(2,1)S(1)} %constant_dynamic-update-slice_fusion.12.rest_0_), channel_id=1, source_target_pairs={{0,2},{1,9},{2,4},{3,11},{4,6},{5,13},{6,0},{7,15},{8,10},{9,17},{... | collective-permute-start | bytes 1572872 | tf_op jit(solution)/shard_map/ppermute | solution.py:443
  118.3 15.0 %collective-permute-start.31 = (bf16[32,64,128]{2,1,0:T(8,128)(2,1)S(1)}, bf16[32,64,128]{2,1,0:T(8,128)(2,1)S(1)}, u32[]{:S(2)}, u32[]{:S(2)}) collective-permute-start(bf16[32,64,128]{2,1,0:T(8,128)(2,1)S(1)} %constant_dynamic-update-slice_fusion.12.rest_0_), channel_id=1, source_target_pairs={{0,4},{1,17},{2,6},{3,19},{4,0},{5,21},{6,2},{7,23},{8,12},{9,25},... | collective-permute-start | bytes 1572872 | tf_op jit(solution)/shard_map/ppermute | solution.py:443
  120.8 12.6 %collective-permute-start.32 = (bf16[32,64,128]{2,1,0:T(8,128)(2,1)S(1)}, bf16[32,64,128]{2,1,0:T(8,128)(2,1)S(1)}, u32[]{:S(2)}, u32[]{:S(2)}) collective-permute-start(bf16[32,64,128]{2,1,0:T(8,128)(2,1)S(1)} %constant_dynamic-update-slice_fusion.12.rest_0_), channel_id=1, source_target_pairs={{0,6},{1,25},{2,0},{3,27},{4,2},{5,29},{6,4},{7,31},{8,14},{9,1},{... | collective-permute-start | bytes 1572872 | tf_op jit(solution)/shard_map/ppermute | solution.py:443
  133.4 8.4 %collective-permute-start.33 = (bf16[32,64,128]{2,1,0:T(8,128)(2,1)S(1)}, bf16[32,64,128]{2,1,0:T(8,128)(2,1)S(1)}, u32[]{:S(2)}, u32[]{:S(2)}) collective-permute-start(bf16[32,64,128]{2,1,0:T(8,128)(2,1)S(1)} %constant_dynamic-update-slice_fusion.12.rest_0_), channel_id=1, source_target_pairs={{0,1},{1,0},{2,3},{3,2},{4,5},{5,4},{6,7},{7,6},{8,9},{9,8},{10,11... | collective-permute-start | bytes 1572872 | tf_op jit(solution)/shard_map/ppermute | solution.py:448
  139.3 3.0 %collective-permute-start.34 = (bf16[32,64,128]{2,1,0:T(8,128)(2,1)S(1)}, bf16[32,64,128]{2,1,0:T(8,128)(2,1)S(1)}, u32[]{:S(2)}, u32[]{:S(2)}) collective-permute-start(bf16[32,64,128]{2,1,0:T(8,128)(2,1)S(1)} %collective-permute-done.30.rest_1_), channel_id=1, source_target_pairs={{0,1},{1,0},{2,3},{3,2},{4,5},{5,4},{6,7},{7,6},{8,9},{9,8},{10,11... | collective-permute-start | bytes 1572872 | tf_op jit(solution)/shard_map/ppermute | solution.py:448
  139.3 3.2 %collective-permute-start.35 = (bf16[32,64,128]{2,1,0:T(8,128)(2,1)S(1)}, bf16[32,64,128]{2,1,0:T(8,128)(2,1)}, u32[]{:S(2)}, u32[]{:S(2)}) collective-permute-start(bf16[32,64,128]{2,1,0:T(8,128)(2,1)S(1)} %collective-permute-done.31.rest_2_), channel_id=1, source_target_pairs={{0,1},{1,0},{2,3},{3,2},{4,5},{5,4},{6,7},{7,6},{8,9},{9,8},{10,11... | collective-permute-start | bytes 1572872 | tf_op jit(solution)/shard_map/ppermute | solution.py:448
  139.8 3.4 %collective-permute-start.36 = (bf16[32,64,128]{2,1,0:T(8,128)(2,1)S(1)}, bf16[32,64,128]{2,1,0:T(8,128)(2,1)}, u32[]{:S(2)}, u32[]{:S(2)}) collective-permute-start(bf16[32,64,128]{2,1,0:T(8,128)(2,1)S(1)} %collective-permute-done.32.rest_3_), channel_id=1, source_target_pairs={{0,1},{1,0},{2,3},{3,2},{4,5},{5,4},{6,7},{7,6},{8,9},{9,8},{10,11... | collective-permute-start | bytes 1572872 | tf_op jit(solution)/shard_map/ppermute | solution.py:448
  (5 other events, 111.7 us)

commit v4 on v3

--- a/solution.py
+++ b/solution.py
@@ -365,10 +365,11 @@
     )(slots, loads, w, target, *blocks)
 
 
-def second_kernel(slots, loads, w_hbm, *rest):
-    blocks, image, (colors, w, sems, w_sems) = rest[:8], rest[8], rest[9:]
+def second_kernel(slots, loads, w_hbm, packed, *rest):
+    blocks, image, news, (colors, w, sems, w_sems, n_sems) = rest[:8], rest[8], rest[9:12], rest[12:]
     copies = load_colors(blocks, colors, sems)
     fetch_weights(loads, w_hbm, w, w_sems)
+    moves = fetch([(packed.at[:, pl.ds(i * C, C)], new) for i, new in enumerate(news)], n_sems)
     for copy in copies:
         copy.wait()
 
@@ -376,24 +377,28 @@
         image[tile] = picture(slots, tile, w, size, colors)
 
     over_tiles(loads, w_hbm, w, w_sems, body)
-
-
-def second_render(slots, loads, w, blocks):
+    for move in moves:
+        move.wait()
+
+
+def second_render(slots, loads, w, packed, blocks):
+    wide = jax.ShapeDtypeStruct((BINS, C, GB), f32)
     return pl.pallas_call(
         second_kernel,
-        out_shape=jax.ShapeDtypeStruct((TILES, C, PIX), f32),
-        in_specs=[SM, SM, ANY] + [ANY] * 8,
-        out_specs=VM,
+        out_shape=(jax.ShapeDtypeStruct((TILES, C, PIX), f32), wide, wide, wide),
+        in_specs=[SM, SM, ANY, ANY] + [ANY] * 8,
+        out_specs=(VM, ANY, ANY, ANY),
         scratch_shapes=[
             pltpu.VMEM((N_TILE * BINS, C, GB), bf16),
             pltpu.VMEM((TILES, LBLK, GB, PIX), bf16),
             pltpu.SemaphoreType.DMA((8,)),
             pltpu.SemaphoreType.DMA((TILES,)),
+            pltpu.SemaphoreType.DMA((3,)),
         ],
         compiler_params=params(SECOND_MIB),
         cost_estimate=pl.CostEstimate(flops=TILES * LBLK * C * GB * PIX * 2, bytes_accessed=14_000_000, transcendentals=0),
         name="second_render",
-    )(slots, loads, w, *blocks)
+    )(slots, loads, w, packed, *blocks)
 
 
 def adam_kernel(owner, me, gradient, feat, m1, m2, *rest):
@@ -553,9 +558,10 @@
     screen = across_tile(screen)
     own, screen = gather_plane(gather_line(colors), screen)
     w_first, token = weights(lists_first[0], loads_first[0], shift_first[0], screen, "weights_first")
+    line, *own = own
     *own, token = tie(*own, token)
     slots = color_slots(lists_first[0], lists_first[0] % BINS) + token[0, 0]
-    parts = first_render(slots, loads_first[0], w_first, target[0], swapped(own))
+    parts = first_render(slots, loads_first[0], w_first, target[0], swapped([line] + own))
     line, geometry = scatter_far(parts, geometry)
     screen = screen_again(cameras_second[0], across_view(geometry))
     line, screen = tie(line, screen)
@@ -567,11 +573,13 @@
     colors, packed = tie(colors, packed)
     w_second, token = weights(lists_second[0], loads_second[0], shift_second[0], screen, "weights_second")
     packed = across_view(packed)
-    *own, token = tie(*gather_plane(gather_line(colors)), token)
-    blocks = swapped(own)
+    line, *own = gather_plane(gather_line(colors))
+    *own, token = tie(*own, token)
+    blocks = swapped([line] + own)
     slots = color_slots(lists_second[0], place_of(lists_second[0] % BINS)) + token[0, 0]
-    image = second_render(slots, loads_second[0], w_second, blocks)
-    new_features, new_first, new_second = (packed[:, i * C : i * C + C] for i in range(3))
+    image, new_features, new_first, new_second = second_render(
+        slots, loads_second[0], w_second, packed, blocks
+    )
     return (image[None], new_features, new_first, new_second)
 
 

time: 151 us -> 150 us (level); the launches traced: 152 us -> 148 us
  starting transfers between devices: 66.8 us -> 69.7 us
  blocking collectives: 17.9 us -> 15.1 us
  local copies, waits for them, and re-layouts: 6.01 us -> 3.81 us
    ppermute x12, starting transfers between devices: 9.13 us -> 12.5 us  [swap_core(): return lax.ppermute(value, 'tile', pairs)]
    all_to_all x1, blocking collectives: 17.9 us -> 15.1 us  [across_view(): lax.all_to_all(value, 'view', split_axis=0, concat_axis=0, tiled=True)]
    slice x1 -> x0, local copies, waits for them, and re-layouts: 2.01 us -> none  [local(): packed[:, i * C:i * C + C]]
  transfers between devices with their start and end apart: 40 -> 40, of which waited for: 11 -> 8; matrix products, arithmetic and copies ran while one was open for 4% -> 4% of each run, Pallas kernels for 21% -> 16%
where the time goes in v4:
time: 150 us; the launch traced here: 148 us
  starting transfers between devices  69.7 us (46%)
  Pallas kernels  42.3 us (28%)
  blocking collectives  15.1 us (10%)
  waiting for transfers between devices  13.6 us (9%)
  local copies, waits for them, and re-layouts  3.81 us (3%)
  other arithmetic  2.64 us (2%)
    ppermute x18, starting transfers between devices, shift_by(): return lax.ppermute(value, 'tile', pairs)  25.2 us
    pallas_call x2, Pallas kernels, weights(): pl.pallas_call(weights_kernel, out_shape=(jax.ShapeDtypeStruct((TILES, LB...  20.5 us
    all_to_all x2, starting transfers between devices, across_tile(): lax.all_to_all(value, 'tile', split_axis=0, concat_axis=0, tiled=True)  15.2 us
    all_to_all x1, blocking collectives, across_view(): lax.all_to_all(value, 'view', split_axis=0, concat_axis=0, tiled=True)  15.1 us
    ppermute x12, starting transfers between devices, swap_core(): return lax.ppermute(value, 'tile', pairs)  12.5 us
    ppermute x7, starting transfers between devices, exchange_views(): got[r] = lax.ppermute(value, 'view', [(v, v ^ r) for v in range(N_VIEW)])  10.7 us
    pallas_call x1, Pallas kernels, first_render(): pl.pallas_call(first_kernel, out_shape=(jax.ShapeDtypeStruct((32, C, GB),...  9.55 us
    pallas_call x1, Pallas kernels, second_render(): pl.pallas_call(second_kernel, out_shape=(jax.ShapeDtypeStruct((TILES, C,...  6.86 us
  transfers between devices with their start and end apart: 40, of which 8 were waited for; matrix products, arithmetic and copies ran while one was open for 4% of the time, Pallas kernels for 16%

profile of v4, /device:TPU:1, one launch (start us, length us, event | category | flops | bytes accessed | tf_op | source)
XLA Modules:
  0.0 148.5 jit_solution(7298070993983178186)
XLA Ops:
  0.7 2.0 %prep.1 = (bf16[8,64,128]{2,1,0:T(8,128)(2,1)}, bf16[32,32,128]{2,1,0:T(8,128)(2,1)}, f32[8,8,128]{2,1,0:T(8,128)}) custom-call(f32[1,2,4]{2,1,0:T(2,128)} %camera_hbm.1, s32[8]{0:T(128)} %owner.1, f32[8,64,128]{2,1,0:T(8,128)} %feat.1, f32[3,8,128]{2,1,0:T(8,128)} %bitcast.27, f32[8,128]{1,0:T(8,128)} %scales_hbm.1, f32[8,128]{1,0:T(8,128)} %opacity_hbm.1), custom_call_target="tpu_custom_call" | custom-call | tf_op jit(solution)/shard_map/prep/pallas_call | solution.py:118
  2.7 2.2 %collective-permute-start = (bf16[8,64,128]{2,1,0:T(8,128)(2,1)}, bf16[8,64,128]{2,1,0:T(8,128)(2,1)S(1)}, u32[]{:S(2)}, u32[]{:S(2)}) collective-permute-start(bf16[8,64,128]{2,1,0:T(8,128)(2,1)} %get-tuple-element.50), channel_id=1, source_target_pairs={{0,8},{1,3},{2,10},{3,5},{4,12},{5,7},{6,14},{7,1},{8,16},{9,11},{... | collective-permute-start | bytes 393224 | tf_op jit(solution)/shard_map/ppermute | solution.py:448
  4.9 2.6 %collective-permute-start.1 = (bf16[8,64,128]{2,1,0:T(8,128)(2,1)}, bf16[8,64,128]{2,1,0:T(8,128)(2,1)S(1)}, u32[]{:S(2)}, u32[]{:S(2)}) collective-permute-start(bf16[8,64,128]{2,1,0:T(8,128)(2,1)} %get-tuple-element.50), channel_id=1, source_target_pairs={{0,16},{1,5},{2,18},{3,7},{4,20},{5,1},{6,22},{7,3},{8,24},{9,13},... | collective-permute-start | bytes 393224 | tf_op jit(solution)/shard_map/ppermute | solution.py:448
  7.5 1.1 collective-permute-start.2
  8.6 6.0 %all-to-all-start = ((bf16[32,32,128]{2,1,0:T(8,128)(2,1)}), bf16[32,32,128]{2,1,0:T(8,128)(2,1)S(1)}, u32[]{:S(2)}, u32[]{:S(2)}) async-start(bf16[32,32,128]{2,1,0:T(8,128)(2,1)} %get-tuple-element.51), calls=%async_computation | async-start | bytes 524288 | tf_op jit(solution)/shard_map/all_to_all | solution.py:535
  14.6 0.9 constant_dynamic-update-slice_fusion.3
  15.6 1.5 collective-permute-start.3
  17.1 2.4 %collective-permute-start.4 = (bf16[32,64,128]{2,1,0:T(8,128)(2,1)S(1)}, bf16[32,64,128]{2,1,0:T(8,128)(2,1)S(1)}, u32[]{:S(2)}, u32[]{:S(2)}) collective-permute-start(bf16[32,64,128]{2,1,0:T(8,128)(2,1)S(1)} %constant_dynamic-update-slice_fusion.rest_0_), channel_id=1, source_target_pairs={{0,4},{1,17},{2,6},{3,19},{4,0},{5,21},{6,2},{7,23},{8,12},{9,25},... | collective-permute-start | bytes 1572872 | tf_op jit(solution)/shard_map/ppermute | solution.py:448
  19.5 4.4 %all-to-all-done.screen_hbm = bf16[32,32,128]{2,1,0:T(8,128)(2,1)S(1)} async-done(((bf16[32,32,128]{2,1,0:T(8,128)(2,1)}), bf16[32,32,128]{2,1,0:T(8,128)(2,1)S(1)}, u32[]{:S(2)}, u32[]{:S(2)}) %all-to-all-start) | async-done | bytes 262176 | tf_op jit(solution)/shard_map/all_to_all | solution.py:535
  24.4 0.8 collective-permute-start.6
  25.2 10.2 %weights_first.1 = (bf16[16,8,128,256]{3,2,1,0:T(8,128)(2,1)}, s32[8,128]{1,0:T(8,128)}) custom-call(s32[8,16]{1,0:T(8,128)} %bitcast.28, s32[16]{0:T(128)} %bitcast.23, f32[2,16]{1,0:T(2,128)} %bitcast.33, bf16[32,32,128]{2,1,0:T(8,128)(2,1)} %copy-done.9), custom_call_target="tpu_custom_call" | custom-call | flops 58720256 | bytes 10000000 | tf_op jit(solution)/shard_map/weights_first/pallas_call | solution.py:258
  35.4 1.8 %collective-permute-start.7 = (bf16[32,64,128]{2,1,0:T(8,128)(2,1)S(1)}, bf16[32,64,128]{2,1,0:T(8,128)(2,1)}, u32[]{:S(2)}, u32[]{:S(2)}) collective-permute-start(bf16[32,64,128]{2,1,0:T(8,128)(2,1)S(1)} %collective-permute-done.3.rest_1_), channel_id=1, source_target_pairs={{0,1},{1,0},{2,3},{3,2},{4,5},{5,4},{6,7},{7,6},{8,9},{9,8},{10,11... | collective-permute-start | bytes 1572872 | tf_op jit(solution)/shard_map/ppermute | solution.py:453
  37.8 1.2 slice.21
  39.0 0.7 fusion.16.slots
  39.7 0.7 collective-permute-done.9.rest_7_
  40.4 9.5 %first_render.1 = (f32[32,64,128]{2,1,0:T(8,128)S(1)}, f32[32,64,128]{2,1,0:T(8,128)S(1)}, f32[32,64,128]{2,1,0:T(8,128)S(1)}, f32[32,64,128]{2,1,0:T(8,128)S(1)...) custom-call(s32[16,8]{1,0:T(8,128)S(1)} %fusion.16.slots, ...), custom_call_target="tpu_custom_call" | custom-call | flops 1073741824 | bytes 25000000 | tf_op jit(solution)/shard_map/first_render/pallas_call | solution.py:348
  50.0 1.3 collective-permute-start.11
  51.9 1.7 %collective-permute-done.11 = f32[32,64,128]{2,1,0:T(8,128)S(1)} collective-permute-done((f32[32,64,128]{2,1,0:T(8,128)S(1)}, f32[32,64,128]{2,1,0:T(8,128)S(1)}, u32[]{:S(2)}, u32[]{:S(2)}) %collective-permute-start.11) | collective-permute-done | bytes 1048608 | tf_op jit(solution)/shard_map/ppermute | solution.py:453
  54.1 1.0 collective-permute-done.13
  55.4 1.2 collective-permute-done.15
  57.2 15.1 %all_to_all.20.geometry = f32[8,8,128]{2,1,0:T(8,128)S(1)} all-to-all(f32[8,8,128]{2,1,0:T(8,128)S(1)} %copy-done.10), channel_id=1, replica_groups=mesh['view'=8,'tile'=32] {'view'}, dimensions={0} | all-to-all | bytes 65536 | tf_op jit(solution)/shard_map/all_to_all | solution.py:531
  72.3 1.4 screen_again.1
  74.5 1.1 collective-permute-start.17
  75.6 3.0 %collective-permute-start.18 = (f16[8,64,128]{2,1,0:T(8,128)(2,1)S(1)}, f16[8,64,128]{2,1,0:T(8,128)(2,1)S(1)}, u32[]{:S(2)}, u32[]{:S(2)}) collective-permute-start(f16[8,64,128]{2,1,0:T(8,128)(2,1)S(1)} %get-tuple-element.98), channel_id=1, source_target_pairs={{0,24},{1,7},{2,26},{3,1},{4,28},{5,3},{6,30},{7,5},{8,0},{9,15},{... | collective-permute-start | bytes 393224 | tf_op jit(solution)/shard_map/ppermute | solution.py:448
  78.6 9.2 %all-to-all-start.2 = ((bf16[32,32,128]{2,1,0:T(8,128)(2,1)}), bf16[32,32,128]{2,1,0:T(8,128)(2,1)S(1)}, u32[]{:S(2)}, u32[]{:S(2)}) async-start(bf16[32,32,128]{2,1,0:T(8,128)(2,1)} %screen_again.1), calls=%async_computation.2 | async-start | bytes 524288 | tf_op jit(solution)/shard_map/all_to_all | solution.py:535
  88.1 1.9 %adam.1 = (bf16[1,64,128]{2,1,0:T(8,128)(2,1)S(1)}, bf16[1,64,128]{2,1,0:T(8,128)(2,1)S(1)}, bf16[1,64,128]{2,1,0:T(8,128)(2,1)S(1)}, bf16[1,64,128]{2,1,0:T(8,1...) custom-call(s32[8]{0:T(128)S(1)} %copy-done.4, ...), custom_call_target="tpu_custom_call" | custom-call | tf_op jit(solution)/shard_map/adam/pallas_call | solution.py:423
  90.3 1.0 collective-permute-start.22
  91.3 2.2 %collective-permute-start.23 = (bf16[1,64,128]{2,1,0:T(8,128)(2,1)S(1)}, bf16[1,64,128]{2,1,0:T(8,128)(2,1)S(1)}, u32[]{:S(2)}, u32[]{:S(2)}) collective-permute-start(bf16[1,64,128]{2,1,0:T(8,128)(2,1)S(1)} %get-tuple-element.78), channel_id=1, source_target_pairs={{0,128},{32,160},{64,192},{96,224},{128,0},{160,32},{192,64},{224,... | collective-permute-start | bytes 49160 | tf_op jit(solution)/shard_map/ppermute | solution.py:522
  93.5 2.1 %collective-permute-start.24 = (bf16[1,64,128]{2,1,0:T(8,128)(2,1)S(1)}, bf16[1,64,128]{2,1,0:T(8,128)(2,1)S(1)}, u32[]{:S(2)}, u32[]{:S(2)}) collective-permute-start(bf16[1,64,128]{2,1,0:T(8,128)(2,1)S(1)} %get-tuple-element.79), channel_id=1, source_target_pairs={{0,160},{32,128},{64,224},{96,192},{128,32},{160,0},{192,96},{224,... | collective-permute-start | bytes 49160 | tf_op jit(solution)/shard_map/ppermute | solution.py:522
  95.6 1.4 collective-permute-start.25
  97.0 1.2 collective-permute-start.21
  98.2 2.7 %collective-permute-done.21 = bf16[1,64,128]{2,1,0:T(8,128)(2,1)S(1)} collective-permute-done((bf16[1,64,128]{2,1,0:T(8,128)(2,1)S(1)}, bf16[1,64,128]{2,1,0:T(8,128)(2,1)S(1)}, u32[]{:S(2)}, u32[]{:S(2)}) %collective-permute-start.21) | collective-permute-done | bytes 16416 | tf_op jit(solution)/shard_map/ppermute | solution.py:522
  100.9 2.5 %collective-permute-start.26 = (bf16[1,64,128]{2,1,0:T(8,128)(2,1)S(1)}, bf16[1,64,128]{2,1,0:T(8,128)(2,1)S(1)}, u32[]{:S(2)}, u32[]{:S(2)}) collective-permute-start(bf16[1,64,128]{2,1,0:T(8,128)(2,1)S(1)} %get-tuple-element.81), channel_id=1, source_target_pairs={{0,224},{32,192},{64,160},{96,128},{128,96},{160,64},{192,32},{224... | collective-permute-start | bytes 49160 | tf_op jit(solution)/shard_map/ppermute | solution.py:522
  103.5 1.2 collective-permute-done.26
  104.7 1.5 %collective-permute-start.27 = (bf16[8,64,128]{2,1,0:T(8,128)(2,1)S(1)}, bf16[8,64,128]{2,1,0:T(8,128)(2,1)S(1)}, u32[]{:S(2)}, u32[]{:S(2)}) collective-permute-start(bf16[8,64,128]{2,1,0:T(8,128)(2,1)S(1)} %constant_dynamic-update-slice_fusion.4), channel_id=1, source_target_pairs={{0,8},{1,3},{2,10},{3,5},{4,12},{5,7},{6,14},{7,1},{8,16},{9,11},{... | collective-permute-start | bytes 393224 | tf_op jit(solution)/shard_map/ppermute | solution.py:448
  106.2 2.4 %collective-permute-start.28 = (bf16[8,64,128]{2,1,0:T(8,128)(2,1)S(1)}, bf16[8,64,128]{2,1,0:T(8,128)(2,1)S(1)}, u32[]{:S(2)}, u32[]{:S(2)}) collective-permute-start(bf16[8,64,128]{2,1,0:T(8,128)(2,1)S(1)} %constant_dynamic-update-slice_fusion.4), channel_id=1, source_target_pairs={{0,16},{1,5},{2,18},{3,7},{4,20},{5,1},{6,22},{7,3},{8,24},{9,13},... | collective-permute-start | bytes 393224 | tf_op jit(solution)/shard_map/ppermute | solution.py:448
  108.6 1.3 collective-permute-start.29
  109.9 6.0 %all-to-all-start.3 = ((f32[8,192,128]{2,1,0:T(8,128)}), f32[8,192,128]{2,1,0:T(8,128)S(1)}, u32[]{:S(2)}, u32[]{:S(2)}) async-start(f32[8,192,128]{2,1,0:T(8,128)} %get-tuple-element.88), calls=%async_computation.3 | async-start | bytes 1572864 | tf_op jit(solution)/shard_map/all_to_all | solution.py:531
  116.0 1.3 collective-permute-start.30
  117.3 2.5 %collective-permute-start.31 = (bf16[32,64,128]{2,1,0:T(8,128)(2,1)S(1)}, bf16[32,64,128]{2,1,0:T(8,128)(2,1)S(1)}, u32[]{:S(2)}, u32[]{:S(2)}) collective-permute-start(bf16[32,64,128]{2,1,0:T(8,128)(2,1)S(1)} %constant_dynamic-update-slice_fusion.12.rest_0_), channel_id=1, source_target_pairs={{0,4},{1,17},{2,6},{3,19},{4,0},{5,21},{6,2},{7,23},{8,12},{9,25},... | collective-permute-start | bytes 1572872 | tf_op jit(solution)/shard_map/ppermute | solution.py:448
  119.8 1.1 collective-permute-start.32
  120.9 10.3 %weights_second.1 = (bf16[16,8,128,256]{3,2,1,0:T(8,128)(2,1)}, s32[8,128]{1,0:T(8,128)}) custom-call(s32[8,16]{1,0:T(8,128)} %bitcast.30, s32[16]{0:T(128)} %bitcast.25, f32[2,16]{1,0:T(2,128)} %bitcast.34, bf16[32,32,128]{2,1,0:T(8,128)(2,1)} %copy-done.8), custom_call_target="tpu_custom_call" | custom-call | flops 58720256 | bytes 10000000 | tf_op jit(solution)/shard_map/weights_second/pallas_call | solution.py:258
  131.2 5.1 %collective-permute-start.33 = (bf16[32,64,128]{2,1,0:T(8,128)(2,1)S(1)}, bf16[32,64,128]{2,1,0:T(8,128)(2,1)S(1)}, u32[]{:S(2)}, u32[]{:S(2)}) collective-permute-start(bf16[32,64,128]{2,1,0:T(8,128)(2,1)S(1)} %constant_dynamic-update-slice_fusion.12.rest_0_), channel_id=1, source_target_pairs={{0,1},{1,0},{2,3},{3,2},{4,5},{5,4},{6,7},{7,6},{8,9},{9,8},{10,11... | collective-permute-start | bytes 1572872 | tf_op jit(solution)/shard_map/ppermute | solution.py:453
  136.3 1.9 %collective-permute-start.34 = (bf16[32,64,128]{2,1,0:T(8,128)(2,1)S(1)}, bf16[32,64,128]{2,1,0:T(8,128)(2,1)}, u32[]{:S(2)}, u32[]{:S(2)}) collective-permute-start(bf16[32,64,128]{2,1,0:T(8,128)(2,1)S(1)} %collective-permute-done.30.rest_1_), channel_id=1, source_target_pairs={{0,1},{1,0},{2,3},{3,2},{4,5},{5,4},{6,7},{7,6},{8,9},{9,8},{10,11... | collective-permute-start | bytes 1572872 | tf_op jit(solution)/shard_map/ppermute | solution.py:453
  138.8 1.2 slice.26
  140.0 0.7 fusion.8.slots
  140.7 0.7 collective-permute-done.36.rest_7_
  141.4 6.9 %second_render.1 = (f32[16,64,256]{2,1,0:T(8,128)}, f32[8,64,128]{2,1,0:T(8,128)}, f32[8,64,128]{2,1,0:T(8,128)}, f32[8,64,128]{2,1,0:T(8,128)}) custom-call(s32[16,8]{1,0:T(8,128)S(1)} %fusion.8.slots, s32[16]{0:T(128)S(1)} %bitcast.26, bf16[16,8,128,256]{3,2,1,0:T(8,128)(2,1)} %get-tuple-element.87.w_hbm, f32[8,192,128]{2,1,0:T(8,128)S(1)} %all-to-all-done.3.packed, ...), custom_call_target="tpu_custom_call" | custom-call | flops 536870912 | bytes 14000000 | tf_op jit(solution)/shard_map/second_render/pallas_call | solution.py:386
  (95 shorter events, 5.0 us)
Async XLA Ops:
  0.6 39.8 %copy-start.6 = (s32[1,16]{1,0:T(1,128)S(1)}, s32[1,16]{1,0:T(1,128)}, u32[]{:S(2)}) copy-start(s32[1,16]{1,0:T(1,128)} %param.25) | copy-start | bytes 196
  0.7 39.8 %copy-start.1 = (bf16[1,16,64,256]{3,2,1,0:T(8,128)(2,1)S(1)}, bf16[1,16,64,256]{3,2,1,0:T(8,128)(2,1)}, u32[]{:S(2)}) copy-start(bf16[1,16,64,256]{3,2,1,0:T(8,128)(2,1)} %param.26) | copy-start | bytes 1572868
  2.7 12.8 %collective-permute-start = (bf16[8,64,128]{2,1,0:T(8,128)(2,1)}, bf16[8,64,128]{2,1,0:T(8,128)(2,1)S(1)}, u32[]{:S(2)}, u32[]{:S(2)}) collective-permute-start(bf16[8,64,128]{2,1,0:T(8,128)(2,1)} %get-tuple-element.50), channel_id=1, source_target_pairs={{0,8},{1,3},{2,10},{3,5},{4,12},{5,7},{6,14},{7,1},{8,16},{9,11},{... | collective-permute-start | bytes 393224 | tf_op jit(solution)/shard_map/ppermute | solution.py:448
  4.9 10.7 %collective-permute-start.1 = (bf16[8,64,128]{2,1,0:T(8,128)(2,1)}, bf16[8,64,128]{2,1,0:T(8,128)(2,1)S(1)}, u32[]{:S(2)}, u32[]{:S(2)}) collective-permute-start(bf16[8,64,128]{2,1,0:T(8,128)(2,1)} %get-tuple-element.50), channel_id=1, source_target_pairs={{0,16},{1,5},{2,18},{3,7},{4,20},{5,1},{6,22},{7,3},{8,24},{9,13},... | collective-permute-start | bytes 393224 | tf_op jit(solution)/shard_map/ppermute | solution.py:448
  7.5 8.1 %collective-permute-start.2 = (bf16[8,64,128]{2,1,0:T(8,128)(2,1)}, bf16[8,64,128]{2,1,0:T(8,128)(2,1)S(1)}, u32[]{:S(2)}, u32[]{:S(2)}) collective-permute-start(bf16[8,64,128]{2,1,0:T(8,128)(2,1)} %get-tuple-element.50), channel_id=1, source_target_pairs={{0,24},{1,7},{2,26},{3,1},{4,28},{5,3},{6,30},{7,5},{8,0},{9,15},{... | collective-permute-start | bytes 393224 | tf_op jit(solution)/shard_map/ppermute | solution.py:448
  8.6 15.3 %all-to-all-start = ((bf16[32,32,128]{2,1,0:T(8,128)(2,1)}), bf16[32,32,128]{2,1,0:T(8,128)(2,1)S(1)}, u32[]{:S(2)}, u32[]{:S(2)}) async-start(bf16[32,32,128]{2,1,0:T(8,128)(2,1)} %get-tuple-element.51), calls=%async_computation | async-start | bytes 524288 | tf_op jit(solution)/shard_map/all_to_all | solution.py:535
  15.6 19.8 %collective-permute-start.3 = (bf16[32,64,128]{2,1,0:T(8,128)(2,1)S(1)}, bf16[32,64,128]{2,1,0:T(8,128)(2,1)S(1)}, u32[]{:S(2)}, u32[]{:S(2)}) collective-permute-start(bf16[32,64,128]{2,1,0:T(8,128)(2,1)S(1)} %constant_dynamic-update-slice_fusion.rest_0_), channel_id=1, source_target_pairs={{0,2},{1,9},{2,4},{3,11},{4,6},{5,13},{6,0},{7,15},{8,10},{9,17},{... | collective-permute-start | bytes 1572872 | tf_op jit(solution)/shard_map/ppermute | solution.py:448
  17.1 18.3 %collective-permute-start.4 = (bf16[32,64,128]{2,1,0:T(8,128)(2,1)S(1)}, bf16[32,64,128]{2,1,0:T(8,128)(2,1)S(1)}, u32[]{:S(2)}, u32[]{:S(2)}) collective-permute-start(bf16[32,64,128]{2,1,0:T(8,128)(2,1)S(1)} %constant_dynamic-update-slice_fusion.rest_0_), channel_id=1, source_target_pairs={{0,4},{1,17},{2,6},{3,19},{4,0},{5,21},{6,2},{7,23},{8,12},{9,25},... | collective-permute-start | bytes 1572872 | tf_op jit(solution)/shard_map/ppermute | solution.py:448
  23.9 11.5 %collective-permute-start.5 = (bf16[32,64,128]{2,1,0:T(8,128)(2,1)S(1)}, bf16[32,64,128]{2,1,0:T(8,128)(2,1)S(1)}, u32[]{:S(2)}, u32[]{:S(2)}) collective-permute-start(bf16[32,64,128]{2,1,0:T(8,128)(2,1)S(1)} %constant_dynamic-update-slice_fusion.rest_0_), channel_id=1, source_target_pairs={{0,6},{1,25},{2,0},{3,27},{4,2},{5,29},{6,4},{7,31},{8,14},{9,1},{... | collective-permute-start | bytes 1572872 | tf_op jit(solution)/shard_map/ppermute | solution.py:448
  24.4 15.3 %collective-permute-start.6 = (bf16[32,64,128]{2,1,0:T(8,128)(2,1)S(1)}, bf16[32,64,128]{2,1,0:T(8,128)(2,1)S(1)}, u32[]{:S(2)}, u32[]{:S(2)}) collective-permute-start(bf16[32,64,128]{2,1,0:T(8,128)(2,1)S(1)} %constant_dynamic-update-slice_fusion.rest_0_), channel_id=1, source_target_pairs={{0,1},{1,0},{2,3},{3,2},{4,5},{5,4},{6,7},{7,6},{8,9},{9,8},{10,11... | collective-permute-start | bytes 1572872 | tf_op jit(solution)/shard_map/ppermute | solution.py:453
  35.4 4.3 %collective-permute-start.7 = (bf16[32,64,128]{2,1,0:T(8,128)(2,1)S(1)}, bf16[32,64,128]{2,1,0:T(8,128)(2,1)}, u32[]{:S(2)}, u32[]{:S(2)}) collective-permute-start(bf16[32,64,128]{2,1,0:T(8,128)(2,1)S(1)} %collective-permute-done.3.rest_1_), channel_id=1, source_target_pairs={{0,1},{1,0},{2,3},{3,2},{4,5},{5,4},{6,7},{7,6},{8,9},{9,8},{10,11... | collective-permute-start | bytes 1572872 | tf_op jit(solution)/shard_map/ppermute | solution.py:453
  37.2 2.5 %collective-permute-start.8 = (bf16[32,64,128]{2,1,0:T(8,128)(2,1)S(1)}, bf16[32,64,128]{2,1,0:T(8,128)(2,1)}, u32[]{:S(2)}, u32[]{:S(2)}) collective-permute-start(bf16[32,64,128]{2,1,0:T(8,128)(2,1)S(1)} %collective-permute-done.4.rest_2_), channel_id=1, source_target_pairs={{0,1},{1,0},{2,3},{3,2},{4,5},{5,4},{6,7},{7,6},{8,9},{9,8},{10,11... | collective-permute-start | bytes 1572872 | tf_op jit(solution)/shard_map/ppermute | solution.py:453
  37.3 3.1 %collective-permute-start.9 = (bf16[32,64,128]{2,1,0:T(8,128)(2,1)S(1)}, bf16[32,64,128]{2,1,0:T(8,128)(2,1)}, u32[]{:S(2)}, u32[]{:S(2)}) collective-permute-start(bf16[32,64,128]{2,1,0:T(8,128)(2,1)S(1)} %collective-permute-done.5.rest_3_), channel_id=1, source_target_pairs={{0,1},{1,0},{2,3},{3,2},{4,5},{5,4},{6,7},{7,6},{8,9},{9,8},{10,11... | collective-permute-start | bytes 1572872 | tf_op jit(solution)/shard_map/ppermute | solution.py:453
  50.0 38.0 %copy-start = (f32[8,64,128]{2,1,0:T(8,128)S(1)}, f32[8,64,128]{2,1,0:T(8,128)}, u32[]{:S(2)}) copy-start(f32[8,64,128]{2,1,0:T(8,128)} %feat.1) | copy-start | bytes 786436
  50.0 38.0 %copy-start.2 = (f32[8,64,128]{2,1,0:T(8,128)S(1)}, f32[8,64,128]{2,1,0:T(8,128)}, u32[]{:S(2)}) copy-start(f32[8,64,128]{2,1,0:T(8,128)} %m1.1) | copy-start | bytes 786436
  50.0 38.0 %copy-start.3 = (f32[8,64,128]{2,1,0:T(8,128)S(1)}, f32[8,64,128]{2,1,0:T(8,128)}, u32[]{:S(2)}) copy-start(f32[8,64,128]{2,1,0:T(8,128)} %m2.1) | copy-start | bytes 786436
  50.0 38.0 %copy-start.4 = (s32[8]{0:T(128)S(1)}, s32[8]{0:T(128)}, u32[]{:S(2)}) copy-start(s32[8]{0:T(128)} %owner.1) | copy-start | bytes 100
  50.0 3.6 %collective-permute-start.11 = (f32[32,64,128]{2,1,0:T(8,128)S(1)}, f32[32,64,128]{2,1,0:T(8,128)S(1)}, u32[]{:S(2)}, u32[]{:S(2)}) collective-permute-start(f32[32,64,128]{2,1,0:T(8,128)S(1)} %get-tuple-element.63), channel_id=1, source_target_pairs={{0,1},{1,0},{2,3},{3,2},{4,5},{5,4},{6,7},{7,6},{8,9},{9,8},{10,11... | collective-permute-start | bytes 3145736 | tf_op jit(solution)/shard_map/ppermute | solution.py:453
  51.3 3.8 %collective-permute-start.13 = (f32[32,64,128]{2,1,0:T(8,128)S(1)}, f32[32,64,128]{2,1,0:T(8,128)S(1)}, u32[]{:S(2)}, u32[]{:S(2)}) collective-permute-start(f32[32,64,128]{2,1,0:T(8,128)S(1)} %get-tuple-element.65), channel_id=1, source_target_pairs={{0,1},{1,0},{2,3},{3,2},{4,5},{5,4},{6,7},{7,6},{8,9},{9,8},{10,11... | collective-permute-start | bytes 3145736 | tf_op jit(solution)/shard_map/ppermute | solution.py:453
  51.4 5.2 %collective-permute-start.15 = (f32[32,64,128]{2,1,0:T(8,128)S(1)}, f32[32,64,128]{2,1,0:T(8,128)S(1)}, u32[]{:S(2)}, u32[]{:S(2)}) collective-permute-start(f32[32,64,128]{2,1,0:T(8,128)S(1)} %get-tuple-element.67), channel_id=1, source_target_pairs={{0,1},{1,0},{2,3},{3,2},{4,5},{5,4},{6,7},{7,6},{8,9},{9,8},{10,11... | collective-permute-start | bytes 3145736 | tf_op jit(solution)/shard_map/ppermute | solution.py:453
  51.8 21.9 %collective-permute-start.10 = (f32[32,64,128]{2,1,0:T(8,128)S(1)}, f32[32,64,128]{2,1,0:T(8,128)S(1)}, u32[]{:S(2)}, u32[]{:S(2)}) collective-permute-start(f32[32,64,128]{2,1,0:T(8,128)S(1)} %get-tuple-element.61), channel_id=1, source_target_pairs={{0,1},{1,0},{2,3},{3,2},{4,5},{5,4},{6,7},{7,6},{8,9},{9,8},{10,11... | collective-permute-start | bytes 3145736 | tf_op jit(solution)/shard_map/ppermute | solution.py:453
  53.8 19.9 %collective-permute-start.12 = (f16[32,64,128]{2,1,0:T(8,128)(2,1)S(1)}, f16[32,64,128]{2,1,0:T(8,128)(2,1)S(1)}, u32[]{:S(2)}, u32[]{:S(2)}) collective-permute-start(f16[32,64,128]{2,1,0:T(8,128)(2,1)S(1)} %add_convert_fusion.2), channel_id=1, source_target_pairs={{0,4},{1,17},{2,6},{3,19},{4,0},{5,21},{6,2},{7,23},{8,12},{9,25},... | collective-permute-start | bytes 1572872 | tf_op jit(solution)/shard_map/ppermute | solution.py:448
  55.3 18.4 %collective-permute-start.14 = (f16[32,64,128]{2,1,0:T(8,128)(2,1)S(1)}, f16[32,64,128]{2,1,0:T(8,128)(2,1)S(1)}, u32[]{:S(2)}, u32[]{:S(2)}) collective-permute-start(f16[32,64,128]{2,1,0:T(8,128)(2,1)S(1)} %add_convert_fusion.1), channel_id=1, source_target_pairs={{0,6},{1,25},{2,0},{3,27},{4,2},{5,29},{6,4},{7,31},{8,14},{9,1},{... | collective-permute-start | bytes 1572872 | tf_op jit(solution)/shard_map/ppermute | solution.py:448
  56.8 16.9 %collective-permute-start.16 = (f16[32,64,128]{2,1,0:T(8,128)(2,1)S(1)}, f16[32,64,128]{2,1,0:T(8,128)(2,1)S(1)}, u32[]{:S(2)}, u32[]{:S(2)}) collective-permute-start(f16[32,64,128]{2,1,0:T(8,128)(2,1)S(1)} %add_convert_fusion), channel_id=1, source_target_pairs={{0,2},{1,9},{2,4},{3,11},{4,6},{5,13},{6,0},{7,15},{8,10},{9,17},{... | collective-permute-start | bytes 1572872 | tf_op jit(solution)/shard_map/ppermute | solution.py:448
  74.2 64.5 %copy-start.12 = (s32[1,16,8]{1,2,0:T(8,128)S(1)}, s32[1,16,8]{1,2,0:T(8,128)}, u32[]{:S(2)}) copy-start(s32[1,16,8]{1,2,0:T(8,128)} %param.30) | copy-start | bytes 1540
  74.2 67.2 %copy-start.7 = (s32[1,16]{1,0:T(1,128)S(1)}, s32[1,16]{1,0:T(1,128)}, u32[]{:S(2)}) copy-start(s32[1,16]{1,0:T(1,128)} %param.31) | copy-start | bytes 196
  74.5 13.4 %collective-permute-start.17 = (f16[8,64,128]{2,1,0:T(8,128)(2,1)S(1)}, f16[8,64,128]{2,1,0:T(8,128)(2,1)S(1)}, u32[]{:S(2)}, u32[]{:S(2)}) collective-permute-start(f16[8,64,128]{2,1,0:T(8,128)(2,1)S(1)} %get-tuple-element.96), channel_id=1, source_target_pairs={{0,16},{1,5},{2,18},{3,7},{4,20},{5,1},{6,22},{7,3},{8,24},{9,13},... | collective-permute-start | bytes 393224 | tf_op jit(solution)/shard_map/ppermute | solution.py:448
  75.6 12.3 %collective-permute-start.18 = (f16[8,64,128]{2,1,0:T(8,128)(2,1)S(1)}, f16[8,64,128]{2,1,0:T(8,128)(2,1)S(1)}, u32[]{:S(2)}, u32[]{:S(2)}) collective-permute-start(f16[8,64,128]{2,1,0:T(8,128)(2,1)S(1)} %get-tuple-element.98), channel_id=1, source_target_pairs={{0,24},{1,7},{2,26},{3,1},{4,28},{5,3},{6,30},{7,5},{8,0},{9,15},{... | collective-permute-start | bytes 393224 | tf_op jit(solution)/shard_map/ppermute | solution.py:448
  78.6 9.3 %collective-permute-start.19 = (f16[8,64,128]{2,1,0:T(8,128)(2,1)S(1)}, f16[8,64,128]{2,1,0:T(8,128)(2,1)S(1)}, u32[]{:S(2)}, u32[]{:S(2)}) collective-permute-start(f16[8,64,128]{2,1,0:T(8,128)(2,1)S(1)} %get-tuple-element.97), channel_id=1, source_target_pairs={{0,8},{1,3},{2,10},{3,5},{4,12},{5,7},{6,14},{7,1},{8,16},{9,11},{... | collective-permute-start | bytes 393224 | tf_op jit(solution)/shard_map/ppermute | solution.py:448
  78.6 18.4 %all-to-all-start.2 = ((bf16[32,32,128]{2,1,0:T(8,128)(2,1)}), bf16[32,32,128]{2,1,0:T(8,128)(2,1)S(1)}, u32[]{:S(2)}, u32[]{:S(2)}) async-start(bf16[32,32,128]{2,1,0:T(8,128)(2,1)} %screen_again.1), calls=%async_computation.2 | async-start | bytes 524288 | tf_op jit(solution)/shard_map/all_to_all | solution.py:535
  90.0 7.1 %collective-permute-start.20 = (bf16[1,64,128]{2,1,0:T(8,128)(2,1)S(1)}, bf16[1,64,128]{2,1,0:T(8,128)(2,1)S(1)}, u32[]{:S(2)}, u32[]{:S(2)}) collective-permute-start(bf16[1,64,128]{2,1,0:T(8,128)(2,1)S(1)} %get-tuple-element.73), channel_id=1, source_target_pairs={{0,32},{32,0},{64,96},{96,64},{128,160},{160,128},{192,224},{224,1... | collective-permute-start | bytes 49160 | tf_op jit(solution)/shard_map/ppermute | solution.py:522
  90.3 13.2 %collective-permute-start.22 = (bf16[1,64,128]{2,1,0:T(8,128)(2,1)S(1)}, bf16[1,64,128]{2,1,0:T(8,128)(2,1)S(1)}, u32[]{:S(2)}, u32[]{:S(2)}) collective-permute-start(bf16[1,64,128]{2,1,0:T(8,128)(2,1)S(1)} %get-tuple-element.77), channel_id=1, source_target_pairs={{0,96},{32,64},{64,32},{96,0},{128,224},{160,192},{192,160},{224,1... | collective-permute-start | bytes 49160 | tf_op jit(solution)/shard_map/ppermute | solution.py:522
  91.3 12.2 %collective-permute-start.23 = (bf16[1,64,128]{2,1,0:T(8,128)(2,1)S(1)}, bf16[1,64,128]{2,1,0:T(8,128)(2,1)S(1)}, u32[]{:S(2)}, u32[]{:S(2)}) collective-permute-start(bf16[1,64,128]{2,1,0:T(8,128)(2,1)S(1)} %get-tuple-element.78), channel_id=1, source_target_pairs={{0,128},{32,160},{64,192},{96,224},{128,0},{160,32},{192,64},{224,... | collective-permute-start | bytes 49160 | tf_op jit(solution)/shard_map/ppermute | solution.py:522
  93.5 10.0 %collective-permute-start.24 = (bf16[1,64,128]{2,1,0:T(8,128)(2,1)S(1)}, bf16[1,64,128]{2,1,0:T(8,128)(2,1)S(1)}, u32[]{:S(2)}, u32[]{:S(2)}) collective-permute-start(bf16[1,64,128]{2,1,0:T(8,128)(2,1)S(1)} %get-tuple-element.79), channel_id=1, source_target_pairs={{0,160},{32,128},{64,224},{96,192},{128,32},{160,0},{192,96},{224,... | collective-permute-start | bytes 49160 | tf_op jit(solution)/shard_map/ppermute | solution.py:522
  95.6 7.9 %collective-permute-start.25 = (bf16[1,64,128]{2,1,0:T(8,128)(2,1)S(1)}, bf16[1,64,128]{2,1,0:T(8,128)(2,1)S(1)}, u32[]{:S(2)}, u32[]{:S(2)}) collective-permute-start(bf16[1,64,128]{2,1,0:T(8,128)(2,1)S(1)} %get-tuple-element.80), channel_id=1, source_target_pairs={{0,192},{32,224},{64,128},{96,160},{128,64},{160,96},{192,0},{224,... | collective-permute-start | bytes 49160 | tf_op jit(solution)/shard_map/ppermute | solution.py:522
  97.0 3.9 %collective-permute-start.21 = (bf16[1,64,128]{2,1,0:T(8,128)(2,1)S(1)}, bf16[1,64,128]{2,1,0:T(8,128)(2,1)S(1)}, u32[]{:S(2)}, u32[]{:S(2)}) collective-permute-start(bf16[1,64,128]{2,1,0:T(8,128)(2,1)S(1)} %get-tuple-element.76), channel_id=1, source_target_pairs={{0,64},{32,96},{64,0},{96,32},{128,192},{160,224},{192,128},{224,1... | collective-permute-start | bytes 49160 | tf_op jit(solution)/shard_map/ppermute | solution.py:522
  100.9 3.8 %collective-permute-start.26 = (bf16[1,64,128]{2,1,0:T(8,128)(2,1)S(1)}, bf16[1,64,128]{2,1,0:T(8,128)(2,1)S(1)}, u32[]{:S(2)}, u32[]{:S(2)}) collective-permute-start(bf16[1,64,128]{2,1,0:T(8,128)(2,1)S(1)} %get-tuple-element.81), channel_id=1, source_target_pairs={{0,224},{32,192},{64,160},{96,128},{128,96},{160,64},{192,32},{224... | collective-permute-start | bytes 49160 | tf_op jit(solution)/shard_map/ppermute | solution.py:522
  104.7 11.2 %collective-permute-start.27 = (bf16[8,64,128]{2,1,0:T(8,128)(2,1)S(1)}, bf16[8,64,128]{2,1,0:T(8,128)(2,1)S(1)}, u32[]{:S(2)}, u32[]{:S(2)}) collective-permute-start(bf16[8,64,128]{2,1,0:T(8,128)(2,1)S(1)} %constant_dynamic-update-slice_fusion.4), channel_id=1, source_target_pairs={{0,8},{1,3},{2,10},{3,5},{4,12},{5,7},{6,14},{7,1},{8,16},{9,11},{... | collective-permute-start | bytes 393224 | tf_op jit(solution)/shard_map/ppermute | solution.py:448
  106.2 9.7 %collective-permute-start.28 = (bf16[8,64,128]{2,1,0:T(8,128)(2,1)S(1)}, bf16[8,64,128]{2,1,0:T(8,128)(2,1)S(1)}, u32[]{:S(2)}, u32[]{:S(2)}) collective-permute-start(bf16[8,64,128]{2,1,0:T(8,128)(2,1)S(1)} %constant_dynamic-update-slice_fusion.4), channel_id=1, source_target_pairs={{0,16},{1,5},{2,18},{3,7},{4,20},{5,1},{6,22},{7,3},{8,24},{9,13},... | collective-permute-start | bytes 393224 | tf_op jit(solution)/shard_map/ppermute | solution.py:448
  108.6 7.4 %collective-permute-start.29 = (bf16[8,64,128]{2,1,0:T(8,128)(2,1)S(1)}, bf16[8,64,128]{2,1,0:T(8,128)(2,1)S(1)}, u32[]{:S(2)}, u32[]{:S(2)}) collective-permute-start(bf16[8,64,128]{2,1,0:T(8,128)(2,1)S(1)} %constant_dynamic-update-slice_fusion.4), channel_id=1, source_target_pairs={{0,24},{1,7},{2,26},{3,1},{4,28},{5,3},{6,30},{7,5},{8,0},{9,15},{... | collective-permute-start | bytes 393224 | tf_op jit(solution)/shard_map/ppermute | solution.py:448
  109.9 31.5 %all-to-all-start.3 = ((f32[8,192,128]{2,1,0:T(8,128)}), f32[8,192,128]{2,1,0:T(8,128)S(1)}, u32[]{:S(2)}, u32[]{:S(2)}) async-start(f32[8,192,128]{2,1,0:T(8,128)} %get-tuple-element.88), calls=%async_computation.3 | async-start | bytes 1572864 | tf_op jit(solution)/shard_map/all_to_all | solution.py:531
  116.0 20.3 %collective-permute-start.30 = (bf16[32,64,128]{2,1,0:T(8,128)(2,1)S(1)}, bf16[32,64,128]{2,1,0:T(8,128)(2,1)S(1)}, u32[]{:S(2)}, u32[]{:S(2)}) collective-permute-start(bf16[32,64,128]{2,1,0:T(8,128)(2,1)S(1)} %constant_dynamic-update-slice_fusion.12.rest_0_), channel_id=1, source_target_pairs={{0,2},{1,9},{2,4},{3,11},{4,6},{5,13},{6,0},{7,15},{8,10},{9,17},{... | collective-permute-start | bytes 1572872 | tf_op jit(solution)/shard_map/ppermute | solution.py:448
  117.3 19.0 %collective-permute-start.31 = (bf16[32,64,128]{2,1,0:T(8,128)(2,1)S(1)}, bf16[32,64,128]{2,1,0:T(8,128)(2,1)S(1)}, u32[]{:S(2)}, u32[]{:S(2)}) collective-permute-start(bf16[32,64,128]{2,1,0:T(8,128)(2,1)S(1)} %constant_dynamic-update-slice_fusion.12.rest_0_), channel_id=1, source_target_pairs={{0,4},{1,17},{2,6},{3,19},{4,0},{5,21},{6,2},{7,23},{8,12},{9,25},... | collective-permute-start | bytes 1572872 | tf_op jit(solution)/shard_map/ppermute | solution.py:448
  119.8 16.6 %collective-permute-start.32 = (bf16[32,64,128]{2,1,0:T(8,128)(2,1)S(1)}, bf16[32,64,128]{2,1,0:T(8,128)(2,1)S(1)}, u32[]{:S(2)}, u32[]{:S(2)}) collective-permute-start(bf16[32,64,128]{2,1,0:T(8,128)(2,1)S(1)} %constant_dynamic-update-slice_fusion.12.rest_0_), channel_id=1, source_target_pairs={{0,6},{1,25},{2,0},{3,27},{4,2},{5,29},{6,4},{7,31},{8,14},{9,1},{... | collective-permute-start | bytes 1572872 | tf_op jit(solution)/shard_map/ppermute | solution.py:448
  131.2 9.5 %collective-permute-start.33 = (bf16[32,64,128]{2,1,0:T(8,128)(2,1)S(1)}, bf16[32,64,128]{2,1,0:T(8,128)(2,1)S(1)}, u32[]{:S(2)}, u32[]{:S(2)}) collective-permute-start(bf16[32,64,128]{2,1,0:T(8,128)(2,1)S(1)} %constant_dynamic-update-slice_fusion.12.rest_0_), channel_id=1, source_target_pairs={{0,1},{1,0},{2,3},{3,2},{4,5},{5,4},{6,7},{7,6},{8,9},{9,8},{10,11... | collective-permute-start | bytes 1572872 | tf_op jit(solution)/shard_map/ppermute | solution.py:453
  136.3 4.4 %collective-permute-start.34 = (bf16[32,64,128]{2,1,0:T(8,128)(2,1)S(1)}, bf16[32,64,128]{2,1,0:T(8,128)(2,1)}, u32[]{:S(2)}, u32[]{:S(2)}) collective-permute-start(bf16[32,64,128]{2,1,0:T(8,128)(2,1)S(1)} %collective-permute-done.30.rest_1_), channel_id=1, source_target_pairs={{0,1},{1,0},{2,3},{3,2},{4,5},{5,4},{6,7},{7,6},{8,9},{9,8},{10,11... | collective-permute-start | bytes 1572872 | tf_op jit(solution)/shard_map/ppermute | solution.py:453
  138.2 2.5 %collective-permute-start.35 = (bf16[32,64,128]{2,1,0:T(8,128)(2,1)S(1)}, bf16[32,64,128]{2,1,0:T(8,128)(2,1)}, u32[]{:S(2)}, u32[]{:S(2)}) collective-permute-start(bf16[32,64,128]{2,1,0:T(8,128)(2,1)S(1)} %collective-permute-done.31.rest_2_), channel_id=1, source_target_pairs={{0,1},{1,0},{2,3},{3,2},{4,5},{5,4},{6,7},{7,6},{8,9},{9,8},{10,11... | collective-permute-start | bytes 1572872 | tf_op jit(solution)/shard_map/ppermute | solution.py:453
  138.2 3.2 %collective-permute-start.36 = (bf16[32,64,128]{2,1,0:T(8,128)(2,1)S(1)}, bf16[32,64,128]{2,1,0:T(8,128)(2,1)}, u32[]{:S(2)}, u32[]{:S(2)}) collective-permute-start(bf16[32,64,128]{2,1,0:T(8,128)(2,1)S(1)} %collective-permute-done.32.rest_3_), channel_id=1, source_target_pairs={{0,1},{1,0},{2,3},{3,2},{4,5},{5,4},{6,7},{7,6},{8,9},{9,8},{10,11... | collective-permute-start | bytes 1572872 | tf_op jit(solution)/shard_map/ppermute | solution.py:453
  (5 other events, 110.9 us)

commit v5 on v4

--- a/solution.py
+++ b/solution.py
@@ -560,7 +560,7 @@
     w_first, token = weights(lists_first[0], loads_first[0], shift_first[0], screen, "weights_first")
     line, *own = own
     *own, token = tie(*own, token)
-    slots = color_slots(lists_first[0], lists_first[0] % BINS) + token[0, 0]
+    slots = color_slots(lists_first[0], lists_first[0] % BINS) + token[0:1, 0:LBLK]
     parts = first_render(slots, loads_first[0], w_first, target[0], swapped([line] + own))
     line, geometry = scatter_far(parts, geometry)
     screen = screen_again(cameras_second[0], across_view(geometry))
@@ -576,7 +576,7 @@
     line, *own = gather_plane(gather_line(colors))
     *own, token = tie(*own, token)
     blocks = swapped([line] + own)
-    slots = color_slots(lists_second[0], place_of(lists_second[0] % BINS)) + token[0, 0]
+    slots = color_slots(lists_second[0], place_of(lists_second[0] % BINS)) + token[0:1, 0:LBLK]
     image, new_features, new_first, new_second = second_render(
         slots, loads_second[0], w_second, packed, blocks
     )

time: 150 us -> 149 us (level); the launches traced: 148 us -> 149 us
  Pallas kernels: 42.3 us -> 44 us
    ppermute x12, starting transfers between devices: 12.5 us -> 10 us  [swap_core(): return lax.ppermute(value, 'tile', pairs)]
    slice x2 -> x0, local copies, waits for them, and re-layouts: 2.39 us -> none  [the longest x1 1.2 us: local(): token[0, 0]]
    ppermute x18, starting transfers between devices: 25.2 us -> 26.7 us  [shift_by(): return lax.ppermute(value, 'tile', pairs)]
  transfers between devices with their start and end apart: 40 -> 40, of which waited for: 8 -> 10; matrix products, arithmetic and copies ran while one was open for 4% -> 2% of each run, Pallas kernels for 16% -> 17%
where the time goes in v5:
time: 149 us
  starting transfers between devices  69.7 us (47%)
  Pallas kernels  44 us (30%)
  blocking collectives  16.3 us (11%)
  waiting for transfers between devices  13.9 us (9%)
  local copies, waits for them, and re-layouts  2.79 us (2%)
    ppermute x18, starting transfers between devices, shift_by(): return lax.ppermute(value, 'tile', pairs)  26.7 us
    pallas_call x2, Pallas kernels, weights(): pl.pallas_call(weights_kernel, out_shape=(jax.ShapeDtypeStruct((TILES, LB...  21.5 us
    all_to_all x1, blocking collectives, across_view(): lax.all_to_all(value, 'view', split_axis=0, concat_axis=0, tiled=True)  16.3 us
    all_to_all x2, starting transfers between devices, across_tile(): lax.all_to_all(value, 'tile', split_axis=0, concat_axis=0, tiled=True)  16.1 us
    ppermute x7, starting transfers between devices, exchange_views(): got[r] = lax.ppermute(value, 'view', [(v, v ^ r) for v in range(N_VIEW)])  10.7 us
    pallas_call x1, Pallas kernels, first_render(): pl.pallas_call(first_kernel, out_shape=(jax.ShapeDtypeStruct((32, C, GB),...  10.1 us
    ppermute x12, starting transfers between devices, swap_core(): return lax.ppermute(value, 'tile', pairs)  10 us
    pallas_call x1, Pallas kernels, second_render(): pl.pallas_call(second_kernel, out_shape=(jax.ShapeDtypeStruct((TILES, C,...  7.01 us
  transfers between devices with their start and end apart: 40, of which 10 were waited for; matrix products, arithmetic and copies ran while one was open for 2% of the time, Pallas kernels for 17%

profile of v5, /device:TPU:1, one launch (start us, length us, event | category | flops | bytes accessed | tf_op | source)
XLA Modules:
  0.0 149.4 jit_solution(12761426255704706609)
XLA Ops:
  0.7 2.0 %prep.1 = (bf16[8,64,128]{2,1,0:T(8,128)(2,1)}, bf16[32,32,128]{2,1,0:T(8,128)(2,1)}, f32[8,8,128]{2,1,0:T(8,128)}) custom-call(f32[1,2,4]{2,1,0:T(2,128)} %camera_hbm.1, s32[8]{0:T(128)} %owner.1, f32[8,64,128]{2,1,0:T(8,128)} %feat.1, f32[3,8,128]{2,1,0:T(8,128)} %bitcast.29, f32[8,128]{1,0:T(8,128)} %scales_hbm.1, f32[8,128]{1,0:T(8,128)} %opacity_hbm.1), custom_call_target="tpu_custom_call" | custom-call | tf_op jit(solution)/shard_map/prep/pallas_call | solution.py:118
  2.7 2.2 %collective-permute-start = (bf16[8,64,128]{2,1,0:T(8,128)(2,1)}, bf16[8,64,128]{2,1,0:T(8,128)(2,1)S(1)}, u32[]{:S(2)}, u32[]{:S(2)}) collective-permute-start(bf16[8,64,128]{2,1,0:T(8,128)(2,1)} %get-tuple-element.50), channel_id=1, source_target_pairs={{0,8},{1,3},{2,10},{3,5},{4,12},{5,7},{6,14},{7,1},{8,16},{9,11},{... | collective-permute-start | bytes 393224 | tf_op jit(solution)/shard_map/ppermute | solution.py:448
  4.9 2.6 %collective-permute-start.1 = (bf16[8,64,128]{2,1,0:T(8,128)(2,1)}, bf16[8,64,128]{2,1,0:T(8,128)(2,1)S(1)}, u32[]{:S(2)}, u32[]{:S(2)}) collective-permute-start(bf16[8,64,128]{2,1,0:T(8,128)(2,1)} %get-tuple-element.50), channel_id=1, source_target_pairs={{0,16},{1,5},{2,18},{3,7},{4,20},{5,1},{6,22},{7,3},{8,24},{9,13},... | collective-permute-start | bytes 393224 | tf_op jit(solution)/shard_map/ppermute | solution.py:448
  7.5 1.1 collective-permute-start.2
  8.6 6.0 %all-to-all-start = ((bf16[32,32,128]{2,1,0:T(8,128)(2,1)}), bf16[32,32,128]{2,1,0:T(8,128)(2,1)S(1)}, u32[]{:S(2)}, u32[]{:S(2)}) async-start(bf16[32,32,128]{2,1,0:T(8,128)(2,1)} %get-tuple-element.51), calls=%async_computation | async-start | bytes 524288 | tf_op jit(solution)/shard_map/all_to_all | solution.py:535
  14.6 0.9 constant_dynamic-update-slice_fusion.3
  15.6 1.5 collective-permute-start.3
  17.1 2.4 %collective-permute-start.4 = (bf16[32,64,128]{2,1,0:T(8,128)(2,1)S(1)}, bf16[32,64,128]{2,1,0:T(8,128)(2,1)S(1)}, u32[]{:S(2)}, u32[]{:S(2)}) collective-permute-start(bf16[32,64,128]{2,1,0:T(8,128)(2,1)S(1)} %constant_dynamic-update-slice_fusion.rest_0_), channel_id=1, source_target_pairs={{0,4},{1,17},{2,6},{3,19},{4,0},{5,21},{6,2},{7,23},{8,12},{9,25},... | collective-permute-start | bytes 1572872 | tf_op jit(solution)/shard_map/ppermute | solution.py:448
  19.5 4.4 %all-to-all-done.screen_hbm = bf16[32,32,128]{2,1,0:T(8,128)(2,1)S(1)} async-done(((bf16[32,32,128]{2,1,0:T(8,128)(2,1)}), bf16[32,32,128]{2,1,0:T(8,128)(2,1)S(1)}, u32[]{:S(2)}, u32[]{:S(2)}) %all-to-all-start) | async-done | bytes 262176 | tf_op jit(solution)/shard_map/all_to_all | solution.py:535
  23.9 0.5 collective-permute-start.5
  24.4 0.8 collective-permute-start.6
  25.2 11.1 %weights_first.1 = (bf16[16,8,128,256]{3,2,1,0:T(8,128)(2,1)}, s32[8,128]{1,0:T(8,128)}) custom-call(s32[8,16]{1,0:T(8,128)} %bitcast.30, s32[16]{0:T(128)} %bitcast.25, f32[2,16]{1,0:T(2,128)} %bitcast.35, bf16[32,32,128]{2,1,0:T(8,128)(2,1)} %copy-done.9), custom_call_target="tpu_custom_call" | custom-call | flops 58720256 | bytes 10000000 | tf_op jit(solution)/shard_map/weights_first/pallas_call | solution.py:258
  37.2 0.7 slice_bitcast_fusion.1
  37.9 0.6 collective-permute-done.7.rest_5_
  38.5 0.7 collective-permute-done.8.rest_6_
  39.3 0.7 collective-permute-done.9.rest_7_
  40.0 10.1 %first_render.1 = (f32[32,64,128]{2,1,0:T(8,128)S(1)}, f32[32,64,128]{2,1,0:T(8,128)S(1)}, f32[32,64,128]{2,1,0:T(8,128)S(1)}, f32[32,64,128]{2,1,0:T(8,128)S(1)...) custom-call(s32[16,8]{1,0:T(8,128)S(1)} %fusion.16.slots, ...), custom_call_target="tpu_custom_call" | custom-call | flops 1073741824 | bytes 25000000 | tf_op jit(solution)/shard_map/first_render/pallas_call | solution.py:348
  51.3 1.6 %collective-permute-done.11 = f32[32,64,128]{2,1,0:T(8,128)S(1)} collective-permute-done((f32[32,64,128]{2,1,0:T(8,128)S(1)}, f32[32,64,128]{2,1,0:T(8,128)S(1)}, u32[]{:S(2)}, u32[]{:S(2)}) %collective-permute-start.11) | collective-permute-done | bytes 1048608 | tf_op jit(solution)/shard_map/ppermute | solution.py:453
  53.2 3.2 %collective-permute-start.12 = (f16[32,64,128]{2,1,0:T(8,128)(2,1)S(1)}, f16[32,64,128]{2,1,0:T(8,128)(2,1)S(1)}, u32[]{:S(2)}, u32[]{:S(2)}) collective-permute-start(f16[32,64,128]{2,1,0:T(8,128)(2,1)S(1)} %add_convert_fusion.2), channel_id=1, source_target_pairs={{0,4},{1,17},{2,6},{3,19},{4,0},{5,21},{6,2},{7,23},{8,12},{9,25},... | collective-permute-start | bytes 1572872 | tf_op jit(solution)/shard_map/ppermute | solution.py:448
  56.9 1.5 %collective-permute-start.16 = (f16[32,64,128]{2,1,0:T(8,128)(2,1)S(1)}, f16[32,64,128]{2,1,0:T(8,128)(2,1)S(1)}, u32[]{:S(2)}, u32[]{:S(2)}) collective-permute-start(f16[32,64,128]{2,1,0:T(8,128)(2,1)S(1)} %add_convert_fusion), channel_id=1, source_target_pairs={{0,2},{1,9},{2,4},{3,11},{4,6},{5,13},{6,0},{7,15},{8,10},{9,17},{... | collective-permute-start | bytes 1572872 | tf_op jit(solution)/shard_map/ppermute | solution.py:448
  58.4 16.3 %all_to_all.20.geometry = f32[8,8,128]{2,1,0:T(8,128)S(1)} all-to-all(f32[8,8,128]{2,1,0:T(8,128)S(1)} %copy-done.10), channel_id=1, replica_groups=mesh['view'=8,'tile'=32] {'view'}, dimensions={0} | all-to-all | bytes 65536 | tf_op jit(solution)/shard_map/all_to_all | solution.py:531
  74.7 1.4 screen_again.1
  77.0 1.4 collective-permute-start.18
  78.5 10.1 %all-to-all-start.2 = ((bf16[32,32,128]{2,1,0:T(8,128)(2,1)}), bf16[32,32,128]{2,1,0:T(8,128)(2,1)S(1)}, u32[]{:S(2)}, u32[]{:S(2)}) async-start(bf16[32,32,128]{2,1,0:T(8,128)(2,1)} %screen_again.1), calls=%async_computation.2 | async-start | bytes 524288 | tf_op jit(solution)/shard_map/all_to_all | solution.py:535
  88.8 1.9 %adam.1 = (bf16[1,64,128]{2,1,0:T(8,128)(2,1)S(1)}, bf16[1,64,128]{2,1,0:T(8,128)(2,1)S(1)}, bf16[1,64,128]{2,1,0:T(8,128)(2,1)S(1)}, bf16[1,64,128]{2,1,0:T(8,1...) custom-call(s32[8]{0:T(128)S(1)} %copy-done.4, ...), custom_call_target="tpu_custom_call" | custom-call | tf_op jit(solution)/shard_map/adam/pallas_call | solution.py:423
  91.0 1.0 collective-permute-start.22
  92.1 2.2 %collective-permute-start.23 = (bf16[1,64,128]{2,1,0:T(8,128)(2,1)S(1)}, bf16[1,64,128]{2,1,0:T(8,128)(2,1)S(1)}, u32[]{:S(2)}, u32[]{:S(2)}) collective-permute-start(bf16[1,64,128]{2,1,0:T(8,128)(2,1)S(1)} %get-tuple-element.78), channel_id=1, source_target_pairs={{0,128},{32,160},{64,192},{96,224},{128,0},{160,32},{192,64},{224,... | collective-permute-start | bytes 49160 | tf_op jit(solution)/shard_map/ppermute | solution.py:522
  94.2 2.1 %collective-permute-start.24 = (bf16[1,64,128]{2,1,0:T(8,128)(2,1)S(1)}, bf16[1,64,128]{2,1,0:T(8,128)(2,1)S(1)}, u32[]{:S(2)}, u32[]{:S(2)}) collective-permute-start(bf16[1,64,128]{2,1,0:T(8,128)(2,1)S(1)} %get-tuple-element.79), channel_id=1, source_target_pairs={{0,160},{32,128},{64,224},{96,192},{128,32},{160,0},{192,96},{224,... | collective-permute-start | bytes 49160 | tf_op jit(solution)/shard_map/ppermute | solution.py:522
  96.4 1.4 collective-permute-start.25
  97.8 1.2 collective-permute-start.21
  99.0 2.7 %collective-permute-done.21 = bf16[1,64,128]{2,1,0:T(8,128)(2,1)S(1)} collective-permute-done((bf16[1,64,128]{2,1,0:T(8,128)(2,1)S(1)}, bf16[1,64,128]{2,1,0:T(8,128)(2,1)S(1)}, u32[]{:S(2)}, u32[]{:S(2)}) %collective-permute-start.21) | collective-permute-done | bytes 16416 | tf_op jit(solution)/shard_map/ppermute | solution.py:522
  101.7 2.5 %collective-permute-start.26 = (bf16[1,64,128]{2,1,0:T(8,128)(2,1)S(1)}, bf16[1,64,128]{2,1,0:T(8,128)(2,1)S(1)}, u32[]{:S(2)}, u32[]{:S(2)}) collective-permute-start(bf16[1,64,128]{2,1,0:T(8,128)(2,1)S(1)} %get-tuple-element.81), channel_id=1, source_target_pairs={{0,224},{32,192},{64,160},{96,128},{128,96},{160,64},{192,32},{224... | collective-permute-start | bytes 49160 | tf_op jit(solution)/shard_map/ppermute | solution.py:522
  104.3 1.2 collective-permute-done.26
  105.5 1.5 %collective-permute-start.27 = (bf16[8,64,128]{2,1,0:T(8,128)(2,1)S(1)}, bf16[8,64,128]{2,1,0:T(8,128)(2,1)S(1)}, u32[]{:S(2)}, u32[]{:S(2)}) collective-permute-start(bf16[8,64,128]{2,1,0:T(8,128)(2,1)S(1)} %constant_dynamic-update-slice_fusion.4), channel_id=1, source_target_pairs={{0,8},{1,3},{2,10},{3,5},{4,12},{5,7},{6,14},{7,1},{8,16},{9,11},{... | collective-permute-start | bytes 393224 | tf_op jit(solution)/shard_map/ppermute | solution.py:448
  107.0 2.4 %collective-permute-start.28 = (bf16[8,64,128]{2,1,0:T(8,128)(2,1)S(1)}, bf16[8,64,128]{2,1,0:T(8,128)(2,1)S(1)}, u32[]{:S(2)}, u32[]{:S(2)}) collective-permute-start(bf16[8,64,128]{2,1,0:T(8,128)(2,1)S(1)} %constant_dynamic-update-slice_fusion.4), channel_id=1, source_target_pairs={{0,16},{1,5},{2,18},{3,7},{4,20},{5,1},{6,22},{7,3},{8,24},{9,13},... | collective-permute-start | bytes 393224 | tf_op jit(solution)/shard_map/ppermute | solution.py:448
  109.4 1.3 collective-permute-start.29
  110.7 6.0 %all-to-all-start.3 = ((f32[8,192,128]{2,1,0:T(8,128)}), f32[8,192,128]{2,1,0:T(8,128)S(1)}, u32[]{:S(2)}, u32[]{:S(2)}) async-start(f32[8,192,128]{2,1,0:T(8,128)} %get-tuple-element.88), calls=%async_computation.3 | async-start | bytes 1572864 | tf_op jit(solution)/shard_map/all_to_all | solution.py:531
  116.8 1.3 collective-permute-start.30
  118.1 2.5 %collective-permute-start.31 = (bf16[32,64,128]{2,1,0:T(8,128)(2,1)S(1)}, bf16[32,64,128]{2,1,0:T(8,128)(2,1)S(1)}, u32[]{:S(2)}, u32[]{:S(2)}) collective-permute-start(bf16[32,64,128]{2,1,0:T(8,128)(2,1)S(1)} %constant_dynamic-update-slice_fusion.12.rest_0_), channel_id=1, source_target_pairs={{0,4},{1,17},{2,6},{3,19},{4,0},{5,21},{6,2},{7,23},{8,12},{9,25},... | collective-permute-start | bytes 1572872 | tf_op jit(solution)/shard_map/ppermute | solution.py:448
  120.5 1.1 collective-permute-start.32
  121.6 10.4 %weights_second.1 = (bf16[16,8,128,256]{3,2,1,0:T(8,128)(2,1)}, s32[8,128]{1,0:T(8,128)}) custom-call(s32[8,16]{1,0:T(8,128)} %bitcast.32, s32[16]{0:T(128)} %bitcast.27, f32[2,16]{1,0:T(2,128)} %bitcast.36, bf16[32,32,128]{2,1,0:T(8,128)(2,1)} %copy-done.8), custom_call_target="tpu_custom_call" | custom-call | flops 58720256 | bytes 10000000 | tf_op jit(solution)/shard_map/weights_second/pallas_call | solution.py:258
  132.0 5.3 %collective-permute-start.33 = (bf16[32,64,128]{2,1,0:T(8,128)(2,1)S(1)}, bf16[32,64,128]{2,1,0:T(8,128)(2,1)S(1)}, u32[]{:S(2)}, u32[]{:S(2)}) collective-permute-start(bf16[32,64,128]{2,1,0:T(8,128)(2,1)S(1)} %constant_dynamic-update-slice_fusion.12.rest_0_), channel_id=1, source_target_pairs={{0,1},{1,0},{2,3},{3,2},{4,5},{5,4},{6,7},{7,6},{8,9},{9,8},{10,11... | collective-permute-start | bytes 1572872 | tf_op jit(solution)/shard_map/ppermute | solution.py:453
  137.3 1.7 %collective-permute-start.34 = (bf16[32,64,128]{2,1,0:T(8,128)(2,1)S(1)}, bf16[32,64,128]{2,1,0:T(8,128)(2,1)}, u32[]{:S(2)}, u32[]{:S(2)}) collective-permute-start(bf16[32,64,128]{2,1,0:T(8,128)(2,1)S(1)} %collective-permute-done.30.rest_1_), channel_id=1, source_target_pairs={{0,1},{1,0},{2,3},{3,2},{4,5},{5,4},{6,7},{7,6},{8,9},{9,8},{10,11... | collective-permute-start | bytes 1572872 | tf_op jit(solution)/shard_map/ppermute | solution.py:453
  139.0 0.5 collective-permute-start.36
  139.6 0.7 slice_bitcast_fusion
  140.7 0.7 collective-permute-done.35.rest_6_
  141.4 0.7 collective-permute-done.36.rest_7_
  142.2 7.0 %second_render.1 = (f32[16,64,256]{2,1,0:T(8,128)}, f32[8,64,128]{2,1,0:T(8,128)}, f32[8,64,128]{2,1,0:T(8,128)}, f32[8,64,128]{2,1,0:T(8,128)}) custom-call(s32[16,8]{1,0:T(8,128)S(1)} %fusion.8.slots, s32[16]{0:T(128)S(1)} %bitcast.28, bf16[16,8,128,256]{3,2,1,0:T(8,128)(2,1)} %get-tuple-element.87.w_hbm, f32[8,192,128]{2,1,0:T(8,128)S(1)} %all-to-all-done.3.packed, ...), custom_call_target="tpu_custom_call" | custom-call | flops 536870912 | bytes 14000000 | tf_op jit(solution)/shard_map/second_render/pallas_call | solution.py:386
  (95 shorter events, 4.6 us)
Async XLA Ops:
  0.6 39.4 %copy-start.6 = (s32[1,16]{1,0:T(1,128)S(1)}, s32[1,16]{1,0:T(1,128)}, u32[]{:S(2)}) copy-start(s32[1,16]{1,0:T(1,128)} %param.25) | copy-start | bytes 196
  0.7 39.4 %copy-start.1 = (bf16[1,16,64,256]{3,2,1,0:T(8,128)(2,1)S(1)}, bf16[1,16,64,256]{3,2,1,0:T(8,128)(2,1)}, u32[]{:S(2)}) copy-start(bf16[1,16,64,256]{3,2,1,0:T(8,128)(2,1)} %param.26) | copy-start | bytes 1572868
  2.7 12.8 %collective-permute-start = (bf16[8,64,128]{2,1,0:T(8,128)(2,1)}, bf16[8,64,128]{2,1,0:T(8,128)(2,1)S(1)}, u32[]{:S(2)}, u32[]{:S(2)}) collective-permute-start(bf16[8,64,128]{2,1,0:T(8,128)(2,1)} %get-tuple-element.50), channel_id=1, source_target_pairs={{0,8},{1,3},{2,10},{3,5},{4,12},{5,7},{6,14},{7,1},{8,16},{9,11},{... | collective-permute-start | bytes 393224 | tf_op jit(solution)/shard_map/ppermute | solution.py:448
  4.9 10.7 %collective-permute-start.1 = (bf16[8,64,128]{2,1,0:T(8,128)(2,1)}, bf16[8,64,128]{2,1,0:T(8,128)(2,1)S(1)}, u32[]{:S(2)}, u32[]{:S(2)}) collective-permute-start(bf16[8,64,128]{2,1,0:T(8,128)(2,1)} %get-tuple-element.50), channel_id=1, source_target_pairs={{0,16},{1,5},{2,18},{3,7},{4,20},{5,1},{6,22},{7,3},{8,24},{9,13},... | collective-permute-start | bytes 393224 | tf_op jit(solution)/shard_map/ppermute | solution.py:448
  7.5 8.1 %collective-permute-start.2 = (bf16[8,64,128]{2,1,0:T(8,128)(2,1)}, bf16[8,64,128]{2,1,0:T(8,128)(2,1)S(1)}, u32[]{:S(2)}, u32[]{:S(2)}) collective-permute-start(bf16[8,64,128]{2,1,0:T(8,128)(2,1)} %get-tuple-element.50), channel_id=1, source_target_pairs={{0,24},{1,7},{2,26},{3,1},{4,28},{5,3},{6,30},{7,5},{8,0},{9,15},{... | collective-permute-start | bytes 393224 | tf_op jit(solution)/shard_map/ppermute | solution.py:448
  8.6 15.3 %all-to-all-start = ((bf16[32,32,128]{2,1,0:T(8,128)(2,1)}), bf16[32,32,128]{2,1,0:T(8,128)(2,1)S(1)}, u32[]{:S(2)}, u32[]{:S(2)}) async-start(bf16[32,32,128]{2,1,0:T(8,128)(2,1)} %get-tuple-element.51), calls=%async_computation | async-start | bytes 524288 | tf_op jit(solution)/shard_map/all_to_all | solution.py:535
  15.6 20.7 %collective-permute-start.3 = (bf16[32,64,128]{2,1,0:T(8,128)(2,1)S(1)}, bf16[32,64,128]{2,1,0:T(8,128)(2,1)S(1)}, u32[]{:S(2)}, u32[]{:S(2)}) collective-permute-start(bf16[32,64,128]{2,1,0:T(8,128)(2,1)S(1)} %constant_dynamic-update-slice_fusion.rest_0_), channel_id=1, source_target_pairs={{0,2},{1,9},{2,4},{3,11},{4,6},{5,13},{6,0},{7,15},{8,10},{9,17},{... | collective-permute-start | bytes 1572872 | tf_op jit(solution)/shard_map/ppermute | solution.py:448
  17.1 19.3 %collective-permute-start.4 = (bf16[32,64,128]{2,1,0:T(8,128)(2,1)S(1)}, bf16[32,64,128]{2,1,0:T(8,128)(2,1)S(1)}, u32[]{:S(2)}, u32[]{:S(2)}) collective-permute-start(bf16[32,64,128]{2,1,0:T(8,128)(2,1)S(1)} %constant_dynamic-update-slice_fusion.rest_0_), channel_id=1, source_target_pairs={{0,4},{1,17},{2,6},{3,19},{4,0},{5,21},{6,2},{7,23},{8,12},{9,25},... | collective-permute-start | bytes 1572872 | tf_op jit(solution)/shard_map/ppermute | solution.py:448
  23.9 12.5 %collective-permute-start.5 = (bf16[32,64,128]{2,1,0:T(8,128)(2,1)S(1)}, bf16[32,64,128]{2,1,0:T(8,128)(2,1)S(1)}, u32[]{:S(2)}, u32[]{:S(2)}) collective-permute-start(bf16[32,64,128]{2,1,0:T(8,128)(2,1)S(1)} %constant_dynamic-update-slice_fusion.rest_0_), channel_id=1, source_target_pairs={{0,6},{1,25},{2,0},{3,27},{4,2},{5,29},{6,4},{7,31},{8,14},{9,1},{... | collective-permute-start | bytes 1572872 | tf_op jit(solution)/shard_map/ppermute | solution.py:448
  24.4 13.5 %collective-permute-start.6 = (bf16[32,64,128]{2,1,0:T(8,128)(2,1)S(1)}, bf16[32,64,128]{2,1,0:T(8,128)(2,1)S(1)}, u32[]{:S(2)}, u32[]{:S(2)}) collective-permute-start(bf16[32,64,128]{2,1,0:T(8,128)(2,1)S(1)} %constant_dynamic-update-slice_fusion.rest_0_), channel_id=1, source_target_pairs={{0,1},{1,0},{2,3},{3,2},{4,5},{5,4},{6,7},{7,6},{8,9},{9,8},{10,11... | collective-permute-start | bytes 1572872 | tf_op jit(solution)/shard_map/ppermute | solution.py:453
  36.4 2.1 %collective-permute-start.7 = (bf16[32,64,128]{2,1,0:T(8,128)(2,1)S(1)}, bf16[32,64,128]{2,1,0:T(8,128)(2,1)}, u32[]{:S(2)}, u32[]{:S(2)}) collective-permute-start(bf16[32,64,128]{2,1,0:T(8,128)(2,1)S(1)} %collective-permute-done.3.rest_1_), channel_id=1, source_target_pairs={{0,1},{1,0},{2,3},{3,2},{4,5},{5,4},{6,7},{7,6},{8,9},{9,8},{10,11... | collective-permute-start | bytes 1572872 | tf_op jit(solution)/shard_map/ppermute | solution.py:453
  36.5 2.8 %collective-permute-start.8 = (bf16[32,64,128]{2,1,0:T(8,128)(2,1)S(1)}, bf16[32,64,128]{2,1,0:T(8,128)(2,1)}, u32[]{:S(2)}, u32[]{:S(2)}) collective-permute-start(bf16[32,64,128]{2,1,0:T(8,128)(2,1)S(1)} %collective-permute-done.4.rest_2_), channel_id=1, source_target_pairs={{0,1},{1,0},{2,3},{3,2},{4,5},{5,4},{6,7},{7,6},{8,9},{9,8},{10,11... | collective-permute-start | bytes 1572872 | tf_op jit(solution)/shard_map/ppermute | solution.py:453
  37.0 3.0 %collective-permute-start.9 = (bf16[32,64,128]{2,1,0:T(8,128)(2,1)S(1)}, bf16[32,64,128]{2,1,0:T(8,128)(2,1)}, u32[]{:S(2)}, u32[]{:S(2)}) collective-permute-start(bf16[32,64,128]{2,1,0:T(8,128)(2,1)S(1)} %collective-permute-done.5.rest_3_), channel_id=1, source_target_pairs={{0,1},{1,0},{2,3},{3,2},{4,5},{5,4},{6,7},{7,6},{8,9},{9,8},{10,11... | collective-permute-start | bytes 1572872 | tf_op jit(solution)/shard_map/ppermute | solution.py:453
  50.2 38.6 %copy-start = (f32[8,64,128]{2,1,0:T(8,128)S(1)}, f32[8,64,128]{2,1,0:T(8,128)}, u32[]{:S(2)}) copy-start(f32[8,64,128]{2,1,0:T(8,128)} %feat.1) | copy-start | bytes 786436
  50.2 38.6 %copy-start.2 = (f32[8,64,128]{2,1,0:T(8,128)S(1)}, f32[8,64,128]{2,1,0:T(8,128)}, u32[]{:S(2)}) copy-start(f32[8,64,128]{2,1,0:T(8,128)} %m1.1) | copy-start | bytes 786436
  50.2 38.6 %copy-start.3 = (f32[8,64,128]{2,1,0:T(8,128)S(1)}, f32[8,64,128]{2,1,0:T(8,128)}, u32[]{:S(2)}) copy-start(f32[8,64,128]{2,1,0:T(8,128)} %m2.1) | copy-start | bytes 786436
  50.2 38.6 %copy-start.4 = (s32[8]{0:T(128)S(1)}, s32[8]{0:T(128)}, u32[]{:S(2)}) copy-start(s32[8]{0:T(128)} %owner.1) | copy-start | bytes 100
  50.2 2.7 %collective-permute-start.11 = (f32[32,64,128]{2,1,0:T(8,128)S(1)}, f32[32,64,128]{2,1,0:T(8,128)S(1)}, u32[]{:S(2)}, u32[]{:S(2)}) collective-permute-start(f32[32,64,128]{2,1,0:T(8,128)S(1)} %get-tuple-element.63), channel_id=1, source_target_pairs={{0,1},{1,0},{2,3},{3,2},{4,5},{5,4},{6,7},{7,6},{8,9},{9,8},{10,11... | collective-permute-start | bytes 3145736 | tf_op jit(solution)/shard_map/ppermute | solution.py:453
  50.3 6.0 %collective-permute-start.13 = (f32[32,64,128]{2,1,0:T(8,128)S(1)}, f32[32,64,128]{2,1,0:T(8,128)S(1)}, u32[]{:S(2)}, u32[]{:S(2)}) collective-permute-start(f32[32,64,128]{2,1,0:T(8,128)S(1)} %get-tuple-element.65), channel_id=1, source_target_pairs={{0,1},{1,0},{2,3},{3,2},{4,5},{5,4},{6,7},{7,6},{8,9},{9,8},{10,11... | collective-permute-start | bytes 3145736 | tf_op jit(solution)/shard_map/ppermute | solution.py:453
  50.8 5.9 %collective-permute-start.15 = (f32[32,64,128]{2,1,0:T(8,128)S(1)}, f32[32,64,128]{2,1,0:T(8,128)S(1)}, u32[]{:S(2)}, u32[]{:S(2)}) collective-permute-start(f32[32,64,128]{2,1,0:T(8,128)S(1)} %get-tuple-element.67), channel_id=1, source_target_pairs={{0,1},{1,0},{2,3},{3,2},{4,5},{5,4},{6,7},{7,6},{8,9},{9,8},{10,11... | collective-permute-start | bytes 3145736 | tf_op jit(solution)/shard_map/ppermute | solution.py:453
  50.9 25.2 %collective-permute-start.10 = (f32[32,64,128]{2,1,0:T(8,128)S(1)}, f32[32,64,128]{2,1,0:T(8,128)S(1)}, u32[]{:S(2)}, u32[]{:S(2)}) collective-permute-start(f32[32,64,128]{2,1,0:T(8,128)S(1)} %get-tuple-element.61), channel_id=1, source_target_pairs={{0,1},{1,0},{2,3},{3,2},{4,5},{5,4},{6,7},{7,6},{8,9},{9,8},{10,11... | collective-permute-start | bytes 3145736 | tf_op jit(solution)/shard_map/ppermute | solution.py:453
  53.2 23.0 %collective-permute-start.12 = (f16[32,64,128]{2,1,0:T(8,128)(2,1)S(1)}, f16[32,64,128]{2,1,0:T(8,128)(2,1)S(1)}, u32[]{:S(2)}, u32[]{:S(2)}) collective-permute-start(f16[32,64,128]{2,1,0:T(8,128)(2,1)S(1)} %add_convert_fusion.2), channel_id=1, source_target_pairs={{0,4},{1,17},{2,6},{3,19},{4,0},{5,21},{6,2},{7,23},{8,12},{9,25},... | collective-permute-start | bytes 1572872 | tf_op jit(solution)/shard_map/ppermute | solution.py:448
  56.6 19.6 %collective-permute-start.14 = (f16[32,64,128]{2,1,0:T(8,128)(2,1)S(1)}, f16[32,64,128]{2,1,0:T(8,128)(2,1)S(1)}, u32[]{:S(2)}, u32[]{:S(2)}) collective-permute-start(f16[32,64,128]{2,1,0:T(8,128)(2,1)S(1)} %add_convert_fusion.1), channel_id=1, source_target_pairs={{0,6},{1,25},{2,0},{3,27},{4,2},{5,29},{6,4},{7,31},{8,14},{9,1},{... | collective-permute-start | bytes 1572872 | tf_op jit(solution)/shard_map/ppermute | solution.py:448
  56.9 19.3 %collective-permute-start.16 = (f16[32,64,128]{2,1,0:T(8,128)(2,1)S(1)}, f16[32,64,128]{2,1,0:T(8,128)(2,1)S(1)}, u32[]{:S(2)}, u32[]{:S(2)}) collective-permute-start(f16[32,64,128]{2,1,0:T(8,128)(2,1)S(1)} %add_convert_fusion), channel_id=1, source_target_pairs={{0,2},{1,9},{2,4},{3,11},{4,6},{5,13},{6,0},{7,15},{8,10},{9,17},{... | collective-permute-start | bytes 1572872 | tf_op jit(solution)/shard_map/ppermute | solution.py:448
  76.6 62.9 %copy-start.12 = (s32[1,16,8]{1,2,0:T(8,128)S(1)}, s32[1,16,8]{1,2,0:T(8,128)}, u32[]{:S(2)}) copy-start(s32[1,16,8]{1,2,0:T(8,128)} %param.30) | copy-start | bytes 1540
  76.6 65.5 %copy-start.7 = (s32[1,16]{1,0:T(1,128)S(1)}, s32[1,16]{1,0:T(1,128)}, u32[]{:S(2)}) copy-start(s32[1,16]{1,0:T(1,128)} %param.31) | copy-start | bytes 196
  76.9 11.8 %collective-permute-start.17 = (f16[8,64,128]{2,1,0:T(8,128)(2,1)S(1)}, f16[8,64,128]{2,1,0:T(8,128)(2,1)S(1)}, u32[]{:S(2)}, u32[]{:S(2)}) collective-permute-start(f16[8,64,128]{2,1,0:T(8,128)(2,1)S(1)} %get-tuple-element.96), channel_id=1, source_target_pairs={{0,16},{1,5},{2,18},{3,7},{4,20},{5,1},{6,22},{7,3},{8,24},{9,13},... | collective-permute-start | bytes 393224 | tf_op jit(solution)/shard_map/ppermute | solution.py:448
  77.0 11.7 %collective-permute-start.18 = (f16[8,64,128]{2,1,0:T(8,128)(2,1)S(1)}, f16[8,64,128]{2,1,0:T(8,128)(2,1)S(1)}, u32[]{:S(2)}, u32[]{:S(2)}) collective-permute-start(f16[8,64,128]{2,1,0:T(8,128)(2,1)S(1)} %get-tuple-element.98), channel_id=1, source_target_pairs={{0,24},{1,7},{2,26},{3,1},{4,28},{5,3},{6,30},{7,5},{8,0},{9,15},{... | collective-permute-start | bytes 393224 | tf_op jit(solution)/shard_map/ppermute | solution.py:448
  78.4 10.3 %collective-permute-start.19 = (f16[8,64,128]{2,1,0:T(8,128)(2,1)S(1)}, f16[8,64,128]{2,1,0:T(8,128)(2,1)S(1)}, u32[]{:S(2)}, u32[]{:S(2)}) collective-permute-start(f16[8,64,128]{2,1,0:T(8,128)(2,1)S(1)} %get-tuple-element.97), channel_id=1, source_target_pairs={{0,8},{1,3},{2,10},{3,5},{4,12},{5,7},{6,14},{7,1},{8,16},{9,11},{... | collective-permute-start | bytes 393224 | tf_op jit(solution)/shard_map/ppermute | solution.py:448
  78.5 19.3 %all-to-all-start.2 = ((bf16[32,32,128]{2,1,0:T(8,128)(2,1)}), bf16[32,32,128]{2,1,0:T(8,128)(2,1)S(1)}, u32[]{:S(2)}, u32[]{:S(2)}) async-start(bf16[32,32,128]{2,1,0:T(8,128)(2,1)} %screen_again.1), calls=%async_computation.2 | async-start | bytes 524288 | tf_op jit(solution)/shard_map/all_to_all | solution.py:535
  90.7 7.1 %collective-permute-start.20 = (bf16[1,64,128]{2,1,0:T(8,128)(2,1)S(1)}, bf16[1,64,128]{2,1,0:T(8,128)(2,1)S(1)}, u32[]{:S(2)}, u32[]{:S(2)}) collective-permute-start(bf16[1,64,128]{2,1,0:T(8,128)(2,1)S(1)} %get-tuple-element.73), channel_id=1, source_target_pairs={{0,32},{32,0},{64,96},{96,64},{128,160},{160,128},{192,224},{224,1... | collective-permute-start | bytes 49160 | tf_op jit(solution)/shard_map/ppermute | solution.py:522
  91.0 13.2 %collective-permute-start.22 = (bf16[1,64,128]{2,1,0:T(8,128)(2,1)S(1)}, bf16[1,64,128]{2,1,0:T(8,128)(2,1)S(1)}, u32[]{:S(2)}, u32[]{:S(2)}) collective-permute-start(bf16[1,64,128]{2,1,0:T(8,128)(2,1)S(1)} %get-tuple-element.77), channel_id=1, source_target_pairs={{0,96},{32,64},{64,32},{96,0},{128,224},{160,192},{192,160},{224,1... | collective-permute-start | bytes 49160 | tf_op jit(solution)/shard_map/ppermute | solution.py:522
  92.1 12.2 %collective-permute-start.23 = (bf16[1,64,128]{2,1,0:T(8,128)(2,1)S(1)}, bf16[1,64,128]{2,1,0:T(8,128)(2,1)S(1)}, u32[]{:S(2)}, u32[]{:S(2)}) collective-permute-start(bf16[1,64,128]{2,1,0:T(8,128)(2,1)S(1)} %get-tuple-element.78), channel_id=1, source_target_pairs={{0,128},{32,160},{64,192},{96,224},{128,0},{160,32},{192,64},{224,... | collective-permute-start | bytes 49160 | tf_op jit(solution)/shard_map/ppermute | solution.py:522
  94.2 10.0 %collective-permute-start.24 = (bf16[1,64,128]{2,1,0:T(8,128)(2,1)S(1)}, bf16[1,64,128]{2,1,0:T(8,128)(2,1)S(1)}, u32[]{:S(2)}, u32[]{:S(2)}) collective-permute-start(bf16[1,64,128]{2,1,0:T(8,128)(2,1)S(1)} %get-tuple-element.79), channel_id=1, source_target_pairs={{0,160},{32,128},{64,224},{96,192},{128,32},{160,0},{192,96},{224,... | collective-permute-start | bytes 49160 | tf_op jit(solution)/shard_map/ppermute | solution.py:522
  96.4 7.9 %collective-permute-start.25 = (bf16[1,64,128]{2,1,0:T(8,128)(2,1)S(1)}, bf16[1,64,128]{2,1,0:T(8,128)(2,1)S(1)}, u32[]{:S(2)}, u32[]{:S(2)}) collective-permute-start(bf16[1,64,128]{2,1,0:T(8,128)(2,1)S(1)} %get-tuple-element.80), channel_id=1, source_target_pairs={{0,192},{32,224},{64,128},{96,160},{128,64},{160,96},{192,0},{224,... | collective-permute-start | bytes 49160 | tf_op jit(solution)/shard_map/ppermute | solution.py:522
  97.8 3.9 %collective-permute-start.21 = (bf16[1,64,128]{2,1,0:T(8,128)(2,1)S(1)}, bf16[1,64,128]{2,1,0:T(8,128)(2,1)S(1)}, u32[]{:S(2)}, u32[]{:S(2)}) collective-permute-start(bf16[1,64,128]{2,1,0:T(8,128)(2,1)S(1)} %get-tuple-element.76), channel_id=1, source_target_pairs={{0,64},{32,96},{64,0},{96,32},{128,192},{160,224},{192,128},{224,1... | collective-permute-start | bytes 49160 | tf_op jit(solution)/shard_map/ppermute | solution.py:522
  101.7 3.8 %collective-permute-start.26 = (bf16[1,64,128]{2,1,0:T(8,128)(2,1)S(1)}, bf16[1,64,128]{2,1,0:T(8,128)(2,1)S(1)}, u32[]{:S(2)}, u32[]{:S(2)}) collective-permute-start(bf16[1,64,128]{2,1,0:T(8,128)(2,1)S(1)} %get-tuple-element.81), channel_id=1, source_target_pairs={{0,224},{32,192},{64,160},{96,128},{128,96},{160,64},{192,32},{224... | collective-permute-start | bytes 49160 | tf_op jit(solution)/shard_map/ppermute | solution.py:522
  105.5 11.2 %collective-permute-start.27 = (bf16[8,64,128]{2,1,0:T(8,128)(2,1)S(1)}, bf16[8,64,128]{2,1,0:T(8,128)(2,1)S(1)}, u32[]{:S(2)}, u32[]{:S(2)}) collective-permute-start(bf16[8,64,128]{2,1,0:T(8,128)(2,1)S(1)} %constant_dynamic-update-slice_fusion.4), channel_id=1, source_target_pairs={{0,8},{1,3},{2,10},{3,5},{4,12},{5,7},{6,14},{7,1},{8,16},{9,11},{... | collective-permute-start | bytes 393224 | tf_op jit(solution)/shard_map/ppermute | solution.py:448
  107.0 9.7 %collective-permute-start.28 = (bf16[8,64,128]{2,1,0:T(8,128)(2,1)S(1)}, bf16[8,64,128]{2,1,0:T(8,128)(2,1)S(1)}, u32[]{:S(2)}, u32[]{:S(2)}) collective-permute-start(bf16[8,64,128]{2,1,0:T(8,128)(2,1)S(1)} %constant_dynamic-update-slice_fusion.4), channel_id=1, source_target_pairs={{0,16},{1,5},{2,18},{3,7},{4,20},{5,1},{6,22},{7,3},{8,24},{9,13},... | collective-permute-start | bytes 393224 | tf_op jit(solution)/shard_map/ppermute | solution.py:448
  109.4 7.4 %collective-permute-start.29 = (bf16[8,64,128]{2,1,0:T(8,128)(2,1)S(1)}, bf16[8,64,128]{2,1,0:T(8,128)(2,1)S(1)}, u32[]{:S(2)}, u32[]{:S(2)}) collective-permute-start(bf16[8,64,128]{2,1,0:T(8,128)(2,1)S(1)} %constant_dynamic-update-slice_fusion.4), channel_id=1, source_target_pairs={{0,24},{1,7},{2,26},{3,1},{4,28},{5,3},{6,30},{7,5},{8,0},{9,15},{... | collective-permute-start | bytes 393224 | tf_op jit(solution)/shard_map/ppermute | solution.py:448
  110.7 31.5 %all-to-all-start.3 = ((f32[8,192,128]{2,1,0:T(8,128)}), f32[8,192,128]{2,1,0:T(8,128)S(1)}, u32[]{:S(2)}, u32[]{:S(2)}) async-start(f32[8,192,128]{2,1,0:T(8,128)} %get-tuple-element.88), calls=%async_computation.3 | async-start | bytes 1572864 | tf_op jit(solution)/shard_map/all_to_all | solution.py:531
  116.8 20.5 %collective-permute-start.30 = (bf16[32,64,128]{2,1,0:T(8,128)(2,1)S(1)}, bf16[32,64,128]{2,1,0:T(8,128)(2,1)S(1)}, u32[]{:S(2)}, u32[]{:S(2)}) collective-permute-start(bf16[32,64,128]{2,1,0:T(8,128)(2,1)S(1)} %constant_dynamic-update-slice_fusion.12.rest_0_), channel_id=1, source_target_pairs={{0,2},{1,9},{2,4},{3,11},{4,6},{5,13},{6,0},{7,15},{8,10},{9,17},{... | collective-permute-start | bytes 1572872 | tf_op jit(solution)/shard_map/ppermute | solution.py:448
  118.1 19.3 %collective-permute-start.31 = (bf16[32,64,128]{2,1,0:T(8,128)(2,1)S(1)}, bf16[32,64,128]{2,1,0:T(8,128)(2,1)S(1)}, u32[]{:S(2)}, u32[]{:S(2)}) collective-permute-start(bf16[32,64,128]{2,1,0:T(8,128)(2,1)S(1)} %constant_dynamic-update-slice_fusion.12.rest_0_), channel_id=1, source_target_pairs={{0,4},{1,17},{2,6},{3,19},{4,0},{5,21},{6,2},{7,23},{8,12},{9,25},... | collective-permute-start | bytes 1572872 | tf_op jit(solution)/shard_map/ppermute | solution.py:448
  120.5 16.8 %collective-permute-start.32 = (bf16[32,64,128]{2,1,0:T(8,128)(2,1)S(1)}, bf16[32,64,128]{2,1,0:T(8,128)(2,1)S(1)}, u32[]{:S(2)}, u32[]{:S(2)}) collective-permute-start(bf16[32,64,128]{2,1,0:T(8,128)(2,1)S(1)} %constant_dynamic-update-slice_fusion.12.rest_0_), channel_id=1, source_target_pairs={{0,6},{1,25},{2,0},{3,27},{4,2},{5,29},{6,4},{7,31},{8,14},{9,1},{... | collective-permute-start | bytes 1572872 | tf_op jit(solution)/shard_map/ppermute | solution.py:448
  132.0 8.3 %collective-permute-start.33 = (bf16[32,64,128]{2,1,0:T(8,128)(2,1)S(1)}, bf16[32,64,128]{2,1,0:T(8,128)(2,1)S(1)}, u32[]{:S(2)}, u32[]{:S(2)}) collective-permute-start(bf16[32,64,128]{2,1,0:T(8,128)(2,1)S(1)} %constant_dynamic-update-slice_fusion.12.rest_0_), channel_id=1, source_target_pairs={{0,1},{1,0},{2,3},{3,2},{4,5},{5,4},{6,7},{7,6},{8,9},{9,8},{10,11... | collective-permute-start | bytes 1572872 | tf_op jit(solution)/shard_map/ppermute | solution.py:453
  137.3 3.3 %collective-permute-start.34 = (bf16[32,64,128]{2,1,0:T(8,128)(2,1)S(1)}, bf16[32,64,128]{2,1,0:T(8,128)(2,1)}, u32[]{:S(2)}, u32[]{:S(2)}) collective-permute-start(bf16[32,64,128]{2,1,0:T(8,128)(2,1)S(1)} %collective-permute-done.30.rest_1_), channel_id=1, source_target_pairs={{0,1},{1,0},{2,3},{3,2},{4,5},{5,4},{6,7},{7,6},{8,9},{9,8},{10,11... | collective-permute-start | bytes 1572872 | tf_op jit(solution)/shard_map/ppermute | solution.py:453
  139.0 2.4 %collective-permute-start.35 = (bf16[32,64,128]{2,1,0:T(8,128)(2,1)S(1)}, bf16[32,64,128]{2,1,0:T(8,128)(2,1)}, u32[]{:S(2)}, u32[]{:S(2)}) collective-permute-start(bf16[32,64,128]{2,1,0:T(8,128)(2,1)S(1)} %collective-permute-done.31.rest_2_), channel_id=1, source_target_pairs={{0,1},{1,0},{2,3},{3,2},{4,5},{5,4},{6,7},{7,6},{8,9},{9,8},{10,11... | collective-permute-start | bytes 1572872 | tf_op jit(solution)/shard_map/ppermute | solution.py:453
  139.0 3.2 %collective-permute-start.36 = (bf16[32,64,128]{2,1,0:T(8,128)(2,1)S(1)}, bf16[32,64,128]{2,1,0:T(8,128)(2,1)}, u32[]{:S(2)}, u32[]{:S(2)}) collective-permute-start(bf16[32,64,128]{2,1,0:T(8,128)(2,1)S(1)} %collective-permute-done.32.rest_3_), channel_id=1, source_target_pairs={{0,1},{1,0},{2,3},{3,2},{4,5},{5,4},{6,7},{7,6},{8,9},{9,8},{10,11... | collective-permute-start | bytes 1572872 | tf_op jit(solution)/shard_map/ppermute | solution.py:453
  (5 other events, 114.7 us)
